TPU v7x, 32 devices: a whole 2x2x4 slice. The times are simulated.
32 devices in a mesh: tm: 4 (over y, core), roll: 8 (over z, x).
Axes of the slice: x: 2, y: 2, z: 4, core: 2. Of those that a mesh axis runs over, the one named last changes fastest.
Arguments:
- layer_input: bfloat16 [8, 3072, 256], P('roll', 'tm'), may hold values from -6 to 6
- start_memory: bfloat16 [8, 48, 256], P('roll'), may hold values from -6 to 6
- horizon: int32 [8, 64], P('roll'), may hold values from 0 to 15, as said below
- cotangent: bfloat16 [8, 3072, 256], P('roll', 'tm'), may hold values from -6 to 6
- first_gain: float32 [256], replicated, may hold values from 0.5 to 1.5
- first_shift: float32 [256], replicated, may hold values from -2 to 2
- query_projection_weight: bfloat16 [256, 256], replicated, may hold values from -0.375 to 0.375
- key_projection_weight: bfloat16 [256, 256], replicated, may hold values from -0.375 to 0.375
- value_projection_weight: bfloat16 [256, 256], replicated, may hold values from -0.375 to 0.375
- relative_weight: bfloat16 [256, 256], replicated, may hold values from -0.375 to 0.375
- content_bias: float32 [256], replicated, may hold values from -3 to 3
- position_bias: float32 [256], replicated, may hold values from -3 to 3
- output_weight: bfloat16 [256, 256], replicated, may hold values from -2 to 2
- second_gain: float32 [256], replicated, may hold values from 0.5 to 1.5
- second_shift: float32 [256], replicated, may hold values from -2 to 2
- expand_weight: bfloat16 [256, 1024], replicated, may hold values from -0.375 to 0.375
- expand_bias: float32 [1024], replicated, may hold values from -2 to 2
- shrink_weight: bfloat16 [1024, 256], replicated, may hold values from -0.25 to 0.25
- shrink_bias: float32 [256], replicated, may hold values from -2 to 2
Outputs:
- layer_output: bfloat16 [8, 3072, 256], P('roll', 'tm')
- input_grad: bfloat16 [8, 3072, 256], P('roll', 'tm')
- first_gain_grad: float32 [256], replicated
- first_shift_grad: float32 [256], replicated
- query_weight_grad: float32 [256, 256], replicated
- key_weight_grad: float32 [256, 256], replicated
- value_weight_grad: float32 [256, 256], replicated
- relative_weight_grad: float32 [256, 256], replicated
- content_bias_grad: float32 [256], replicated
- position_bias_grad: float32 [256], replicated
- output_weight_grad: float32 [256, 256], replicated
- second_gain_grad: float32 [256], replicated
- second_shift_grad: float32 [256], replicated
- expand_weight_grad: float32 [256, 1024], replicated
- expand_bias_grad: float32 [1024], replicated
- shrink_weight_grad: float32 [1024, 256], replicated
- shrink_bias_grad: float32 [256], replicated
Inputs may be any that keep to these rules, and one draw needn't show every extreme that they name: `horizon`: in every pair of consecutive rollouts (0 and 1, 2 and 3, and so on) one rollout has 15 in every segment.
All inputs are finite; a program needn't handle non-finite values.
Results may differ from a plain program's by a relative error of at most 0.012.
The roundings to bfloat16 on the way count: a program that leaves them out, or rounds other values in their place, can miss the bound.
Values may be sent and summed in bfloat16 or wider, within the bound.
No kernel may reach another device: no remote copies, remote signals or barrier semaphores. Data moves between devices by JAX's collectives and lax.ppermute only.
A program may use at most 64 MiB of HBM per device.

v0:
```python
import math

import jax
import jax.numpy as jnp
from jax import lax
from jax.sharding import PartitionSpec as P

HEADS = 8
HEAD_DIM = 32
SEGMENT_TOKENS = 48
STEP = 3


EPSILON = 1e-05
MASKED = -1000000000.0


def from_behind(value, axis, steps):
    count = lax.axis_size(axis)
    initial, last = (max(0, -steps), min(count, count - steps))
    return lax.ppermute(value, axis, [(source, source + steps) for source in range(initial, last)])


def norm_layer(values, gain, shift):
    center = values - jnp.mean(values, axis=-1, keepdims=True)
    spread = jnp.mean(center * center, axis=-1, keepdims=True)
    return center * lax.rsqrt(spread + EPSILON) * gain + shift


def shift_relative(scores):
    leading = scores.shape[:-2]
    row_count = scores.shape[-2]
    col_count = scores.shape[-1]
    padded = jnp.pad(scores, [(0, 0)] * len(leading) + [(0, 0), (1, 0)])
    padded = padded.reshape(leading + (col_count + 1, row_count))
    return padded[..., 1:, :].reshape(leading + (row_count, col_count))


def position_table(count, features):
    half_width = features // 2
    distance = (count - 1 - jnp.arange(count)).astype(jnp.float32)
    freqs = 10000.0 ** (-(2.0 * jnp.arange(half_width).astype(jnp.float32)) / features)
    angles = distance[:, None] * freqs[None, :]
    return jnp.concatenate([jnp.sin(angles), jnp.cos(angles)], axis=-1)


def key_mask(previous, current, seg_len, step_len):
    query_pos = jnp.arange(seg_len)[:, None]
    key_pos = jnp.arange(2 * seg_len)[None, :]
    causal = key_pos <= query_pos + seg_len
    itself = key_pos == query_pos + seg_len
    key_step = jnp.where(key_pos < seg_len, key_pos, key_pos - seg_len) // step_len
    limit = jnp.where(key_pos < seg_len, previous[:, None], current[:, None])
    live = key_step < limit
    return causal[None] & (live[:, None, :] | itself[None])


def activation(values):
    return jax.nn.gelu(values, approximate=True)


def body(
    layer_input,
    start_memory,
    horizon,
    cotangent,
    first_gain,
    first_shift,
    query_projection_weight,
    key_projection_weight,
    value_projection_weight,
    relative_weight,
    content_bias,
    position_bias,
    output_weight,
    second_gain,
    second_shift,
    expand_weight,
    expand_bias,
    shrink_weight,
    shrink_bias,
):
    rollout_rows, columns, features = layer_input.shape
    per_device = columns // SEGMENT_TOKENS
    count = rollout_rows * per_device
    scaling = 1.0 / math.sqrt(HEAD_DIM)
    position = lax.axis_index("tm")
    blocks = layer_input.reshape(rollout_rows, per_device, SEGMENT_TOKENS, features)
    arrived = from_behind(blocks[:, -1], "tm", 1)
    first_memory = jnp.where(position == 0, start_memory, arrived)
    memory = jnp.concatenate([first_memory[:, None], blocks[:, :-1]], axis=1).reshape(
        count, SEGMENT_TOKENS, features
    )
    segment = blocks.reshape(count, SEGMENT_TOKENS, features)
    padded = jnp.concatenate(
        [jnp.full((rollout_rows, 1), SEGMENT_TOKENS // STEP, jnp.int32), horizon], axis=1
    )
    offset = position * per_device
    current = lax.dynamic_slice_in_dim(padded, offset + 1, per_device, 1).reshape(count)
    previous = lax.dynamic_slice_in_dim(padded, offset, per_device, 1).reshape(count)
    allowed = key_mask(previous, current, SEGMENT_TOKENS, STEP)[:, None]
    joined = jnp.concatenate([memory, segment], axis=1).astype(jnp.float32)
    layer_normalized, first_back = jax.vjp(norm_layer, joined, first_gain, first_shift)
    normed_low = layer_normalized.astype(jnp.bfloat16)
    query_vectors = jnp.dot(
        normed_low[:, SEGMENT_TOKENS:], query_projection_weight, preferred_element_type=jnp.float32
    )
    key_matrix_rows = jnp.dot(
        normed_low, key_projection_weight, preferred_element_type=jnp.float32
    ).astype(jnp.bfloat16)
    value_matrix_rows = jnp.dot(
        normed_low, value_projection_weight, preferred_element_type=jnp.float32
    ).astype(jnp.bfloat16)
    key_heads = key_matrix_rows.reshape(count, 2 * SEGMENT_TOKENS, HEADS, HEAD_DIM)
    value_heads = value_matrix_rows.reshape(count, 2 * SEGMENT_TOKENS, HEADS, HEAD_DIM)
    content = (
        (query_vectors + content_bias)
        .astype(jnp.bfloat16)
        .reshape(count, SEGMENT_TOKENS, HEADS, HEAD_DIM)
    )
    placed = (
        (query_vectors + position_bias)
        .astype(jnp.bfloat16)
        .reshape(count, SEGMENT_TOKENS, HEADS, HEAD_DIM)
    )
    table_low = position_table(2 * SEGMENT_TOKENS, features).astype(jnp.bfloat16)
    relative = jnp.dot(table_low, relative_weight, preferred_element_type=jnp.float32).astype(
        jnp.bfloat16
    )
    rel_heads = relative.reshape(2 * SEGMENT_TOKENS, HEADS, HEAD_DIM)

    def score_block():
        direct = jnp.einsum(
            "bihe,bjhe->bhij", content, key_heads, preferred_element_type=jnp.float32
        )
        raw_scores = jnp.einsum(
            "bihe,jhe->bhij", placed, rel_heads, preferred_element_type=jnp.float32
        )
        shifted, shift_back = jax.vjp(shift_relative, raw_scores)
        return (jnp.where(allowed, (direct + shifted) * scaling, MASKED), shift_back)

    scores, unused = score_block()
    row_top = jnp.max(scores, axis=-1, keepdims=True)
    exponent = jnp.exp(scores - row_top)
    row_total = jnp.sum(exponent, axis=-1, keepdims=True)
    summary = row_top + jnp.log(row_total)
    probs_low = (exponent / row_total).astype(jnp.bfloat16)
    mixed = jnp.einsum(
        "bhij,bjhe->bihe", probs_low, value_heads, preferred_element_type=jnp.float32
    )
    mixed = mixed.reshape(count, SEGMENT_TOKENS, features).astype(jnp.bfloat16)
    hidden = segment.astype(jnp.float32) + jnp.dot(
        mixed, output_weight, preferred_element_type=jnp.float32
    )
    normed2, second_back = jax.vjp(norm_layer, hidden, second_gain, second_shift)
    normed2_low = normed2.astype(jnp.bfloat16)
    pre_act = jnp.dot(normed2_low, expand_weight, preferred_element_type=jnp.float32) + expand_bias
    activated, act_back = jax.vjp(activation, pre_act)
    activated_low = activated.astype(jnp.bfloat16)
    output = (
        hidden
        + jnp.dot(activated_low, shrink_weight, preferred_element_type=jnp.float32)
        + shrink_bias
    )
    back_out_low = cotangent.reshape(count, SEGMENT_TOKENS, features)
    back_out = back_out_low.astype(jnp.float32)
    shrink_bias_grad = jnp.sum(back_out, axis=(0, 1))
    shrink_grad = jnp.einsum(
        "bsf,bsd->fd", activated_low, back_out_low, preferred_element_type=jnp.float32
    )
    back_act = jnp.einsum(
        "bsd,fd->bsf", back_out_low, shrink_weight, preferred_element_type=jnp.float32
    )
    (back_pre,) = act_back(back_act)
    expand_bias_grad = jnp.sum(back_pre, axis=(0, 1))
    back_pre_low = back_pre.astype(jnp.bfloat16)
    expand_grad = jnp.einsum(
        "bsd,bsf->df", normed2_low, back_pre_low, preferred_element_type=jnp.float32
    )
    back_normed2 = jnp.einsum(
        "bsf,df->bsd", back_pre_low, expand_weight, preferred_element_type=jnp.float32
    )
    back_norm_hidden, second_gain_grad, second_shift_grad = second_back(back_normed2)
    back_hidden = back_out + back_norm_hidden
    feed_terms = (
        second_gain_grad,
        second_shift_grad,
        expand_grad,
        expand_bias_grad,
        shrink_grad,
        shrink_bias_grad,
    )
    back_hidden_low = back_hidden.astype(jnp.bfloat16)
    output_grad = jnp.einsum(
        "bsd,bse->de", mixed, back_hidden_low, preferred_element_type=jnp.float32
    )
    back_mixed = jnp.einsum(
        "bse,de->bsd", back_hidden_low, output_weight, preferred_element_type=jnp.float32
    )
    back_mixed = back_mixed.astype(jnp.bfloat16).reshape(count, SEGMENT_TOKENS, HEADS, HEAD_DIM)
    scores, shift_back = score_block()
    probs = jnp.exp(scores - summary)
    probs_low = probs.astype(jnp.bfloat16)
    back_probs = jnp.einsum(
        "bihe,bjhe->bhij", back_mixed, value_heads, preferred_element_type=jnp.float32
    )
    value_back = jnp.einsum(
        "bhij,bihe->bjhe", probs_low, back_mixed, preferred_element_type=jnp.float32
    )
    value_back = value_back.astype(jnp.bfloat16).reshape(count, 2 * SEGMENT_TOKENS, features)
    back_scores = probs * (back_probs - jnp.sum(back_probs * probs, axis=-1, keepdims=True))
    back_scores = back_scores.astype(jnp.bfloat16)
    back_content = scaling * jnp.einsum(
        "bhij,bjhe->bihe", back_scores, key_heads, preferred_element_type=jnp.float32
    )
    key_back = scaling * jnp.einsum(
        "bhij,bihe->bjhe", back_scores, content, preferred_element_type=jnp.float32
    )
    key_back = key_back.astype(jnp.bfloat16).reshape(count, 2 * SEGMENT_TOKENS, features)
    (back_raw,) = shift_back(back_scores.astype(jnp.float32))
    back_raw_low = back_raw.astype(jnp.bfloat16)
    back_placed = scaling * jnp.einsum(
        "bhic,che->bihe", back_raw_low, rel_heads, preferred_element_type=jnp.float32
    )
    back_relative = scaling * jnp.einsum(
        "bhic,bihe->che", back_raw_low, placed, preferred_element_type=jnp.float32
    )
    back_relative = back_relative.reshape(2 * SEGMENT_TOKENS, features)
    content_grad = jnp.sum(back_content, axis=(0, 1)).reshape(features)
    position_grad = jnp.sum(back_placed, axis=(0, 1)).reshape(features)
    back_query = (
        (back_content + back_placed).reshape(count, SEGMENT_TOKENS, features).astype(jnp.bfloat16)
    )
    query_grad = jnp.einsum(
        "bsd,bse->de",
        normed_low[:, SEGMENT_TOKENS:],
        back_query,
        preferred_element_type=jnp.float32,
    )
    key_grad = jnp.einsum("bsd,bse->de", normed_low, key_back, preferred_element_type=jnp.float32)
    value_grad = jnp.einsum(
        "bsd,bse->de", normed_low, value_back, preferred_element_type=jnp.float32
    )
    relative_grad = jnp.dot(
        table_low.astype(jnp.float32).T, back_relative, precision=lax.Precision.HIGHEST
    )
    back_normed = jnp.einsum(
        "bse,de->bsd", key_back, key_projection_weight, preferred_element_type=jnp.float32
    )
    back_normed = back_normed + jnp.einsum(
        "bse,de->bsd", value_back, value_projection_weight, preferred_element_type=jnp.float32
    )
    query_part = jnp.einsum(
        "bse,de->bsd", back_query, query_projection_weight, preferred_element_type=jnp.float32
    )
    back_normed = back_normed + jnp.concatenate(
        [jnp.zeros((count, SEGMENT_TOKENS, features), jnp.float32), query_part], axis=1
    )
    back_joined, first_gain_grad, first_shift_grad = first_back(back_normed)
    input_grad = (
        (back_hidden + back_joined[:, SEGMENT_TOKENS:])
        .astype(jnp.bfloat16)
        .reshape(rollout_rows, columns, features)
    )
    mixing_terms = (
        first_gain_grad,
        first_shift_grad,
        query_grad,
        key_grad,
        value_grad,
        relative_grad,
        content_grad,
        position_grad,
        output_grad,
    )
    summed = tuple(lax.psum(mixing_terms + feed_terms, ("tm", "roll")))
    layer_output = output.astype(jnp.bfloat16).reshape(rollout_rows, columns, features)
    return (layer_output, input_grad) + summed


def solution(mesh):
    in_specs = (
        P("roll", "tm", None),
        P("roll", None, None),
        P("roll", None),
        P("roll", "tm", None),
        P(),
        P(),
        P(),
        P(),
        P(),
        P(),
        P(),
        P(),
        P(),
        P(),
        P(),
        P(),
        P(),
        P(),
        P(),
    )
    out_specs = (
        P("roll", "tm", None),
        P("roll", "tm", None),
        P(),
        P(),
        P(),
        P(),
        P(),
        P(),
        P(),
        P(),
        P(),
        P(),
        P(),
        P(),
        P(),
        P(),
        P(),
    )
    return jax.shard_map(body, mesh=mesh, in_specs=in_specs, out_specs=out_specs, check_vma=False)
```

profile of v0, /device:TPU:0, one launch (start us, length us, event | category | flops | bytes accessed | tf_op | source)
XLA Modules:
  0.0 288.1 jit_solution(5568124694171582944)
XLA Ops:
  7.3 0.8 slice_bitcast_fusion
  8.1 2.3 collective-permute-start
  10.6 0.7 pad_add_fusion.1
  11.7 1.1 convolution_convert_fusion.3
  12.9 0.7 or_and_fusion
  13.6 1.7 convert_reduce_fusion.1
  15.2 1.0 slice.25
  16.3 0.7 copy.62
  17.0 0.7 select_bitcast_fusion
  19.9 1.3 convolution_convert_fusion
  21.1 1.6 copy.60
  22.8 1.2 convolution_convert_fusion.1
  24.0 2.2 copy.59
  26.3 1.0 add_convert_fusion.2
  27.8 3.2 %reshape.327 = bf16[16,48,8,32]{3,2,1,0:T(8,128)(2,1)} reshape(bf16[16,48,256]{2,1,0:T(8,128)(2,1)} %get-tuple-element.46) | data formatting | bytes 786432 | tf_op jit(solution)/shard_map/reshape | solution.py:124
  30.9 2.9 %copy.63 = bf16[16,48,8,32]{1,3,0,2:T(8,128)(2,1)} copy(bf16[16,48,8,32]{3,2,1,0:T(8,128)(2,1)} %reshape.327) | data formatting | bytes 786432 | tf_op jit(solution)/shard_map/reshape | solution.py:124
  33.9 1.9 convolution_bitcast_fusion
  36.1 2.6 pad.15.clone
  38.7 7.9 %reshape.328 = f32[16,8,97,48]{3,2,1,0:T(8,128)} reshape(f32[16,8,48,97]{3,2,1,0:T(8,128)} %pad.15.clone) | data formatting | bytes 4767744 | tf_op jit(solution)/shard_map/jvp()/reshape | solution.py:35
  46.6 6.6 %slice.27 = f32[16,8,96,48]{3,2,1,0:T(8,128)} slice(f32[16,8,97,48]{3,2,1,0:T(8,128)} %reshape.328), slice={[0:16], [0:8], [1:97], [0:48]} | slice | bytes 4718592 | tf_op jit(solution)/shard_map/jvp()/slice | solution.py:36
  53.2 6.1 %reshape.329 = f32[16,8,48,96]{3,2,1,0:T(8,128)} reshape(f32[16,8,96,48]{3,2,1,0:T(8,128)} %slice.27) | data formatting | bytes 4718592 | tf_op jit(solution)/shard_map/jvp()/reshape | solution.py:36
  59.3 3.6 %fusion.73 = (f32[16,8,48]{2,1,0:T(8,128)S(1)}, f32[16,8,48,96]{3,2,1,0:T(8,128)S(1)}) fusion(f32[16,8,48,96]{3,2,1,0:T(8,128)} %reshape.329, bf16[16,48,8,32]{1,3,2,0:T(8,128)(2,1)S(1)} %bitcast.159, bf16[16,96,8,32]{1,3,2,0:T(8,128)(2,1)S(1)} %bitcast.161, pred[16,48,96]{2,1,0:T(8,128)(4,1)S(1)} %copy-done.40), kind=kOutput, calls=%fused_computation.136 | convolution fusion | flops 40101888 | bytes 5996544 | tf_op jit(solution)/shard_map/bihe,bjhe->bhij/dot_general | solution.py:133
  62.9 1.9 fusion.6
  64.8 0.6 log_add_fusion
  65.4 2.6 fusion.26
  69.1 2.6 multiply_convert_fusion.1
  71.7 3.3 %fusion.75 = (f32[1024]{0:T(1024)}, bf16[16,48,1024]{2,1,0:T(8,128)(2,1)S(1)}) fusion(f32[16,48,1024]{2,1,0:T(8,128)S(1)} %get-tuple-element.58, f32[1024]{0:T(1024)S(1)} %copy-done.60, bf16[16,48,256]{2,1,0:T(8,128)(2,1)S(1)} %bitcast.172, bf16[1024,256]{1,0:T(8,128)(2,1)S(1)} %copy-done.58), kind=kOutput, calls=%fused_computation.138 | convolution fusion | flops 419953664 | bytes 5644288 | tf_op jit(solution)/shard_map/bsd,fd->bsf/dot_general | solution.py:171
  75.0 1.3 multiply_reduce_fusion.1
  76.2 1.8 convolution_bitcast_fusion.2
  78.6 0.9 copy-done.19
  79.7 1.1 convolution_bitcast_fusion.3
  80.8 1.0 convolution_convert_fusion.2
  81.9 2.3 copy.92
  84.2 3.4 %fusion.27 = bf16[16,8,32,96]{3,2,1,0:T(8,128)(2,1)} fusion(bf16[16,48,8,32]{1,3,2,0:T(8,128)(2,1)} %bitcast.163, f32[16,8,48,96]{3,2,1,0:T(8,128)S(1)} %copy-done.3, f32[16,8,48]{2,1,0:T(8,128)} %log_add_fusion), kind=kOutput, calls=%fused_computation.44 | convolution fusion | flops 39321600 | bytes 3563520 | tf_op jit(solution)/shard_map/bhij,bihe->bjhe/dot_general | solution.py:207
  87.6 2.6 multiply_reduce_fusion
  90.2 2.0 multiply_convert_fusion
  92.8 1.1 copy-done.6
  93.9 1.2 convolution_bitcast_fusion.5
  95.1 1.8 fusion.54
  96.8 2.3 fusion.76
  99.1 5.2 %reshape.335 = bf16[16,8,96,48]{3,2,1,0:T(8,128)(2,1)} reshape(bf16[16,8,48,96]{3,2,1,0:T(8,128)(2,1)} %copy-done.4) | data formatting | bytes 2359296 | tf_op jit(solution)/shard_map/transpose(jvp())/reshape | solution.py:36
  104.3 3.2 %convolution_bitcast_fusion.1 = f32[1024,256]{1,0:T(8,128)} fusion(bf16[16,48,1024]{2,1,0:T(8,128)(2,1)} %get-tuple-element.57, bf16[16,48,256]{2,1,0:T(8,128)(2,1)S(1)} %bitcast.174), kind=kOutput, calls=%fused_computation.47 | convolution fusion | flops 402653184 | bytes 3014656 | tf_op jit(solution)/shard_map/bsf,bsd->fd/dot_general | solution.py:168
  107.5 1.2 convolution_bitcast_fusion.4
  108.7 3.1 %pad.16 = bf16[16,8,97,48]{3,2,1,0:T(8,128)(2,1)} pad(bf16[16,8,96,48]{3,2,1,0:T(8,128)(2,1)S(1)} %copy-done.8, bf16[]{:T(256)} %constant.84.clone.1), padding=0_0x0_0x1_0x0_0 | pad | bytes 2371586 | tf_op jit(solution)/shard_map/transpose(jvp())/pad | solution.py:36
  111.8 7.7 %reshape.336 = bf16[16,8,48,97]{3,2,1,0:T(8,128)(2,1)} reshape(bf16[16,8,97,48]{3,2,1,0:T(8,128)(2,1)} %pad.16) | data formatting | bytes 2383872 | tf_op jit(solution)/shard_map/transpose(jvp())/reshape | solution.py:35
  119.5 2.7 fusion.35
  122.4 2.1 bitcast_reduce_fusion
  124.4 1.2 convolution_bitcast_fusion.6
  125.7 1.0 fusion.64
  127.0 1.3 fusion.59
  129.0 3.3 %fusion.17 = (f32[256]{0:T(256)}, f32[16,96]{1,0:T(8,128)S(1)}, f32[256]{0:T(256)}, f32[16,96,256]{2,1,0:T(8,128)S(1)}) fusion(f32[16,96]{1,0:T(8,128)S(1)} %fusion.65, f32[16,96]{1,0:T(8,128)S(1)} %broadcast_multiply_fusion.1, bf16[16,48,256]{2,1,0:T(8,128)(2,1)S(1)} %bitcast.155, bf16[16,48,256]{2,1,0:T(8,128)(2,1)S(1)} %copy-done.10, ...), kind=kOutput, calls=%fused_computation.34 | convolution fusion | flops 206829568 | bytes 5657600 | tf_op jit(solution)/shard_map/bse,de->bsd/dot_general | solution.py:250
  132.3 1.1 fusion.71
  133.6 0.9 reshape.339
  134.4 41.8 %all-reduce.3 = (f32[256]{0:T(256)}, f32[256]{0:T(256)}, f32[256]{0:T(256)}, f32[256]{0:T(256)}, f32[256]{0:T(256)}, /*index=5*/f32[256]{0:T(256)}, f32[1024]{0:T(1024)}, f32[256]{0:T(256)}) all-reduce(f32[256]{0:T(256)} %get-tuple-element.17, f32[256]{0:T(256)} %get-tuple-element.21, ...), channel_id=1, replica_groups=mesh['tm'=4,'roll'=8] {'tm','roll'}, use_global_device_ids=true, to_apply=%region_12.13 | all-reduce | flops 2816 | bytes 22528 | tf_op jit(solution)/shard_map/psum | solution.py:276
  176.2 2.1 fusion.39
  178.3 2.7 fusion.31
  181.0 90.7 %all-reduce.7.cloned.1.call-done = (f32[256,256]{1,0:T(8,128)}, f32[256,256]{1,0:T(8,128)}, f32[256,256]{1,0:T(8,128)}, f32[256,256]{1,0:T(8,128)}, f32[256,256]...) async-done(((f32[256,256]{1,0:T(8,128)}, f32[256,256]{1,0:T(8,128)}, f32[256,256]{1,0:T(8,128)}, f32[256,256]{1,0:T(8,128)}, f32[256,256]{1,0:T(8,128)}, ...) | async-done | bytes 3407888 | tf_op jit(solution)/shard_map/psum | solution.py:276
  271.8 1.8 copy.108
  273.5 1.8 copy.109
  275.3 1.7 copy.110
  277.0 1.7 copy.111
  278.6 0.7 copy.112
  279.3 1.0 copy.113
  280.3 1.0 copy.114
  (157 shorter events, 7.0 us)
Async XLA Ops:
  7.2 61.9 %copy-start = (bf16[256,1024]{1,0:T(8,128)(2,1)S(1)}, bf16[256,1024]{1,0:T(8,128)(2,1)}, u32[]{:S(2)}) copy-start(bf16[256,1024]{1,0:T(8,128)(2,1)} %param.34) | copy-start | bytes 1572868
  7.2 10.6 %copy-start.7 = (bf16[1,768,256]{2,1,0:T(8,128)(2,1)S(1)}, bf16[1,768,256]{2,1,0:T(8,128)(2,1)}, u32[]{:S(2)}) copy-start(bf16[1,768,256]{2,1,0:T(8,128)(2,1)} %param.19) | copy-start | bytes 1179652
  7.2 264.5 %all-reduce.7.cloned.1.call-start = ((), (), s32[]{:S(2)}) async-start(), calls=%async_computation | async-start | bytes 6815744 | tf_op jit(solution)/shard_map/psum | solution.py:276
  8.1 8.9 %collective-permute-start = (bf16[1,48,256]{2,1,0:T(8,128)(2,1)S(1)}, bf16[1,48,256]{2,1,0:T(8,128)(2,1)S(1)}, u32[]{:S(2)}, u32[]{:S(2)}) collective-permute-start(bf16[1,48,256]{2,1,0:T(8,128)(2,1)S(1)} %slice_bitcast_fusion), channel_id=1, source_target_pairs={{0,8},{8,16},{16,24},{1,9},{9,17},{17,25},{2,10},{10,18},{18,26},{... | collective-permute-start | bytes 73736 | tf_op jit(solution)/shard_map/ppermute | solution.py:21
  10.5 8.9 %copy-start.51 = (f32[256]{0:T(256)S(1)}, f32[256]{0:T(256)}, u32[]{:S(2)}) copy-start(f32[256]{0:T(256)} %param.23) | copy-start | bytes 3076
  10.5 8.9 %copy-start.54 = (f32[256]{0:T(256)S(1)}, f32[256]{0:T(256)}, u32[]{:S(2)}) copy-start(f32[256]{0:T(256)} %param.24) | copy-start | bytes 3076
  11.6 3.6 %copy-start.42 = (bf16[96,128]{1,0:T(8,128)(2,1)}, bf16[96,128]{1,0:T(8,128)(2,1)S(1)}, u32[]{:S(2)}) copy-start(bf16[96,128]{1,0:T(8,128)(2,1)S(1)} %get-tuple-element.47) | copy-start | bytes 73732
  11.6 3.6 %copy-start.44 = (bf16[96,128]{1,0:T(8,128)(2,1)}, bf16[96,128]{1,0:T(8,128)(2,1)S(1)}, u32[]{:S(2)}) copy-start(bf16[96,128]{1,0:T(8,128)(2,1)S(1)} %get-tuple-element.48) | copy-start | bytes 73732
  16.3 3.6 %copy-start.38 = (bf16[256,256]{1,0:T(8,128)(2,1)S(1)}, bf16[256,256]{1,0:T(8,128)(2,1)}, u32[]{:S(2)}) copy-start(bf16[256,256]{1,0:T(8,128)(2,1)} %param.26) | copy-start | bytes 393220
  17.8 3.4 %copy-start.9 = (bf16[16,48,256]{2,1,0:T(8,128)(2,1)}, bf16[16,48,256]{2,1,0:T(8,128)(2,1)S(1)}, u32[]{:S(2)}) copy-start(bf16[16,48,256]{2,1,0:T(8,128)(2,1)S(1)} %maximum_bitcast_fusion) | copy-start | bytes 1179652
  19.9 6.4 %copy-start.5 = (bf16[16,96,256]{2,1,0:T(8,128)(2,1)}, bf16[16,96,256]{2,1,0:T(8,128)(2,1)S(1)}, u32[]{:S(2)}) copy-start(bf16[16,96,256]{2,1,0:T(8,128)(2,1)S(1)} %fusion.16) | copy-start | bytes 2359300
  19.9 2.9 copy-start.46
  22.7 36.6 %copy-start.13 = (bf16[16,96,256]{1,2,0:T(8,128)(2,1)}, bf16[16,96,256]{1,2,0:T(8,128)(2,1)S(1)}, u32[]{:S(2)}) copy-start(bf16[16,96,256]{1,2,0:T(8,128)(2,1)S(1)} %copy.60) | copy-start | bytes 2359300
  22.7 3.5 %copy-start.36 = (bf16[256,256]{1,0:T(8,128)(2,1)S(1)}, bf16[256,256]{1,0:T(8,128)(2,1)}, u32[]{:S(2)}) copy-start(bf16[256,256]{1,0:T(8,128)(2,1)} %param.25) | copy-start | bytes 393220
  22.8 3.5 %copy-start.55 = (f32[256]{0:T(256)S(1)}, f32[256]{0:T(256)}, u32[]{:S(2)}) copy-start(f32[256]{0:T(256)} %param.29) | copy-start | bytes 3076
  22.8 3.5 %copy-start.56 = (f32[256]{0:T(256)S(1)}, f32[256]{0:T(256)}, u32[]{:S(2)}) copy-start(f32[256]{0:T(256)} %param.30) | copy-start | bytes 3076
  27.8 31.5 %copy-start.11 = (bf16[16,48,256]{1,2,0:T(8,128)(2,1)}, bf16[16,48,256]{1,2,0:T(8,128)(2,1)S(1)}, u32[]{:S(2)}) copy-start(bf16[16,48,256]{1,2,0:T(8,128)(2,1)S(1)} %copy.91) | copy-start | bytes 1179652
  27.8 6.1 %copy-start.33 = (bf16[96,256]{0,1:T(8,128)(2,1)S(1)}, bf16[96,256]{0,1:T(8,128)(2,1)}, u32[]{:S(2)}) copy-start(bf16[96,256]{0,1:T(8,128)(2,1)} %copy.62) | copy-start | bytes 147460
  53.2 6.1 %copy-start.40 = (pred[16,48,96]{2,1,0:T(8,128)(4,1)S(1)}, pred[16,48,96]{2,1,0:T(8,128)(4,1)}, u32[]{:S(2)}) copy-start(pred[16,48,96]{2,1,0:T(8,128)(4,1)} %or_and_fusion) | copy-start | bytes 221188
  62.9 5.2 %copy-start.2 = (f32[16,8,48,96]{3,2,1,0:T(8,128)}, f32[16,8,48,96]{3,2,1,0:T(8,128)S(1)}, u32[]{:S(2)}) copy-start(f32[16,8,48,96]{3,2,1,0:T(8,128)S(1)} %get-tuple-element.54) | copy-start | bytes 7077892
  62.9 2.5 copy-start.26
  65.4 2.7 copy-start.35
  68.1 1.0 copy-start.57
  68.1 1.0 copy-start.60
  68.1 1.0 copy-start.61
  68.7 9.4 %copy-start.17 = (f32[16,48,256]{2,1,0:T(8,128)}, f32[16,48,256]{2,1,0:T(8,128)S(1)}, u32[]{:S(2)}) copy-start(f32[16,48,256]{2,1,0:T(8,128)S(1)} %get-tuple-element.56) | copy-start | bytes 2359300
  69.1 2.6 copy-start.28
  69.1 2.6 copy-start.58
  78.6 0.9 copy-start.19
  78.6 0.9 copy-start.48
  79.7 4.5 %copy-start.3 = (f32[16,8,48,96]{3,2,1,0:T(8,128)S(1)}, f32[16,8,48,96]{3,2,1,0:T(8,128)}, u32[]{:S(2)}) copy-start(f32[16,8,48,96]{3,2,1,0:T(8,128)} %copy-done.2) | copy-start | bytes 7077892
  84.2 3.4 %copy-start.15 = (bf16[16,48,256]{1,2,0:T(8,128)(2,1)S(1)}, bf16[16,48,256]{1,2,0:T(8,128)(2,1)}, u32[]{:S(2)}) copy-start(bf16[16,48,256]{1,2,0:T(8,128)(2,1)} %copy.92) | copy-start | bytes 1179652
  84.2 3.4 %copy-start.27 = (bf16[16,96,256]{1,2,0:T(8,128)(2,1)S(1)}, bf16[16,96,256]{1,2,0:T(8,128)(2,1)}, u32[]{:S(2)}) copy-start(bf16[16,96,256]{1,2,0:T(8,128)(2,1)} %copy.59) | copy-start | bytes 2359300
  84.2 3.4 %copy-start.30 = (f32[16,8,48]{2,1,0:T(8,128)S(1)}, f32[16,8,48]{2,1,0:T(8,128)}, u32[]{:S(2)}) copy-start(f32[16,8,48]{2,1,0:T(8,128)} %log_add_fusion) | copy-start | bytes 73732
  90.2 2.0 copy-start.12
  92.2 4.7 %copy-start.4 = (bf16[16,8,48,96]{3,2,1,0:T(8,128)(2,1)}, bf16[16,8,48,96]{3,2,1,0:T(8,128)(2,1)S(1)}, u32[]{:S(2)}) copy-start(bf16[16,8,48,96]{3,2,1,0:T(8,128)(2,1)S(1)} %multiply_convert_fusion) | copy-start | bytes 3538948
  92.2 1.7 copy-start.6
  92.2 2.9 %copy-start.39 = (bf16[256,256]{1,0:T(8,128)(2,1)S(1)}, bf16[256,256]{1,0:T(8,128)(2,1)}, u32[]{:S(2)}) copy-start(bf16[256,256]{1,0:T(8,128)(2,1)} %param.26) | copy-start | bytes 393220
  93.9 3.0 %copy-start.14 = (bf16[16,96,256]{1,2,0:T(8,128)(2,1)S(1)}, bf16[16,96,256]{1,2,0:T(8,128)(2,1)}, u32[]{:S(2)}) copy-start(bf16[16,96,256]{1,2,0:T(8,128)(2,1)} %copy-done.13) | copy-start | bytes 2359300
  99.1 5.2 %copy-start.29 = (bf16[1,768,256]{2,1,0:T(8,128)(2,1)S(1)}, bf16[1,768,256]{2,1,0:T(8,128)(2,1)}, u32[]{:S(2)}) copy-start(bf16[1,768,256]{2,1,0:T(8,128)(2,1)} %param.22) | copy-start | bytes 1179652
  104.3 3.2 %copy-start.22 = (bf16[16,8,32,96]{3,2,1,0:T(8,128)(2,1)S(1)}, bf16[16,8,32,96]{3,2,1,0:T(8,128)(2,1)}, u32[]{:S(2)}) copy-start(bf16[16,8,32,96]{3,2,1,0:T(8,128)(2,1)} %fusion.27) | copy-start | bytes 2359300
  104.3 4.4 %copy-start.8 = (bf16[16,8,96,48]{3,2,1,0:T(8,128)(2,1)S(1)}, bf16[16,8,96,48]{3,2,1,0:T(8,128)(2,1)}, u32[]{:S(2)}) copy-start(bf16[16,8,96,48]{3,2,1,0:T(8,128)(2,1)} %reshape.335) | copy-start | bytes 3538948
  119.5 2.7 copy-start.16
  119.5 2.8 copy-start.21
  119.5 2.8 copy-start.34
  122.4 3.3 %copy-start.43 = (bf16[96,128]{1,0:T(8,128)(2,1)S(1)}, bf16[96,128]{1,0:T(8,128)(2,1)}, u32[]{:S(2)}) copy-start(bf16[96,128]{1,0:T(8,128)(2,1)} %copy-done.42) | copy-start | bytes 73732
  122.4 3.3 %copy-start.45 = (bf16[96,128]{1,0:T(8,128)(2,1)S(1)}, bf16[96,128]{1,0:T(8,128)(2,1)}, u32[]{:S(2)}) copy-start(bf16[96,128]{1,0:T(8,128)(2,1)} %copy-done.44) | copy-start | bytes 73732
  124.4 1.2 copy-start.24
  125.7 1.1 copy-start.37
  125.7 1.3 copy-start.25
  126.7 2.3 copy-start.10
  126.7 2.3 copy-start.23
  126.7 2.3 copy-start.47
  126.7 2.3 copy-start.52
  129.0 3.3 %copy-start.50 = (f32[16,96]{1,0:T(8,128)S(1)}, f32[16,96]{1,0:T(8,128)}, u32[]{:S(2)}) copy-start(f32[16,96]{1,0:T(8,128)} %copy-done.49) | copy-start | bytes 18436
  129.0 3.3 %copy-start.53 = (f32[256]{0:T(256)S(1)}, f32[256]{0:T(256)}, u32[]{:S(2)}) copy-start(f32[256]{0:T(256)} %param.23) | copy-start | bytes 3076
  132.3 43.9 %copy-start.20 = (f32[16,48,256]{2,1,0:T(8,128)S(1)}, f32[16,48,256]{2,1,0:T(8,128)}, u32[]{:S(2)}) copy-start(f32[16,48,256]{2,1,0:T(8,128)} %copy-done.19) | copy-start | bytes 2359300
  133.4 44.8 %copy-start.18 = (f32[16,48,256]{2,1,0:T(8,128)S(1)}, f32[16,48,256]{2,1,0:T(8,128)}, u32[]{:S(2)}) copy-start(f32[16,48,256]{2,1,0:T(8,128)} %copy-done.17) | copy-start | bytes 2359300
  133.5 44.8 %copy-start.62 = (f32[256]{0:T(256)S(1)}, f32[256]{0:T(256)}, u32[]{:S(2)}) copy-start(f32[256]{0:T(256)} %param.37) | copy-start | bytes 3076
  176.2 2.1 copy-start.59
  271.8 6.9 %copy-start.41 = (f32[256,256]{1,0:T(8,128)S(1)}, f32[256,256]{1,0:T(8,128)}, u32[]{:S(2)}) copy-start(f32[256,256]{1,0:T(8,128)} %get-tuple-element.77) | copy-start | bytes 786436
  271.8 7.6 %copy-start.32 = (f32[256,1024]{1,0:T(8,128)S(1)}, f32[256,1024]{1,0:T(8,128)}, u32[]{:S(2)}) copy-start(f32[256,1024]{1,0:T(8,128)} %get-tuple-element.80) | copy-start | bytes 3145732
  273.5 6.8 %copy-start.31 = (f32[1024,256]{1,0:T(8,128)S(1)}, f32[1024,256]{1,0:T(8,128)}, u32[]{:S(2)}) copy-start(f32[1024,256]{1,0:T(8,128)} %get-tuple-element.82) | copy-start | bytes 3145732
  278.6 2.7 copy-start.1
  (1 other events, 0.6 us)
Sparse Core Ops, SparseCore 0:
  126.9 144.8 all-reduce.6
where the time goes:
time: 289 us; the launch traced here: 288 us
  waiting for transfers between devices  90.7 us (31%)
  local copies, waits for them, and re-layouts  69.2 us (24%)
  matrix products  54.8 us (19%)
  blocking collectives  41.8 us (14%)
  between operations  14.8 us (5%)
  other arithmetic  14.5 us (5%)
    psum x1, waiting for transfers between devices, body(): summed = tuple(lax.psum(mixing_terms + feed_terms, ('tm', 'roll')))  90.7 us
    psum x1, blocking collectives, body(): summed = tuple(lax.psum(mixing_terms + feed_terms, ('tm', 'roll')))  41.8 us
    reshape x2, local copies, waits for them, and re-layouts, shift_relative(): padded = padded.reshape(leading + (col_count + 1, row_count))  15.6 us
    unnamed x134, local copies, waits for them, and re-layouts  13.1 us
    reshape x2, local copies, waits for them, and re-layouts, shift_relative(): return padded[..., 1:, :].reshape(leading + (row_count, col_count))  11.3 us
    slice x1, local copies, waits for them, and re-layouts, shift_relative(): return padded[..., 1:, :].reshape(leading + (row_count, col_count))  6.61 us
    reshape x2, local copies, waits for them, and re-layouts, body(): placed = (query_vectors + position_bias).astype(jnp.bfloat16).reshape(cou...  6.07 us
  transfers between devices with their start and end apart: 2, of which 1 were waited for; matrix products, arithmetic and copies ran while one was open for 6% of the time, Pallas kernels for 0%

commit v1 on v0

v1 whole, which is shorter than its diff:
```python
import functools
import math

import jax
import jax.numpy as jnp
import numpy as np
from jax import lax
from jax.experimental import pallas as pl
from jax.experimental.pallas import tpu as pltpu
from jax.sharding import PartitionSpec as P

HEADS = 8
HEAD_DIM = 32
SEG = 48
STEP = 3
FEATURES = 256
HIDDEN = 1024
LANES = 128
GROUP = LANES // HEAD_DIM
EPSILON = 1e-05
MASKED = -1000000000.0
SCALING = 1.0 / math.sqrt(HEAD_DIM)
GELU_A = 0.7978845608028654
GELU_B = 0.044715 * GELU_A
BF = jnp.bfloat16
F32 = jnp.float32

EXPAND_AT = 0
SHRINK_AT = 1024
QUERY_AT = 2048
KEY_AT = 2304
VALUE_AT = 2560
OUTPUT_AT = 2816
RELATIVE_AT = 3072
VECTOR_AT = 3200
BUFFER_ROWS = 3328
(V_CONTENT, V_POSITION, V_GAIN1, V_SHIFT1, V_GAIN2, V_SHIFT2, V_SHRINK, V_EXPAND) = range(8)
VECTOR_ROWS = 16


def position_rows():
    distance = (2 * SEG - 1 - np.arange(2 * SEG)).astype(np.float32)
    freqs = 10000.0 ** (-(2.0 * np.arange(FEATURES // 2)) / FEATURES)
    angles = distance[:, None] * freqs.astype(np.float32)[None, :]
    table = np.concatenate([np.sin(angles), np.cos(angles)], axis=-1)
    return np.pad(table, ((0, LANES - 2 * SEG), (0, 0))).astype(BF)


def relative_basis():
    count = 2 * SEG
    k, c = np.arange(count)[:, None], np.arange(count)[None, :]
    basis = np.cos(np.pi * k * (2 * c + 1) / (2 * count)) * np.where(k == 0, np.sqrt(1.0 / count), np.sqrt(2.0 / count))
    basis = np.pad(basis, ((0, LANES - count), (0, LANES - count)))

    def parts(values):
        high = values.astype(BF)
        low = (values - high.astype(np.float64)).astype(BF)
        return np.concatenate([high, low], axis=0)

    return parts(basis), parts(basis @ position_rows().astype(np.float64))


def tables():
    return jnp.asarray(position_rows()), jnp.asarray(relative_basis()[0])


def dot(a, b):
    return lax.dot_general(a, b, (((1,), (0,)), ((), ())), preferred_element_type=F32)


def dot_t(a, b):
    return lax.dot_general(a, b, (((1,), (1,)), ((), ())), preferred_element_type=F32)


def t_dot(a, b):
    return lax.dot_general(a, b, (((0,), (0,)), ((), ())), preferred_element_type=F32)


def normalize(rows):
    center = rows - jnp.mean(rows, axis=-1, keepdims=True)
    spread = jnp.mean(center * center, axis=-1, keepdims=True)
    scale = lax.rsqrt(spread + EPSILON)
    return center * scale, scale


def column_sum(rows):
    return jnp.sum(rows, axis=0, keepdims=True)


def stack_heads(rows, head_masks):
    return jnp.concatenate([rows * mask for mask in head_masks], axis=0)


def unshift(rows, row_bits):
    rolled = jnp.concatenate(
        [pltpu.roll(rows[a : a + 8], SEG - 8 - a, 1) for a in range(0, SEG - 8, 8)] + [rows[SEG - 8 :]], axis=0
    )
    for step, bit in row_bits:
        rolled = jnp.where(bit, pltpu.roll(rolled, step, 1), rolled)
    return rolled


def pick_heads(rows, lane_head):
    picked = rows[0:SEG]
    for h in range(1, GROUP):
        picked = jnp.where(lane_head == h, rows[h * SEG : (h + 1) * SEG], picked)
    return picked


COPIES = 21
(C_X, C_START, C_ARRIVED, C_COT, C_GAIN1, C_SHIFT1, C_WQ, C_WK, C_WV, C_WR, C_CBIAS, C_PBIAS, C_WO,
 C_GAIN2, C_SHIFT2, C_W1, C_B1, C_W2, C_B2, C_TABLE, C_BASIS) = range(COPIES)
FIRST_COPIES = (C_TABLE, C_WR, C_X, C_GAIN1, C_SHIFT1, C_WQ, C_WK, C_WV, C_START, C_ARRIVED, C_CBIAS, C_PBIAS)
LATER_COPIES = (C_WO, C_GAIN2, C_SHIFT2, C_W1, C_B1, C_COT, C_W2, C_B2, C_BASIS)


def layer_kernel(place, horizon, *refs):
    sources, outputs, targets = refs[:COPIES], refs[COPIES : COPIES + 3], refs[COPIES + 3 : 2 * COPIES + 3]
    sems, scratch = refs[2 * COPIES + 3], refs[2 * COPIES + 4 :]
    moves = [pltpu.make_async_copy(a, b, sems.at[i]) for i, (a, b) in enumerate(zip(sources, targets))]
    for i in FIRST_COPIES + LATER_COPIES:
        moves[i].start()
    compute_layer(place, horizon, moves, *targets, *outputs, *scratch)


def compute_layer(
    place, horizon, moves, x, start, arrived, cot, gain1, shift1, wq, wk, wv, wr, cbias, pbias, wo,
    gain2, shift2, w1, b1, w2, b2, table, basis,
    out, dx, grads,
    nl, xhat, rstd, content, placed, keys, values, relblock, raw, probs, mixed,
    hid, n2, act, bpre, bmix, bhid, bhl, bcont, braw, kgm, kgs, vgm, vgs, vec,
):
    rows = x.shape[0]
    segments = rows // SEG
    position = place[0]
    vec[...] = jnp.zeros_like(vec)

    def loop(count, step):
        def body(i, carry):
            step(i)
            return carry
        lax.fori_loop(0, count, body, 0)

    for i in FIRST_COPIES:
        moves[i].wait()
    rel = dot(table[...], wr[...])
    wide_head = lax.broadcasted_iota(jnp.int32, (LANES, FEATURES), 1) // HEAD_DIM
    for h in range(HEADS):
        relblock[h * LANES : (h + 1) * LANES] = jnp.where(wide_head == h, rel, 0.0).astype(BF)

    def project(normed, at, count):
        keys[pl.ds(at, count)] = dot(normed, wk[...]).astype(BF)
        values[pl.ds(at, count)] = dot(normed, wv[...]).astype(BF)

    memory = jnp.where(position == 0, start[...].astype(F32), arrived[...].astype(F32))
    unit, scale = normalize(memory)
    xhat[0:SEG] = unit
    rstd[0:SEG] = scale
    normed = (unit * gain1[...] + shift1[...]).astype(BF)
    nl[0:SEG] = normed
    project(normed, 0, SEG)
    tail = keys.shape[0] - rows - SEG
    keys[rows + SEG :] = jnp.zeros((tail, FEATURES), BF)
    values[rows + SEG :] = jnp.zeros((tail, FEATURES), BF)

    block = 4 * SEG

    def first_rows(i):
        r = pl.multiple_of(i * block, block)
        unit, scale = normalize(x[pl.ds(r, block)].astype(F32))
        to = pl.multiple_of(r + SEG, SEG)
        xhat[pl.ds(to, block)] = unit
        rstd[pl.ds(to, block)] = scale
        normed = (unit * gain1[...] + shift1[...]).astype(BF)
        nl[pl.ds(to, block)] = normed
        project(normed, to, block)
        query = dot(normed, wq[...])
        content[pl.ds(r, block)] = (query + cbias[...]).astype(BF)
        low = (query + pbias[...]).astype(BF)
        placed[pl.ds(r, block)] = low
        raw[pl.ds(r, block)] = dot_t(low, relblock[...])

    loop(rows // block, first_rows)

    lane_head = lax.broadcasted_iota(jnp.int32, (SEG, LANES), 1) // HEAD_DIM
    head_masks = [(lane_head == h).astype(F32).astype(BF) for h in range(GROUP)]
    key_at = lax.broadcasted_iota(jnp.int32, (SEG, LANES), 1)
    query_at = lax.broadcasted_iota(jnp.int32, (SEG, LANES), 0) + SEG

    low_row = 7 - (query_at & 7)
    row_bits = [(step, (low_row & step) != 0) for step in (1, 2, 4)]

    def attend(s):
        r = pl.multiple_of(s * SEG, SEG)
        number = position * segments + s
        current = horizon[0, number]
        previous = jnp.where(number == 0, SEG // STEP, horizon[0, jnp.maximum(number - 1, 0)])
        live = key_at < jnp.where(key_at < SEG, STEP * previous, SEG + STEP * current)
        allowed = (key_at <= query_at) & (live | (key_at == query_at))
        for g in range(HEADS // GROUP):
            lanes = slice(g * LANES, (g + 1) * LANES)
            direct = dot_t(stack_heads(content[pl.ds(r, SEG), lanes], head_masks), keys[pl.ds(r, LANES), lanes])
            lows = []
            for h in range(GROUP):
                head = g * GROUP + h
                shifted = pltpu.roll(
                    raw[pl.ds(r, SEG), head * LANES : (head + 1) * LANES],
                    LANES - SEG + 1, 1, stride=1, stride_axis=0,
                )
                scores = jnp.where(allowed, (direct[h * SEG : (h + 1) * SEG] + shifted) * SCALING, MASKED)
                exponent = jnp.exp(scores - jnp.max(scores, axis=-1, keepdims=True))
                prob = exponent / jnp.sum(exponent, axis=-1, keepdims=True)
                probs[pl.ds(pl.multiple_of((s * HEADS + head) * SEG, SEG), SEG)] = prob
                lows.append(prob.astype(BF))
            both = dot(jnp.concatenate(lows, axis=0), values[pl.ds(r, LANES), lanes])
            mixed[pl.ds(r, SEG), lanes] = pick_heads(both, lane_head).astype(BF)

    loop(segments, attend)

    for i in LATER_COPIES:
        moves[i].wait()

    def feed(i):
        r = pl.multiple_of(i * block, block)
        at = pl.ds(r, block)
        hidden = x[at].astype(F32) + dot(mixed[at], wo[...])
        unit, scale = normalize(hidden)
        low = (unit * gain2[...] + shift2[...]).astype(BF)
        n2[at] = low
        back = cot[at]
        for f in range(HIDDEN // FEATURES):
            cols = slice(f * FEATURES, (f + 1) * FEATURES)
            v = dot(low, w1[:, cols]) + b1[:, cols]
            square = v * v
            half = 0.5 + 0.5 * jnp.tanh(v * (GELU_A + GELU_B * square))
            active = v * half
            act[at, cols] = active.astype(BF)
            slope = half + (2.0 * active) * (1.0 - half) * (GELU_A + (3.0 * GELU_B) * square)
            grad = dot_t(back, w2[cols]) * slope
            vec[V_EXPAND + f : V_EXPAND + f + 1] += column_sum(grad)
            bpre[at, cols] = grad.astype(BF)
        out[at] = (hidden + dot(act[at], w2[...]) + b2[...]).astype(BF)
        back = back.astype(F32)
        bn = dot_t(bpre[at], w1[...])
        vec[V_SHRINK : V_SHRINK + 1] += column_sum(back)
        vec[V_GAIN2 : V_GAIN2 + 1] += column_sum(bn * unit)
        vec[V_SHIFT2 : V_SHIFT2 + 1] += column_sum(bn)
        u = bn * gain2[...]
        inner = u - jnp.mean(u, axis=-1, keepdims=True) - unit * jnp.mean(u * unit, axis=-1, keepdims=True)
        bh = back + inner * scale
        bhid[at] = bh
        bl = bh.astype(BF)
        bhl[at] = bl
        bmix[at] = dot_t(bl, wo[...]).astype(BF)

    loop(rows // block, feed)

    for f in range(HIDDEN // FEATURES):
        cols = slice(f * FEATURES, (f + 1) * FEATURES)
        grads[EXPAND_AT + f * FEATURES : EXPAND_AT + (f + 1) * FEATURES] = t_dot(n2[...], bpre[:, cols]).astype(BF)
        grads[SHRINK_AT + f * FEATURES : SHRINK_AT + (f + 1) * FEATURES] = t_dot(act[:, cols], cot[...]).astype(BF)
    grads[OUTPUT_AT : OUTPUT_AT + FEATURES] = t_dot(mixed[...], bhl[...]).astype(BF)

    def attend_back(s):
        r = pl.multiple_of(s * SEG, SEG)
        at = pl.ds(r, SEG)
        for g in range(HEADS // GROUP):
            lanes = slice(g * LANES, (g + 1) * LANES)
            window = pl.ds(r, LANES)
            back = stack_heads(bmix[at, lanes], head_masks)
            wide = dot_t(back, values[window, lanes])
            lows, grad_lows = [], []
            for h in range(GROUP):
                head = g * GROUP + h
                prob = probs[pl.ds(pl.multiple_of((s * HEADS + head) * SEG, SEG), SEG)]
                bp = wide[h * SEG : (h + 1) * SEG]
                bs = prob * (bp - jnp.sum(bp * prob, axis=-1, keepdims=True))
                lows.append(prob.astype(BF))
                grad_lows.append(bs.astype(BF))
                braw[at, head * LANES : (head + 1) * LANES] = unshift(bs, row_bits).astype(BF)
            low = jnp.concatenate(lows, axis=0)
            grad_low = jnp.concatenate(grad_lows, axis=0)
            vg = t_dot(low, back).astype(BF)
            vgm[at, lanes] = vg[0:SEG]
            vgs[at, lanes] = vg[SEG : 2 * SEG]
            kg = (t_dot(grad_low, stack_heads(content[at, lanes], head_masks)) * SCALING).astype(BF)
            kgm[at, lanes] = kg[0:SEG]
            kgs[at, lanes] = kg[SEG : 2 * SEG]
            bcont[at, lanes] = pick_heads(dot(grad_low, keys[window, lanes]), lane_head) * SCALING

    loop(segments, attend_back)

    def last_rows(i):
        r = pl.multiple_of(i * block, block)
        at = pl.ds(r, block)
        to = pl.ds(pl.multiple_of(r + SEG, SEG), block)
        bplace = dot(braw[at], relblock[...]) * SCALING
        bc = bcont[at]
        vec[V_CONTENT : V_CONTENT + 1] += column_sum(bc)
        vec[V_POSITION : V_POSITION + 1] += column_sum(bplace)
        bq = (bc + bplace).astype(BF)
        bhl[at] = bq
        bn = dot_t(bq, wq[...]) + dot_t(kgs[at], wk[...]) + dot_t(vgs[at], wv[...])
        bm = dot_t(kgm[at], wk[...]) + dot_t(vgm[at], wv[...])
        unit = xhat[to]
        vec[V_GAIN1 : V_GAIN1 + 1] += column_sum(bn * unit) + column_sum(bm * xhat[at])
        vec[V_SHIFT1 : V_SHIFT1 + 1] += column_sum(bn) + column_sum(bm)
        u = bn * gain1[...]
        inner = u - jnp.mean(u, axis=-1, keepdims=True) - unit * jnp.mean(u * unit, axis=-1, keepdims=True)
        dx[at] = (bhid[at] + inner * rstd[to]).astype(BF)

    loop(rows // block, last_rows)

    segment_rows = nl[SEG : SEG + rows]
    memory_rows = nl[0:rows]
    grads[QUERY_AT : QUERY_AT + FEATURES] = t_dot(segment_rows, bhl[...]).astype(BF)
    grads[KEY_AT : KEY_AT + FEATURES] = (t_dot(segment_rows, kgs[...]) + t_dot(memory_rows, kgm[...])).astype(BF)
    grads[VALUE_AT : VALUE_AT + FEATURES] = (t_dot(segment_rows, vgs[...]) + t_dot(memory_rows, vgm[...])).astype(BF)
    for g in range(HEADS // GROUP):
        lanes = slice(g * LANES, (g + 1) * LANES)
        across = t_dot(placed[:, lanes], braw[:, g * GROUP * LANES : (g + 1) * GROUP * LANES])
        back = jnp.concatenate(
            [across[h * HEAD_DIM : (h + 1) * HEAD_DIM, h * LANES : (h + 1) * LANES] for h in range(GROUP)], axis=0
        ) * SCALING
        high = back.astype(BF)
        low = (back - high.astype(F32)).astype(BF)
        cosines = dot_t(basis[0:LANES], high) + (dot_t(basis[LANES:], high) + dot_t(basis[0:LANES], low))
        grads[RELATIVE_AT : RELATIVE_AT + LANES, lanes] = cosines.astype(BF)
    grads[VECTOR_AT : VECTOR_AT + VECTOR_ROWS] = vec[...].astype(BF)
    grads[VECTOR_AT + VECTOR_ROWS :] = jnp.zeros((BUFFER_ROWS - VECTOR_AT - VECTOR_ROWS, FEATURES), BF)


def run_layer(place, horizon, x, start, arrived, cot, table, basis, params):
    rows = x.shape[0]
    operands = (x, start, arrived, cot, *params, table, basis)
    vmem = pl.BlockSpec(memory_space=pltpu.VMEM)
    hbm = pl.BlockSpec(memory_space=pltpu.HBM)
    smem = pl.BlockSpec(memory_space=pltpu.SMEM)
    padded = rows + SEG + LANES - 2 * SEG
    scratch = [
        pltpu.VMEM((rows + SEG, FEATURES), BF),
        pltpu.VMEM((rows + SEG, FEATURES), F32),
        pltpu.VMEM((rows + SEG, 1), F32),
        pltpu.VMEM((rows, FEATURES), BF),
        pltpu.VMEM((rows, FEATURES), BF),
        pltpu.VMEM((padded, FEATURES), BF),
        pltpu.VMEM((padded, FEATURES), BF),
        pltpu.VMEM((HEADS * LANES, FEATURES), BF),
        pltpu.VMEM((rows, HEADS * LANES), F32),
        pltpu.VMEM((rows * HEADS, LANES), F32),
        pltpu.VMEM((rows, FEATURES), BF),
        pltpu.VMEM((rows, FEATURES), F32),
        pltpu.VMEM((rows, FEATURES), BF),
        pltpu.VMEM((rows, HIDDEN), BF),
        pltpu.VMEM((rows, HIDDEN), BF),
        pltpu.VMEM((rows, FEATURES), BF),
        pltpu.VMEM((rows, FEATURES), F32),
        pltpu.VMEM((rows, FEATURES), BF),
        pltpu.VMEM((rows, FEATURES), F32),
        pltpu.VMEM((rows, HEADS * LANES), BF),
        pltpu.VMEM((rows, FEATURES), BF),
        pltpu.VMEM((rows, FEATURES), BF),
        pltpu.VMEM((rows, FEATURES), BF),
        pltpu.VMEM((rows, FEATURES), BF),
        pltpu.VMEM((VECTOR_ROWS, FEATURES), F32),
    ]
    return pl.pallas_call(
        layer_kernel,
        out_shape=(
            jax.ShapeDtypeStruct((rows, FEATURES), BF),
            jax.ShapeDtypeStruct((rows, FEATURES), BF),
            jax.ShapeDtypeStruct((BUFFER_ROWS, FEATURES), BF),
        ),
        in_specs=[smem, smem] + [hbm] * COPIES,
        out_specs=(vmem, vmem, vmem),
        scratch_shapes=[pltpu.VMEM(a.shape, a.dtype) for a in operands]
        + [pltpu.SemaphoreType.DMA((COPIES,))]
        + scratch,
        compiler_params=pltpu.CompilerParams(vmem_limit_bytes=63 * 1024 * 1024),
        name="layer",
    )(place, horizon, *operands)


def unpack_kernel(
    place, own, other, turned,
    gain1, shift1, wq, wk, wv, wr, cbias, pbias, wo, gain2, shift2, w1, b1, w2, b2,
    whole,
):
    first = place[1] == 0
    half = BUFFER_ROWS // 2

    @pl.when(first)
    def _():
        whole[0:half] = own[...]
        whole[half:] = other[...]

    @pl.when(jnp.logical_not(first))
    def _():
        whole[0:half] = other[...]
        whole[half:] = own[...]

    for f in range(HIDDEN // FEATURES):
        w1[:, f * FEATURES : (f + 1) * FEATURES] = whole[
            EXPAND_AT + f * FEATURES : EXPAND_AT + (f + 1) * FEATURES
        ].astype(F32)
    w2[...] = whole[SHRINK_AT : SHRINK_AT + HIDDEN].astype(F32)
    for ref, at in ((wq, QUERY_AT), (wk, KEY_AT), (wv, VALUE_AT), (wo, OUTPUT_AT)):
        ref[...] = whole[at : at + FEATURES].astype(F32)
    cosines = whole[RELATIVE_AT : RELATIVE_AT + LANES]
    wr[...] = t_dot(turned[0:LANES], cosines) + t_dot(turned[LANES:], cosines)
    vectors = whole[VECTOR_AT : VECTOR_AT + VECTOR_ROWS].astype(F32)
    for ref, at in (
        (cbias, V_CONTENT), (pbias, V_POSITION), (gain1, V_GAIN1), (shift1, V_SHIFT1),
        (gain2, V_GAIN2), (shift2, V_SHIFT2), (b2, V_SHRINK),
    ):
        ref[...] = vectors[at]
    for f in range(HIDDEN // FEATURES):
        b1[f * FEATURES : (f + 1) * FEATURES] = vectors[V_EXPAND + f]


def unpack(place, own, other, turned):
    vmem = pl.BlockSpec(memory_space=pltpu.VMEM)
    smem = pl.BlockSpec(memory_space=pltpu.SMEM)
    vector = jax.ShapeDtypeStruct((FEATURES,), F32)
    square = jax.ShapeDtypeStruct((FEATURES, FEATURES), F32)
    shapes = (
        vector, vector, square, square, square, square, vector, vector, square, vector, vector,
        jax.ShapeDtypeStruct((FEATURES, HIDDEN), F32),
        jax.ShapeDtypeStruct((HIDDEN,), F32),
        jax.ShapeDtypeStruct((HIDDEN, FEATURES), F32),
        vector,
    )
    return pl.pallas_call(
        unpack_kernel,
        out_shape=shapes,
        in_specs=[smem, vmem, vmem, vmem],
        out_specs=(vmem,) * len(shapes),
        scratch_shapes=[pltpu.VMEM((BUFFER_ROWS, FEATURES), BF)],
        compiler_params=pltpu.CompilerParams(vmem_limit_bytes=32 * 1024 * 1024),
        name="unpack",
    )(place, own, other, turned)


AXES = ("tm", "roll")


def exchange_plan(roll_count, tm_count):
    tm_bits = tm_count.bit_length() - 1
    roll_bits = roll_count.bit_length() - 1
    high = [roll_bits + b for b in range(1, tm_bits)]
    rolls = list(range(roll_bits))
    even = high + rolls
    odd = rolls[:1] + high + rolls[1:]
    return [(roll_bits, roll_bits)] + list(zip(even, odd))


def swap(value, bits, roll_count, count):
    even, odd = bits
    pairs = [(d, d ^ (1 << (odd if (d // roll_count) & 1 else even))) for d in range(count)]
    return lax.ppermute(value, AXES, pairs)


def add_low(a, b):
    return (a.astype(F32) + b.astype(F32)).astype(BF)


def sum_everywhere(buffer, core):
    roll_count, tm_count = lax.axis_size("roll"), lax.axis_size("tm")
    count = roll_count * tm_count
    me = lax.axis_index("tm") * roll_count + lax.axis_index("roll")
    stages = exchange_plan(roll_count, tm_count)
    halving = 4
    bits = []
    for even, odd in stages[:halving]:
        bit = jnp.where(core == 0, (me >> even) & 1, (me >> odd) & 1)
        half = buffer.shape[0] // 2
        sent = lax.dynamic_slice_in_dim(buffer, (1 - bit) * half, half, 0)
        kept = lax.dynamic_slice_in_dim(buffer, bit * half, half, 0)
        buffer = add_low(kept, swap(sent, (even, odd), roll_count, count))
        bits.append(bit)
    for even, odd in stages[halving:]:
        buffer = add_low(buffer, swap(buffer, (even, odd), roll_count, count))
    for (even, odd), bit in list(zip(stages, bits))[:0:-1]:
        other = swap(buffer, (even, odd), roll_count, count)
        first = bit == 0
        buffer = jnp.concatenate([jnp.where(first, buffer, other), jnp.where(first, other, buffer)], axis=0)
    return buffer, swap(buffer, stages[0], roll_count, count)


def body(
    layer_input, start_memory, horizon, cotangent, first_gain, first_shift, query_projection_weight,
    key_projection_weight, value_projection_weight, relative_weight, content_bias, position_bias,
    output_weight, second_gain, second_shift, expand_weight, expand_bias, shrink_weight, shrink_bias,
):
    rollouts, columns, features = layer_input.shape
    x = layer_input.reshape(rollouts * columns, features)
    position = lax.axis_index("tm")
    tm_count = lax.axis_size("tm")
    arrived = lax.ppermute(x[-SEG:], "tm", [(i, i + 1) for i in range(tm_count - 1)])
    core = position & 1
    place = jnp.stack([position, core]).astype(jnp.int32)
    table = jnp.asarray(position_rows())
    basis, turned = (jnp.asarray(part) for part in relative_basis())

    def row(v):
        return v.reshape(1, -1)

    params = (
        row(first_gain), row(first_shift), query_projection_weight, key_projection_weight,
        value_projection_weight, relative_weight, row(content_bias), row(position_bias), output_weight,
        row(second_gain), row(second_shift), expand_weight, row(expand_bias), shrink_weight, row(shrink_bias),
    )
    out, dx, grads = run_layer(
        place, horizon, x, start_memory.reshape(SEG, features), arrived,
        cotangent.reshape(rollouts * columns, features), table, basis, params,
    )
    own, other = sum_everywhere(grads, core)
    summed = unpack(place, own, other, turned)
    return (out.reshape(layer_input.shape), dx.reshape(layer_input.shape)) + tuple(summed)


def solution(mesh):
    in_specs = (
        P("roll", "tm", None), P("roll", None, None), P("roll", None), P("roll", "tm", None),
    ) + (P(),) * 15
    out_specs = (P("roll", "tm", None), P("roll", "tm", None)) + (P(),) * 15
    return jax.shard_map(body, mesh=mesh, in_specs=in_specs, out_specs=out_specs, check_vma=False)
```

time: 289 us -> 112 us (0.39)
  local copies, waits for them, and re-layouts: 69.2 us -> 2.78 us
  matrix products: 54.8 us -> 0 us
  waiting for transfers between devices: 90.7 us -> 39.3 us
  Pallas kernels: 0 us -> 49.5 us
  blocking collectives: 41.8 us -> 0 us
  starting transfers between devices: 2.38 us -> 17.9 us
  between operations: 14.8 us -> 0.78 us
  other arithmetic: 14.5 us -> 1.38 us
    psum x1 -> x0, waiting for transfers between devices: 90.7 us -> none  [body(): summed = tuple(lax.psum(mixing_terms + feed_terms, ('tm', 'roll')))]
    dot_general x29 -> x0, matrix products: 54.8 us -> none  [the longest x1 3.56 us: score_block(): jnp.einsum('bihe,bjhe->bhij', content, key_heads, preferred_element_type=...]
    pallas_call x0 -> x2, Pallas kernels: none -> 49.5 us  [the longest x1 46.9 us: run_layer(): pl.pallas_call(layer_kernel, out_shape=(jax.ShapeDtypeStruct((rows, FEATU...]
    psum x1 -> x0, blocking collectives: 41.8 us -> none  [body(): summed = tuple(lax.psum(mixing_terms + feed_terms, ('tm', 'roll')))]
    ppermute x1 -> x10, waiting for transfers between devices: 0.01 us -> 39.3 us  [the longest x9 39.1 us: swap(): return lax.ppermute(value, AXES, pairs)]
    reshape x10 -> x0, local copies, waits for them, and re-layouts: 37.2 us -> none  [the longest x2 15.6 us: shift_relative(): padded = padded.reshape(leading + (col_count + 1, row_count))]
    ppermute x1 -> x10, starting transfers between devices: 2.35 us -> 17.9 us  [the longest x9 15.6 us: swap(): return lax.ppermute(value, AXES, pairs)]
    unnamed x134 -> x8, local copies, waits for them, and re-layouts: 13.1 us -> 0.62 us
  transfers between devices with their start and end apart: 2 -> 10, of which waited for: 1 -> 10; matrix products, arithmetic and copies ran while one was open for 6% -> 1% of each run, Pallas kernels for 0% -> 0%
where the time goes in v1:
time: 112 us
  Pallas kernels  49.5 us (44%)
  waiting for transfers between devices  39.3 us (35%)
  starting transfers between devices  17.9 us (16%)
  local copies, waits for them, and re-layouts  2.78 us (2%)
  other arithmetic  1.38 us (1%)
    pallas_call x1, Pallas kernels, run_layer(): pl.pallas_call(layer_kernel, out_shape=(jax.ShapeDtypeStruct((rows, FEATU...  46.9 us
    ppermute x9, waiting for transfers between devices, swap(): return lax.ppermute(value, AXES, pairs)  39.1 us
    ppermute x9, starting transfers between devices, swap(): return lax.ppermute(value, AXES, pairs)  15.6 us
    pallas_call x1, Pallas kernels, unpack(): pl.pallas_call(unpack_kernel, out_shape=shapes, in_specs=[smem, vmem, vme...  2.59 us
    ppermute x1, starting transfers between devices, body(): lax.ppermute(x[-SEG:], 'tm', [(i, i + 1) for i in range(tm_count - 1)])  2.35 us
  transfers between devices with their start and end apart: 10, of which 10 were waited for; matrix products, arithmetic and copies ran while one was open for 1% of the time, Pallas kernels for 0%

profile of v1, /device:TPU:0, one launch (start us, length us, event | category | flops | bytes accessed | tf_op | source)
XLA Modules:
  0.0 111.6 jit_solution(10552626450709001134)
XLA Ops:
  0.7 0.7 slice_bitcast_fusion
  1.4 2.3 %collective-permute-start = (bf16[48,256]{1,0:T(8,128)(2,1)S(1)}, bf16[48,256]{1,0:T(8,128)(2,1)S(1)}, u32[]{:S(2)}, u32[]{:S(2)}) collective-permute-start(bf16[48,256]{1,0:T(8,128)(2,1)S(1)} %slice_bitcast_fusion), channel_id=1, source_target_pairs={{0,8},{8,16},{16,24},{1,9},{9,17},{17,25},{2,10},{10,18},{18,26},{... | collective-permute-start | bytes 73736 | tf_op jit(solution)/shard_map/ppermute | solution.py:499
  3.8 0.6 pad_add_fusion.place
  4.3 0.2 collective-permute-done.refs_2_
  4.6 0.0 copy-start.3
  4.6 0.6 copy-done.3
  5.2 46.9 %layer.1 = (bf16[768,256]{1,0:T(8,128)(2,1)}, bf16[768,256]{1,0:T(8,128)(2,1)}, bf16[3328,256]{1,0:T(8,128)(2,1)}) custom-call(s32[2]{0:T(128)} %pad_add_fusion.place, s32[1,64]{1,0:T(1,128)} %horizon.1, bf16[768,256]{1,0:T(8,128)(2,1)} %bitcast.17, bf16[48,256]{1,0:T(8,128)(2,1)} %bitcast.19, bf16[48,256]{1,0:T(8,128)(2,1)} %copy-done.3, ...), custom_call_target="tpu_custom_call" | custom-call | tf_op jit(solution)/shard_map/layer/pallas_call | solution.py:367
  52.1 0.0 copy-start.2
  52.1 1.3 %constant_dynamic-slice_fusion.3 = bf16[1664,256]{1,0:T(8,128)(2,1)S(1)} fusion(bf16[3328,256]{1,0:T(8,128)(2,1)} %get-tuple-element.37, s32[]{:T(128)S(6)} %select_n.75), kind=kLoop, calls=%fused_computation.18 | loop fusion | bytes 1703940 | tf_op jit(solution)/shard_map/dynamic_slice | solution.py:477
  53.4 2.8 %collective-permute-start.1 = (bf16[1664,256]{1,0:T(8,128)(2,1)S(1)}, bf16[1664,256]{1,0:T(8,128)(2,1)S(1)}, u32[]{:S(2)}, u32[]{:S(2)}) collective-permute-start(bf16[1664,256]{1,0:T(8,128)(2,1)S(1)} %constant_dynamic-slice_fusion.3), channel_id=1, source_target_pairs={{0,8},{1,9},{2,10},{3,11},{4,12},{5,13},{6,14},{7,15},{8,0},{9,1},... | collective-permute-start | bytes 2555912 | tf_op jit(solution)/shard_map/ppermute | solution.py:460
  56.2 2.0 %collective-permute-done.1 = bf16[1664,256]{1,0:T(8,128)(2,1)S(1)} collective-permute-done((bf16[1664,256]{1,0:T(8,128)(2,1)S(1)}, bf16[1664,256]{1,0:T(8,128)(2,1)S(1)}, u32[]{:S(2)}, u32[]{:S(2)}) %collective-permute-start.1) | collective-permute-done | bytes 852000 | tf_op jit(solution)/shard_map/ppermute | solution.py:460
  58.2 0.0 copy-done.2
  58.2 0.2 add_convert_fusion
  58.5 2.6 %collective-permute-start.2 = (bf16[832,256]{1,0:T(8,128)(2,1)S(1)}, bf16[832,256]{1,0:T(8,128)(2,1)S(1)}, u32[]{:S(2)}, u32[]{:S(2)}) collective-permute-start(bf16[832,256]{1,0:T(8,128)(2,1)S(1)} %constant_dynamic-slice_fusion.2), channel_id=1, source_target_pairs={{0,16},{1,17},{2,18},{3,19},{4,20},{5,21},{6,22},{7,23},{8,9},{9,8... | collective-permute-start | bytes 1277960 | tf_op jit(solution)/shard_map/ppermute | solution.py:460
  61.1 6.1 %collective-permute-done.2 = bf16[832,256]{1,0:T(8,128)(2,1)S(1)} collective-permute-done((bf16[832,256]{1,0:T(8,128)(2,1)S(1)}, bf16[832,256]{1,0:T(8,128)(2,1)S(1)}, u32[]{:S(2)}, u32[]{:S(2)}) %collective-permute-start.2) | collective-permute-done | bytes 426016 | tf_op jit(solution)/shard_map/ppermute | solution.py:460
  67.2 0.1 add_convert_fusion.1
  67.4 1.6 %collective-permute-start.3 = (bf16[416,256]{1,0:T(8,128)(2,1)S(1)}, bf16[416,256]{1,0:T(8,128)(2,1)S(1)}, u32[]{:S(2)}, u32[]{:S(2)}) collective-permute-start(bf16[416,256]{1,0:T(8,128)(2,1)S(1)} %constant_dynamic-slice_fusion.1), channel_id=1, source_target_pairs={{0,1},{1,0},{2,3},{3,2},{4,5},{5,4},{6,7},{7,6},{8,24},{9,25},{10,... | collective-permute-start | bytes 638984 | tf_op jit(solution)/shard_map/ppermute | solution.py:460
  68.9 4.3 %collective-permute-done.3 = bf16[416,256]{1,0:T(8,128)(2,1)S(1)} collective-permute-done((bf16[416,256]{1,0:T(8,128)(2,1)S(1)}, bf16[416,256]{1,0:T(8,128)(2,1)S(1)}, u32[]{:S(2)}, u32[]{:S(2)}) %collective-permute-start.3) | collective-permute-done | bytes 213024 | tf_op jit(solution)/shard_map/ppermute | solution.py:460
  73.3 0.1 add_convert_fusion.2
  73.4 1.6 %collective-permute-start.4 = (bf16[208,256]{1,0:T(8,128)(2,1)S(1)}, bf16[208,256]{1,0:T(8,128)(2,1)S(1)}, u32[]{:S(2)}, u32[]{:S(2)}) collective-permute-start(bf16[208,256]{1,0:T(8,128)(2,1)S(1)} %constant_dynamic-slice_fusion), channel_id=1, source_target_pairs={{0,2},{1,3},{2,0},{3,1},{4,6},{5,7},{6,4},{7,5},{8,10},{9,11},{10,... | collective-permute-start | bytes 319496 | tf_op jit(solution)/shard_map/ppermute | solution.py:460
  75.0 3.1 %collective-permute-done.4 = bf16[208,256]{1,0:T(8,128)(2,1)S(1)} collective-permute-done((bf16[208,256]{1,0:T(8,128)(2,1)S(1)}, bf16[208,256]{1,0:T(8,128)(2,1)S(1)}, u32[]{:S(2)}, u32[]{:S(2)}) %collective-permute-start.4) | collective-permute-done | bytes 106528 | tf_op jit(solution)/shard_map/ppermute | solution.py:460
  78.2 2.7 %collective-permute-start.5 = (bf16[208,256]{1,0:T(8,128)(2,1)S(1)}, bf16[208,256]{1,0:T(8,128)(2,1)S(1)}, u32[]{:S(2)}, u32[]{:S(2)}) collective-permute-start(bf16[208,256]{1,0:T(8,128)(2,1)S(1)} %add_convert_fusion.4), channel_id=1, source_target_pairs={{0,4},{1,5},{2,6},{3,7},{4,0},{5,1},{6,2},{7,3},{8,12},{9,13},{10,... | collective-permute-start | bytes 319496 | tf_op jit(solution)/shard_map/ppermute | solution.py:460
  80.8 4.3 %collective-permute-done.5 = bf16[208,256]{1,0:T(8,128)(2,1)S(1)} collective-permute-done((bf16[208,256]{1,0:T(8,128)(2,1)S(1)}, bf16[208,256]{1,0:T(8,128)(2,1)S(1)}, u32[]{:S(2)}, u32[]{:S(2)}) %collective-permute-start.5) | collective-permute-done | bytes 106528 | tf_op jit(solution)/shard_map/ppermute | solution.py:460
  85.1 0.7 collective-permute-start.6
  85.8 4.1 %collective-permute-done.6 = bf16[208,256]{1,0:T(8,128)(2,1)S(1)} collective-permute-done((bf16[208,256]{1,0:T(8,128)(2,1)S(1)}, bf16[208,256]{1,0:T(8,128)(2,1)S(1)}, u32[]{:S(2)}, u32[]{:S(2)}) %collective-permute-start.6) | collective-permute-done | bytes 106528 | tf_op jit(solution)/shard_map/ppermute | solution.py:460
  89.9 1.6 %collective-permute-start.7 = (bf16[416,256]{1,0:T(8,128)(2,1)S(1)}, bf16[416,256]{1,0:T(8,128)(2,1)S(1)}, u32[]{:S(2)}, u32[]{:S(2)}) collective-permute-start(bf16[416,256]{1,0:T(8,128)(2,1)S(1)} %pad_maximum_fusion.2), channel_id=1, source_target_pairs={{0,1},{1,0},{2,3},{3,2},{4,5},{5,4},{6,7},{7,6},{8,24},{9,25},{10,... | collective-permute-start | bytes 638984 | tf_op jit(solution)/shard_map/ppermute | solution.py:460
  91.5 6.6 %collective-permute-done.7 = bf16[416,256]{1,0:T(8,128)(2,1)S(1)} collective-permute-done((bf16[416,256]{1,0:T(8,128)(2,1)S(1)}, bf16[416,256]{1,0:T(8,128)(2,1)S(1)}, u32[]{:S(2)}, u32[]{:S(2)}) %collective-permute-start.7) | collective-permute-done | bytes 213024 | tf_op jit(solution)/shard_map/ppermute | solution.py:460
  98.1 0.1 broadcast_select_fusion.3
  98.2 2.0 %collective-permute-start.8 = (bf16[832,256]{1,0:T(8,128)(2,1)S(1)}, bf16[832,256]{1,0:T(8,128)(2,1)S(1)}, u32[]{:S(2)}, u32[]{:S(2)}) collective-permute-start(bf16[832,256]{1,0:T(8,128)(2,1)S(1)} %pad_maximum_fusion.1), channel_id=1, source_target_pairs={{0,16},{1,17},{2,18},{3,19},{4,20},{5,21},{6,22},{7,23},{8,9},{9,8... | collective-permute-start | bytes 1277960 | tf_op jit(solution)/shard_map/ppermute | solution.py:460
  100.2 0.0 copy-start
  100.2 0.0 copy-start.1
  100.2 6.2 %collective-permute-done.8 = bf16[832,256]{1,0:T(8,128)(2,1)S(1)} collective-permute-done((bf16[832,256]{1,0:T(8,128)(2,1)S(1)}, bf16[832,256]{1,0:T(8,128)(2,1)S(1)}, u32[]{:S(2)}, u32[]{:S(2)}) %collective-permute-start.8) | collective-permute-done | bytes 426016 | tf_op jit(solution)/shard_map/ppermute | solution.py:460
  106.4 0.1 broadcast_select_fusion.1
  106.5 0.1 pad_maximum_fusion.own
  106.6 0.1 collective-permute-start.9
  106.7 2.4 %collective-permute-done.9.other = bf16[1664,256]{1,0:T(8,128)(2,1)S(1)} collective-permute-done((bf16[1664,256]{1,0:T(8,128)(2,1)S(1)}, bf16[1664,256]{1,0:T(8,128)(2,1)S(1)}, u32[]{:S(2)}, u32[]{:S(2)}) %collective-permute-start.9) | collective-permute-done | bytes 852000 | tf_op jit(solution)/shard_map/ppermute | solution.py:460
  109.0 0.0 copy-done
  109.0 0.0 copy-done.1
  109.0 2.6 %unpack.1 = (f32[256]{0:T(256)}, f32[256]{0:T(256)}, f32[256,256]{1,0:T(8,128)}, f32[256,256]{1,0:T(8,128)}, f32[256,256]{1,0:T(8,128)}, /*index=5*/f32[256,256]...) custom-call(s32[2]{0:T(128)S(1)} %copy-done.1, ...), custom_call_target="tpu_custom_call" | custom-call | tf_op jit(solution)/shard_map/unpack/pallas_call | solution.py:433
  (8 shorter events, 0.2 us)
Async XLA Ops:
  1.4 3.2 %collective-permute-start = (bf16[48,256]{1,0:T(8,128)(2,1)S(1)}, bf16[48,256]{1,0:T(8,128)(2,1)S(1)}, u32[]{:S(2)}, u32[]{:S(2)}) collective-permute-start(bf16[48,256]{1,0:T(8,128)(2,1)S(1)} %slice_bitcast_fusion), channel_id=1, source_target_pairs={{0,8},{8,16},{16,24},{1,9},{9,17},{17,25},{2,10},{10,18},{18,26},{... | collective-permute-start | bytes 73736 | tf_op jit(solution)/shard_map/ppermute | solution.py:499
  4.6 0.6 copy-start.3
  52.1 6.2 %copy-start.2 = (bf16[3328,256]{1,0:T(8,128)(2,1)S(1)}, bf16[3328,256]{1,0:T(8,128)(2,1)}, u32[]{:S(2)}) copy-start(bf16[3328,256]{1,0:T(8,128)(2,1)} %get-tuple-element.37) | copy-start | bytes 5111812
  53.4 4.8 %collective-permute-start.1 = (bf16[1664,256]{1,0:T(8,128)(2,1)S(1)}, bf16[1664,256]{1,0:T(8,128)(2,1)S(1)}, u32[]{:S(2)}, u32[]{:S(2)}) collective-permute-start(bf16[1664,256]{1,0:T(8,128)(2,1)S(1)} %constant_dynamic-slice_fusion.3), channel_id=1, source_target_pairs={{0,8},{1,9},{2,10},{3,11},{4,12},{5,13},{6,14},{7,15},{8,0},{9,1},... | collective-permute-start | bytes 2555912 | tf_op jit(solution)/shard_map/ppermute | solution.py:460
  58.5 8.7 %collective-permute-start.2 = (bf16[832,256]{1,0:T(8,128)(2,1)S(1)}, bf16[832,256]{1,0:T(8,128)(2,1)S(1)}, u32[]{:S(2)}, u32[]{:S(2)}) collective-permute-start(bf16[832,256]{1,0:T(8,128)(2,1)S(1)} %constant_dynamic-slice_fusion.2), channel_id=1, source_target_pairs={{0,16},{1,17},{2,18},{3,19},{4,20},{5,21},{6,22},{7,23},{8,9},{9,8... | collective-permute-start | bytes 1277960 | tf_op jit(solution)/shard_map/ppermute | solution.py:460
  67.4 5.9 %collective-permute-start.3 = (bf16[416,256]{1,0:T(8,128)(2,1)S(1)}, bf16[416,256]{1,0:T(8,128)(2,1)S(1)}, u32[]{:S(2)}, u32[]{:S(2)}) collective-permute-start(bf16[416,256]{1,0:T(8,128)(2,1)S(1)} %constant_dynamic-slice_fusion.1), channel_id=1, source_target_pairs={{0,1},{1,0},{2,3},{3,2},{4,5},{5,4},{6,7},{7,6},{8,24},{9,25},{10,... | collective-permute-start | bytes 638984 | tf_op jit(solution)/shard_map/ppermute | solution.py:460
  73.4 4.8 %collective-permute-start.4 = (bf16[208,256]{1,0:T(8,128)(2,1)S(1)}, bf16[208,256]{1,0:T(8,128)(2,1)S(1)}, u32[]{:S(2)}, u32[]{:S(2)}) collective-permute-start(bf16[208,256]{1,0:T(8,128)(2,1)S(1)} %constant_dynamic-slice_fusion), channel_id=1, source_target_pairs={{0,2},{1,3},{2,0},{3,1},{4,6},{5,7},{6,4},{7,5},{8,10},{9,11},{10,... | collective-permute-start | bytes 319496 | tf_op jit(solution)/shard_map/ppermute | solution.py:460
  78.2 6.9 %collective-permute-start.5 = (bf16[208,256]{1,0:T(8,128)(2,1)S(1)}, bf16[208,256]{1,0:T(8,128)(2,1)S(1)}, u32[]{:S(2)}, u32[]{:S(2)}) collective-permute-start(bf16[208,256]{1,0:T(8,128)(2,1)S(1)} %add_convert_fusion.4), channel_id=1, source_target_pairs={{0,4},{1,5},{2,6},{3,7},{4,0},{5,1},{6,2},{7,3},{8,12},{9,13},{10,... | collective-permute-start | bytes 319496 | tf_op jit(solution)/shard_map/ppermute | solution.py:460
  85.1 4.8 %collective-permute-start.6 = (bf16[208,256]{1,0:T(8,128)(2,1)S(1)}, bf16[208,256]{1,0:T(8,128)(2,1)S(1)}, u32[]{:S(2)}, u32[]{:S(2)}) collective-permute-start(bf16[208,256]{1,0:T(8,128)(2,1)S(1)} %add_convert_fusion.3), channel_id=1, source_target_pairs={{0,2},{1,3},{2,0},{3,1},{4,6},{5,7},{6,4},{7,5},{8,10},{9,11},{10,... | collective-permute-start | bytes 319496 | tf_op jit(solution)/shard_map/ppermute | solution.py:460
  89.9 8.1 %collective-permute-start.7 = (bf16[416,256]{1,0:T(8,128)(2,1)S(1)}, bf16[416,256]{1,0:T(8,128)(2,1)S(1)}, u32[]{:S(2)}, u32[]{:S(2)}) collective-permute-start(bf16[416,256]{1,0:T(8,128)(2,1)S(1)} %pad_maximum_fusion.2), channel_id=1, source_target_pairs={{0,1},{1,0},{2,3},{3,2},{4,5},{5,4},{6,7},{7,6},{8,24},{9,25},{10,... | collective-permute-start | bytes 638984 | tf_op jit(solution)/shard_map/ppermute | solution.py:460
  98.2 8.2 %collective-permute-start.8 = (bf16[832,256]{1,0:T(8,128)(2,1)S(1)}, bf16[832,256]{1,0:T(8,128)(2,1)S(1)}, u32[]{:S(2)}, u32[]{:S(2)}) collective-permute-start(bf16[832,256]{1,0:T(8,128)(2,1)S(1)} %pad_maximum_fusion.1), channel_id=1, source_target_pairs={{0,16},{1,17},{2,18},{3,19},{4,20},{5,21},{6,22},{7,23},{8,9},{9,8... | collective-permute-start | bytes 1277960 | tf_op jit(solution)/shard_map/ppermute | solution.py:460
  100.2 8.9 %copy-start = (bf16[256,256]{1,0:T(8,128)(2,1)S(1)}, bf16[256,256]{1,0:T(8,128)(2,1)}, u32[]{:S(2)}) copy-start(bf16[256,256]{1,0:T(8,128)(2,1)} %constant.36.clone.turned) | copy-start | bytes 393220
  100.2 8.9 %copy-start.1 = (s32[2]{0:T(128)S(1)}, s32[2]{0:T(128)}, u32[]{:S(2)}) copy-start(s32[2]{0:T(128)} %pad_add_fusion.place) | copy-start | bytes 28
  106.6 2.4 %collective-permute-start.9 = (bf16[1664,256]{1,0:T(8,128)(2,1)S(1)}, bf16[1664,256]{1,0:T(8,128)(2,1)S(1)}, u32[]{:S(2)}, u32[]{:S(2)}) collective-permute-start(bf16[1664,256]{1,0:T(8,128)(2,1)S(1)} %pad_maximum_fusion.own), channel_id=1, source_target_pairs={{0,8},{1,9},{2,10},{3,11},{4,12},{5,13},{6,14},{7,15},{8,0},{9,1},... | collective-permute-start | bytes 2555912 | tf_op jit(solution)/shard_map/ppermute | solution.py:460

commit v2 on v1

--- a/solution.py
+++ b/solution.py
@@ -18,8 +18,9 @@
 LANES = 128
 GROUP = LANES // HEAD_DIM
 EPSILON = 1e-05
-MASKED = -1000000000.0
+MASKED = -4000000000.0
 SCALING = 1.0 / math.sqrt(HEAD_DIM)
+SCALING_BITS = SCALING / math.log(2.0)
 GELU_A = 0.7978845608028654
 GELU_B = 0.044715 * GELU_A
 BF = jnp.bfloat16
@@ -34,6 +35,10 @@
 RELATIVE_AT = 3072
 VECTOR_AT = 3200
 BUFFER_ROWS = 3328
+PIPES = 2
+PART_ROWS = BUFFER_ROWS // (2 * PIPES)
+PAIR = 4
+PAIR_BACK = 8
 (V_CONTENT, V_POSITION, V_GAIN1, V_SHIFT1, V_GAIN2, V_SHIFT2, V_SHRINK, V_EXPAND) = range(8)
 VECTOR_ROWS = 16
 
@@ -115,12 +120,23 @@
 
 
 def layer_kernel(place, horizon, *refs):
-    sources, outputs, targets = refs[:COPIES], refs[COPIES : COPIES + 3], refs[COPIES + 3 : 2 * COPIES + 3]
-    sems, scratch = refs[2 * COPIES + 3], refs[2 * COPIES + 4 :]
+    sources, refs = refs[:COPIES], refs[COPIES:]
+    outputs, halves, refs = refs[:2], refs[2 : 2 + 2 * PIPES], refs[2 + 2 * PIPES :]
+    targets, (sems, half_sems, grads, *scratch) = refs[:COPIES], refs[COPIES:]
     moves = [pltpu.make_async_copy(a, b, sems.at[i]) for i, (a, b) in enumerate(zip(sources, targets))]
     for i in FIRST_COPIES + LATER_COPIES:
         moves[i].start()
-    compute_layer(place, horizon, moves, *targets, *outputs, *scratch)
+    compute_layer(place, horizon, moves, *targets, *outputs, grads, *scratch)
+    core = place[1]
+    leaving = []
+    for p in range(PIPES):
+        for k, half in enumerate((core, 1 - core)):
+            at = pl.ds(pl.multiple_of((half * PIPES + p) * PART_ROWS, PART_ROWS), PART_ROWS)
+            leaving.append(pltpu.make_async_copy(grads.at[at], halves[2 * p + k], half_sems.at[2 * p + k]))
+    for move in leaving:
+        move.start()
+    for move in leaving:
+        move.wait()
 
 
 def compute_layer(
@@ -135,11 +151,11 @@
     position = place[0]
     vec[...] = jnp.zeros_like(vec)
 
-    def loop(count, step):
+    def loop(count, step, unroll=1):
         def body(i, carry):
             step(i)
             return carry
-        lax.fori_loop(0, count, body, 0)
+        lax.fori_loop(0, count, body, 0, unroll=unroll)
 
     for i in FIRST_COPIES:
         moves[i].wait()
@@ -150,7 +166,9 @@
 
     def project(normed, at, count):
         keys[pl.ds(at, count)] = dot(normed, wk[...]).astype(BF)
-        values[pl.ds(at, count)] = dot(normed, wv[...]).astype(BF)
+        value = dot(normed, wv[...]).astype(BF)
+        for g in range(HEADS // GROUP):
+            values[pl.ds(at, count), 2 * g * LANES : (2 * g + 1) * LANES] = value[:, g * LANES : (g + 1) * LANES]
 
     memory = jnp.where(position == 0, start[...].astype(F32), arrived[...].astype(F32))
     unit, scale = normalize(memory)
@@ -161,7 +179,9 @@
     project(normed, 0, SEG)
     tail = keys.shape[0] - rows - SEG
     keys[rows + SEG :] = jnp.zeros((tail, FEATURES), BF)
-    values[rows + SEG :] = jnp.zeros((tail, FEATURES), BF)
+    values[rows + SEG :] = jnp.zeros((tail, 2 * FEATURES), BF)
+    for g in range(HEADS // GROUP):
+        values[:, (2 * g + 1) * LANES : (2 * g + 2) * LANES] = jnp.ones((values.shape[0], LANES), BF)
 
     block = 4 * SEG
 
@@ -190,32 +210,55 @@
     low_row = 7 - (query_at & 7)
     row_bits = [(step, (low_row & step) != 0) for step in (1, 2, 4)]
 
-    def attend(s):
-        r = pl.multiple_of(s * SEG, SEG)
-        number = position * segments + s
-        current = horizon[0, number]
-        previous = jnp.where(number == 0, SEG // STEP, horizon[0, jnp.maximum(number - 1, 0)])
-        live = key_at < jnp.where(key_at < SEG, STEP * previous, SEG + STEP * current)
-        allowed = (key_at <= query_at) & (live | (key_at == query_at))
-        for g in range(HEADS // GROUP):
-            lanes = slice(g * LANES, (g + 1) * LANES)
-            direct = dot_t(stack_heads(content[pl.ds(r, SEG), lanes], head_masks), keys[pl.ds(r, LANES), lanes])
-            lows = []
+    def attend(i):
+        units = []
+        for k in range(PAIR):
+            s = i * PAIR + k
+            r = pl.multiple_of(s * SEG, SEG)
+            number = position * segments + s
+            current = horizon[0, number]
+            previous = jnp.where(number == 0, SEG // STEP, horizon[0, jnp.maximum(number - 1, 0)])
+            live = key_at < jnp.where(key_at < SEG, STEP * previous, SEG + STEP * current)
+            allowed = (key_at <= query_at) & (live | (key_at == query_at))
+            units += [(s, r, allowed, g, slice(g * LANES, (g + 1) * LANES)) for g in range(HEADS // GROUP)]
+        direct = [
+            dot_t(stack_heads(content[pl.ds(r, SEG), lanes], head_masks), keys[pl.ds(r, LANES), lanes])
+            for s, r, allowed, g, lanes in units
+        ]
+        scores = [
+            [
+                jnp.where(
+                    allowed,
+                    d[h * SEG : (h + 1) * SEG]
+                    + pltpu.roll(
+                        raw[pl.ds(r, SEG), (g * GROUP + h) * LANES : (g * GROUP + h + 1) * LANES],
+                        LANES - SEG + 1, 1, stride=1, stride_axis=0,
+                    ),
+                    MASKED,
+                )
+                for h in range(GROUP)
+            ]
+            for d, (s, r, allowed, g, lanes) in zip(direct, units)
+        ]
+        tops = [[jnp.max(v, axis=-1, keepdims=True) for v in vs] for vs in scores]
+        lows = [
+            jnp.concatenate([jnp.exp2((v - t) * SCALING_BITS).astype(BF) for v, t in zip(vs, ts)], axis=0)
+            for vs, ts in zip(scores, tops)
+        ]
+        boths = [
+            dot(low, values[pl.ds(r, LANES), 2 * g * LANES : (2 * g + 2) * LANES])
+            for low, (s, r, allowed, g, lanes) in zip(lows, units)
+        ]
+        for low, both, (s, r, allowed, g, lanes) in zip(lows, boths, units):
+            inverse = 1.0 / both[:, LANES:]
+            mx = pick_heads(both[:, :LANES] * inverse, lane_head)
+            mixed[pl.ds(r, SEG), lanes] = mx.astype(BF)
+            bcont[pl.ds(r, SEG), lanes] = mx
             for h in range(GROUP):
-                head = g * GROUP + h
-                shifted = pltpu.roll(
-                    raw[pl.ds(r, SEG), head * LANES : (head + 1) * LANES],
-                    LANES - SEG + 1, 1, stride=1, stride_axis=0,
-                )
-                scores = jnp.where(allowed, (direct[h * SEG : (h + 1) * SEG] + shifted) * SCALING, MASKED)
-                exponent = jnp.exp(scores - jnp.max(scores, axis=-1, keepdims=True))
-                prob = exponent / jnp.sum(exponent, axis=-1, keepdims=True)
-                probs[pl.ds(pl.multiple_of((s * HEADS + head) * SEG, SEG), SEG)] = prob
-                lows.append(prob.astype(BF))
-            both = dot(jnp.concatenate(lows, axis=0), values[pl.ds(r, LANES), lanes])
-            mixed[pl.ds(r, SEG), lanes] = pick_heads(both, lane_head).astype(BF)
-
-    loop(segments, attend)
+                at = pl.ds(pl.multiple_of((s * HEADS + g * GROUP + h) * SEG, SEG), SEG)
+                probs[at] = low[h * SEG : (h + 1) * SEG].astype(F32) * inverse[h * SEG : (h + 1) * SEG]
+
+    loop(segments // PAIR, attend)
 
     for i in LATER_COPIES:
         moves[i].wait()
@@ -261,25 +304,38 @@
         grads[SHRINK_AT + f * FEATURES : SHRINK_AT + (f + 1) * FEATURES] = t_dot(act[:, cols], cot[...]).astype(BF)
     grads[OUTPUT_AT : OUTPUT_AT + FEATURES] = t_dot(mixed[...], bhl[...]).astype(BF)
 
-    def attend_back(s):
-        r = pl.multiple_of(s * SEG, SEG)
-        at = pl.ds(r, SEG)
-        for g in range(HEADS // GROUP):
-            lanes = slice(g * LANES, (g + 1) * LANES)
-            window = pl.ds(r, LANES)
-            back = stack_heads(bmix[at, lanes], head_masks)
-            wide = dot_t(back, values[window, lanes])
-            lows, grad_lows = [], []
+    def attend_back(i):
+        units = []
+        for k in range(PAIR_BACK):
+            s = i * PAIR_BACK + k
+            r = pl.multiple_of(s * SEG, SEG)
+            units += [
+                (s, pl.ds(r, SEG), pl.ds(r, LANES), g, slice(g * LANES, (g + 1) * LANES)) for g in range(HEADS // GROUP)
+            ]
+        backs, wides = [], []
+        for s, at, window, g, lanes in units:
+            rows = bmix[at, lanes]
+            back = stack_heads(rows, head_masks)
+            product = rows.astype(F32) * -bcont[at, lanes]
+            high = product.astype(BF)
+            rest = (product - high.astype(F32)).astype(BF)
+            along = jnp.concatenate([back, stack_heads(high, head_masks)], axis=1)
+            wide = dot_t(along, values[window, 2 * g * LANES : (2 * g + 2) * LANES])
+            wide += dot_t(stack_heads(rest, head_masks), values[window, (2 * g + 1) * LANES : (2 * g + 2) * LANES])
+            backs.append(back)
+            wides.append(wide)
+        lows, grads_low = [], []
+        for wide, (s, at, window, g, lanes) in zip(wides, units):
+            prob = probs[pl.ds(pl.multiple_of((s * HEADS + g * GROUP) * SEG, SEG), GROUP * SEG)]
+            bs = prob * wide
+            lows.append(prob.astype(BF))
+            grads_low.append(bs.astype(BF))
             for h in range(GROUP):
                 head = g * GROUP + h
-                prob = probs[pl.ds(pl.multiple_of((s * HEADS + head) * SEG, SEG), SEG)]
-                bp = wide[h * SEG : (h + 1) * SEG]
-                bs = prob * (bp - jnp.sum(bp * prob, axis=-1, keepdims=True))
-                lows.append(prob.astype(BF))
-                grad_lows.append(bs.astype(BF))
-                braw[at, head * LANES : (head + 1) * LANES] = unshift(bs, row_bits).astype(BF)
-            low = jnp.concatenate(lows, axis=0)
-            grad_low = jnp.concatenate(grad_lows, axis=0)
+                braw[at, head * LANES : (head + 1) * LANES] = unshift(
+                    bs[h * SEG : (h + 1) * SEG], row_bits
+                ).astype(BF)
+        for low, grad_low, back, (s, at, window, g, lanes) in zip(lows, grads_low, backs, units):
             vg = t_dot(low, back).astype(BF)
             vgm[at, lanes] = vg[0:SEG]
             vgs[at, lanes] = vg[SEG : 2 * SEG]
@@ -288,7 +344,7 @@
             kgs[at, lanes] = kg[SEG : 2 * SEG]
             bcont[at, lanes] = pick_heads(dot(grad_low, keys[window, lanes]), lane_head) * SCALING
 
-    loop(segments, attend_back)
+    loop(segments // PAIR_BACK, attend_back)
 
     def last_rows(i):
         r = pl.multiple_of(i * block, block)
@@ -344,7 +400,7 @@
         pltpu.VMEM((rows, FEATURES), BF),
         pltpu.VMEM((rows, FEATURES), BF),
         pltpu.VMEM((padded, FEATURES), BF),
-        pltpu.VMEM((padded, FEATURES), BF),
+        pltpu.VMEM((padded, 2 * FEATURES), BF),
         pltpu.VMEM((HEADS * LANES, FEATURES), BF),
         pltpu.VMEM((rows, HEADS * LANES), F32),
         pltpu.VMEM((rows * HEADS, LANES), F32),
@@ -369,36 +425,30 @@
         out_shape=(
             jax.ShapeDtypeStruct((rows, FEATURES), BF),
             jax.ShapeDtypeStruct((rows, FEATURES), BF),
-            jax.ShapeDtypeStruct((BUFFER_ROWS, FEATURES), BF),
-        ),
+        )
+        + (jax.ShapeDtypeStruct((PART_ROWS, FEATURES), BF),) * (2 * PIPES),
         in_specs=[smem, smem] + [hbm] * COPIES,
-        out_specs=(vmem, vmem, vmem),
+        out_specs=(vmem, vmem) + (hbm,) * (2 * PIPES),
         scratch_shapes=[pltpu.VMEM(a.shape, a.dtype) for a in operands]
-        + [pltpu.SemaphoreType.DMA((COPIES,))]
+        + [
+            pltpu.SemaphoreType.DMA((COPIES,)),
+            pltpu.SemaphoreType.DMA((2 * PIPES,)),
+            pltpu.VMEM((BUFFER_ROWS, FEATURES), BF),
+        ]
         + scratch,
         compiler_params=pltpu.CompilerParams(vmem_limit_bytes=63 * 1024 * 1024),
         name="layer",
     )(place, horizon, *operands)
 
 
-def unpack_kernel(
-    place, own, other, turned,
-    gain1, shift1, wq, wk, wv, wr, cbias, pbias, wo, gain2, shift2, w1, b1, w2, b2,
-    whole,
-):
-    first = place[1] == 0
-    half = BUFFER_ROWS // 2
-
-    @pl.when(first)
-    def _():
-        whole[0:half] = own[...]
-        whole[half:] = other[...]
-
-    @pl.when(jnp.logical_not(first))
-    def _():
-        whole[0:half] = other[...]
-        whole[half:] = own[...]
-
+def unpack_kernel(place, *refs):
+    parts, turned = refs[: 2 * PIPES], refs[2 * PIPES]
+    gain1, shift1, wq, wk, wv, wr, cbias, pbias, wo, gain2, shift2, w1, b1, w2, b2, whole = refs[2 * PIPES + 1 :]
+    core = place[1]
+    for p in range(PIPES):
+        for k, half in enumerate((core, 1 - core)):
+            at = pl.ds(pl.multiple_of((half * PIPES + p) * PART_ROWS, PART_ROWS), PART_ROWS)
+            whole[at] = parts[2 * p + k][...]
     for f in range(HIDDEN // FEATURES):
         w1[:, f * FEATURES : (f + 1) * FEATURES] = whole[
             EXPAND_AT + f * FEATURES : EXPAND_AT + (f + 1) * FEATURES
@@ -418,7 +468,7 @@
         b1[f * FEATURES : (f + 1) * FEATURES] = vectors[V_EXPAND + f]
 
 
-def unpack(place, own, other, turned):
+def unpack(place, parts, turned):
     vmem = pl.BlockSpec(memory_space=pltpu.VMEM)
     smem = pl.BlockSpec(memory_space=pltpu.SMEM)
     vector = jax.ShapeDtypeStruct((FEATURES,), F32)
@@ -433,12 +483,12 @@
     return pl.pallas_call(
         unpack_kernel,
         out_shape=shapes,
-        in_specs=[smem, vmem, vmem, vmem],
+        in_specs=[smem] + [vmem] * (2 * PIPES + 1),
         out_specs=(vmem,) * len(shapes),
         scratch_shapes=[pltpu.VMEM((BUFFER_ROWS, FEATURES), BF)],
         compiler_params=pltpu.CompilerParams(vmem_limit_bytes=32 * 1024 * 1024),
         name="unpack",
-    )(place, own, other, turned)
+    )(place, *parts, turned)
 
 
 AXES = ("tm", "roll")
@@ -464,27 +514,32 @@
     return (a.astype(F32) + b.astype(F32)).astype(BF)
 
 
-def sum_everywhere(buffer, core):
+def sum_everywhere(halves, core):
     roll_count, tm_count = lax.axis_size("roll"), lax.axis_size("tm")
     count = roll_count * tm_count
     me = lax.axis_index("tm") * roll_count + lax.axis_index("roll")
-    stages = exchange_plan(roll_count, tm_count)
-    halving = 4
-    bits = []
-    for even, odd in stages[:halving]:
-        bit = jnp.where(core == 0, (me >> even) & 1, (me >> odd) & 1)
-        half = buffer.shape[0] // 2
-        sent = lax.dynamic_slice_in_dim(buffer, (1 - bit) * half, half, 0)
-        kept = lax.dynamic_slice_in_dim(buffer, bit * half, half, 0)
-        buffer = add_low(kept, swap(sent, (even, odd), roll_count, count))
-        bits.append(bit)
-    for even, odd in stages[halving:]:
-        buffer = add_low(buffer, swap(buffer, (even, odd), roll_count, count))
-    for (even, odd), bit in list(zip(stages, bits))[:0:-1]:
-        other = swap(buffer, (even, odd), roll_count, count)
-        first = bit == 0
-        buffer = jnp.concatenate([jnp.where(first, buffer, other), jnp.where(first, other, buffer)], axis=0)
-    return buffer, swap(buffer, stages[0], roll_count, count)
+    cores, *stages = exchange_plan(roll_count, tm_count)
+    halving = 2
+
+    def chain(kept, sent):
+        buffer = add_low(kept, swap(sent, cores, roll_count, count))
+        bits = []
+        for even, odd in stages[:halving]:
+            bit = jnp.where(core == 0, (me >> even) & 1, (me >> odd) & 1)
+            half = buffer.shape[0] // 2
+            sent = lax.dynamic_slice_in_dim(buffer, (1 - bit) * half, half, 0)
+            kept = lax.dynamic_slice_in_dim(buffer, bit * half, half, 0)
+            buffer = add_low(kept, swap(sent, (even, odd), roll_count, count))
+            bits.append(bit)
+        for even, odd in stages[halving:]:
+            buffer = add_low(buffer, swap(buffer, (even, odd), roll_count, count))
+        for (even, odd), bit in list(zip(stages, bits))[::-1]:
+            other = swap(buffer, (even, odd), roll_count, count)
+            first = bit == 0
+            buffer = jnp.concatenate([jnp.where(first, buffer, other), jnp.where(first, other, buffer)], axis=0)
+        return [buffer, swap(buffer, cores, roll_count, count)]
+
+    return sum([chain(*halves[2 * p : 2 * p + 2]) for p in range(PIPES)], [])
 
 
 def body(
@@ -496,7 +551,7 @@
     x = layer_input.reshape(rollouts * columns, features)
     position = lax.axis_index("tm")
     tm_count = lax.axis_size("tm")
-    arrived = lax.ppermute(x[-SEG:], "tm", [(i, i + 1) for i in range(tm_count - 1)])
+    arrived = lax.ppermute(x[-SEG:], "tm", [(i, (i + 1) % tm_count) for i in range(tm_count)])
     core = position & 1
     place = jnp.stack([position, core]).astype(jnp.int32)
     table = jnp.asarray(position_rows())
@@ -510,12 +565,11 @@
         value_projection_weight, relative_weight, row(content_bias), row(position_bias), output_weight,
         row(second_gain), row(second_shift), expand_weight, row(expand_bias), shrink_weight, row(shrink_bias),
     )
-    out, dx, grads = run_layer(
+    out, dx, *halves = run_layer(
         place, horizon, x, start_memory.reshape(SEG, features), arrived,
         cotangent.reshape(rollouts * columns, features), table, basis, params,
     )
-    own, other = sum_everywhere(grads, core)
-    summed = unpack(place, own, other, turned)
+    summed = unpack(place, sum_everywhere(halves, core), turned)
     return (out.reshape(layer_input.shape), dx.reshape(layer_input.shape)) + tuple(summed)
 
 

time: 112 us -> 83.1 us (0.74)
  waiting for transfers between devices: 39.3 us -> 21.5 us
  Pallas kernels: 49.5 us -> 32.6 us
  starting transfers between devices: 17.9 us -> 24.1 us
  local copies, waits for them, and re-layouts: 2.78 us -> 1.45 us
    ppermute x9 -> x16, waiting for transfers between devices: 39.1 us -> 18.7 us  [swap(): return lax.ppermute(value, AXES, pairs)]
    pallas_call x1, Pallas kernels: 46.9 us -> 30.1 us  [run_layer(): pl.pallas_call(layer_kernel, out_shape=(jax.ShapeDtypeStruct((rows, FEATU...]
    ppermute x9 -> x16, starting transfers between devices: 15.6 us -> 23.6 us  [swap(): return lax.ppermute(value, AXES, pairs)]
    ppermute x1, waiting for transfers between devices: 0.24 us -> 2.88 us  [body(): lax.ppermute(x[-SEG:], 'tm', [(i, (i + 1) % tm_count) for i in range(tm_c...]
    ppermute x1, starting transfers between devices: 2.35 us -> 0.45 us  [body(): lax.ppermute(x[-SEG:], 'tm', [(i, (i + 1) % tm_count) for i in range(tm_c...]
    dynamic_slice x4, local copies, waits for them, and re-layouts: 1.42 us -> 0.08 us  [chain(): sent = lax.dynamic_slice_in_dim(buffer, (1 - bit) * half, half, 0)]
  transfers between devices with their start and end apart: 10 -> 17, of which waited for: 10 -> 14; matrix products, arithmetic and copies ran while one was open for 1% -> 3% of each run, Pallas kernels for 0% -> 0%
where the time goes in v2:
time: 83.1 us; the launch traced here: 82.9 us
  Pallas kernels  32.6 us (39%)
  starting transfers between devices  24.1 us (29%)
  waiting for transfers between devices  21.5 us (26%)
  other arithmetic  2.38 us (3%)
  local copies, waits for them, and re-layouts  1.45 us (2%)
  between operations  0.84 us (1%)
    pallas_call x1, Pallas kernels, run_layer(): pl.pallas_call(layer_kernel, out_shape=(jax.ShapeDtypeStruct((rows, FEATU...  30.1 us
    ppermute x16, starting transfers between devices, swap(): return lax.ppermute(value, AXES, pairs)  23.6 us
    ppermute x16, waiting for transfers between devices, swap(): return lax.ppermute(value, AXES, pairs)  18.7 us
    ppermute x1, waiting for transfers between devices, body(): lax.ppermute(x[-SEG:], 'tm', [(i, (i + 1) % tm_count) for i in range(tm_c...  2.88 us
    pallas_call x1, Pallas kernels, unpack(): pl.pallas_call(unpack_kernel, out_shape=shapes, in_specs=[smem] + [vmem]...  2.55 us
  transfers between devices with their start and end apart: 17, of which 14 were waited for; matrix products, arithmetic and copies ran while one was open for 3% of the time, Pallas kernels for 0%

profile of v2, /device:TPU:0, one launch (start us, length us, event | category | flops | bytes accessed | tf_op | source)
XLA Modules:
  0.0 82.9 jit_solution(7730726970617385922)
XLA Ops:
  0.7 0.7 slice_bitcast_fusion
  1.4 0.5 collective-permute-start
  1.9 0.6 pad_add_fusion.place
  2.4 2.9 %collective-permute-done.refs_2_ = bf16[48,256]{1,0:T(8,128)(2,1)S(1)} collective-permute-done((bf16[48,256]{1,0:T(8,128)(2,1)S(1)}, bf16[48,256]{1,0:T(8,128)(2,1)S(1)}, u32[]{:S(2)}, u32[]{:S(2)}) %collective-permute-start) | collective-permute-done | bytes 24608 | tf_op jit(solution)/shard_map/ppermute | solution.py:554
  5.3 0.0 copy-start.3
  5.3 0.6 copy-done.3
  5.9 30.1 %layer.1 = (bf16[768,256]{1,0:T(8,128)(2,1)}, bf16[768,256]{1,0:T(8,128)(2,1)}, bf16[832,256]{1,0:T(8,128)(2,1)}, bf16[832,256]{1,0:T(8,128)(2,1)}, bf16[832,256]{1,0:T(8,128)(2,1)}, /*index=5*/bf16[832,256]{1,0:T(8,128)(2,1)}) custom-call(s32[2]{0:T(128)} %pad_add_fusion.place, s32[1,64]{1,0:T(1,128)} %horizon.1, bf16[768,256]{1,0:T(8,128)(2,1)} %bitcast.17, ...), custom_call_target="tpu_custom_call" | custom-call | tf_op jit(solution)/shard_map/layer/pallas_call | solution.py:423
  36.0 0.2 collective-permute-start.1
  36.2 0.4 collective-permute-start.9
  36.6 1.5 %collective-permute-done.1 = bf16[832,256]{1,0:T(8,128)(2,1)S(1)} collective-permute-done((bf16[832,256]{1,0:T(8,128)(2,1)}, bf16[832,256]{1,0:T(8,128)(2,1)S(1)}, u32[]{:S(2)}, u32[]{:S(2)}) %collective-permute-start.1) | collective-permute-done | bytes 426016 | tf_op jit(solution)/shard_map/ppermute | solution.py:510
  38.0 1.1 %add_convert_fusion.1 = bf16[832,256]{1,0:T(8,128)(2,1)S(1)} fusion(bf16[832,256]{1,0:T(8,128)(2,1)S(1)} %collective-permute-done.1, bf16[832,256]{1,0:T(8,128)(2,1)} %get-tuple-element.40), kind=kLoop, calls=%fused_computation.1 | loop fusion | flops 851968 | bytes 1277952 | tf_op jit(solution)/shard_map/convert_element_type | solution.py:514
  39.1 0.0 copy-start.2
  39.2 2.4 %collective-permute-start.2 = (bf16[416,256]{1,0:T(8,128)(2,1)S(1)}, bf16[416,256]{1,0:T(8,128)(2,1)S(1)}, u32[]{:S(2)}, u32[]{:S(2)}) collective-permute-start(bf16[416,256]{1,0:T(8,128)(2,1)S(1)} %constant_dynamic-slice_fusion.3), channel_id=1, source_target_pairs={{0,16},{1,17},{2,18},{3,19},{4,20},{5,21},{6,22},{7,23},{8,9},{9,8... | collective-permute-start | bytes 638984 | tf_op jit(solution)/shard_map/ppermute | solution.py:510
  41.6 0.0 collective-permute-done.9
  41.6 0.0 copy-done.2
  41.6 0.1 add_convert_fusion
  41.7 1.0 %collective-permute-start.10 = (bf16[416,256]{1,0:T(8,128)(2,1)S(1)}, bf16[416,256]{1,0:T(8,128)(2,1)S(1)}, u32[]{:S(2)}, u32[]{:S(2)}) collective-permute-start(bf16[416,256]{1,0:T(8,128)(2,1)S(1)} %constant_dynamic-slice_fusion.1), channel_id=1, source_target_pairs={{0,16},{1,17},{2,18},{3,19},{4,20},{5,21},{6,22},{7,23},{8,9},{9,8... | collective-permute-start | bytes 638984 | tf_op jit(solution)/shard_map/ppermute | solution.py:510
  42.7 2.7 %collective-permute-done.2 = bf16[416,256]{1,0:T(8,128)(2,1)S(1)} collective-permute-done((bf16[416,256]{1,0:T(8,128)(2,1)S(1)}, bf16[416,256]{1,0:T(8,128)(2,1)S(1)}, u32[]{:S(2)}, u32[]{:S(2)}) %collective-permute-start.2) | collective-permute-done | bytes 213024 | tf_op jit(solution)/shard_map/ppermute | solution.py:510
  45.4 0.1 add_convert_fusion.3
  45.5 2.1 %collective-permute-start.3 = (bf16[208,256]{1,0:T(8,128)(2,1)S(1)}, bf16[208,256]{1,0:T(8,128)(2,1)S(1)}, u32[]{:S(2)}, u32[]{:S(2)}) collective-permute-start(bf16[208,256]{1,0:T(8,128)(2,1)S(1)} %constant_dynamic-slice_fusion.2), channel_id=1, source_target_pairs={{0,1},{1,0},{2,3},{3,2},{4,5},{5,4},{6,7},{7,6},{8,24},{9,25},{10,... | collective-permute-start | bytes 319496 | tf_op jit(solution)/shard_map/ppermute | solution.py:510
  47.5 0.1 collective-permute-done.10
  47.7 0.1 add_convert_fusion.2
  47.7 2.2 %collective-permute-start.11 = (bf16[208,256]{1,0:T(8,128)(2,1)S(1)}, bf16[208,256]{1,0:T(8,128)(2,1)S(1)}, u32[]{:S(2)}, u32[]{:S(2)}) collective-permute-start(bf16[208,256]{1,0:T(8,128)(2,1)S(1)} %constant_dynamic-slice_fusion), channel_id=1, source_target_pairs={{0,1},{1,0},{2,3},{3,2},{4,5},{5,4},{6,7},{7,6},{8,24},{9,25},{10,... | collective-permute-start | bytes 319496 | tf_op jit(solution)/shard_map/ppermute | solution.py:510
  50.0 0.2 collective-permute-done.3
  50.3 2.1 %collective-permute-start.4 = (bf16[208,256]{1,0:T(8,128)(2,1)S(1)}, bf16[208,256]{1,0:T(8,128)(2,1)S(1)}, u32[]{:S(2)}, u32[]{:S(2)}) collective-permute-start(bf16[208,256]{1,0:T(8,128)(2,1)S(1)} %add_convert_fusion.9), channel_id=1, source_target_pairs={{0,2},{1,3},{2,0},{3,1},{4,6},{5,7},{6,4},{7,5},{8,10},{9,11},{10,... | collective-permute-start | bytes 319496 | tf_op jit(solution)/shard_map/ppermute | solution.py:510
  52.4 0.3 collective-permute-done.11
  52.7 2.2 %collective-permute-start.12 = (bf16[208,256]{1,0:T(8,128)(2,1)S(1)}, bf16[208,256]{1,0:T(8,128)(2,1)S(1)}, u32[]{:S(2)}, u32[]{:S(2)}) collective-permute-start(bf16[208,256]{1,0:T(8,128)(2,1)S(1)} %add_convert_fusion.6), channel_id=1, source_target_pairs={{0,2},{1,3},{2,0},{3,1},{4,6},{5,7},{6,4},{7,5},{8,10},{9,11},{10,... | collective-permute-start | bytes 319496 | tf_op jit(solution)/shard_map/ppermute | solution.py:510
  54.9 1.1 %collective-permute-done.4 = bf16[208,256]{1,0:T(8,128)(2,1)S(1)} collective-permute-done((bf16[208,256]{1,0:T(8,128)(2,1)S(1)}, bf16[208,256]{1,0:T(8,128)(2,1)S(1)}, u32[]{:S(2)}, u32[]{:S(2)}) %collective-permute-start.4) | collective-permute-done | bytes 106528 | tf_op jit(solution)/shard_map/ppermute | solution.py:510
  56.0 3.3 %collective-permute-start.5 = (bf16[208,256]{1,0:T(8,128)(2,1)S(1)}, bf16[208,256]{1,0:T(8,128)(2,1)S(1)}, u32[]{:S(2)}, u32[]{:S(2)}) collective-permute-start(bf16[208,256]{1,0:T(8,128)(2,1)S(1)} %add_convert_fusion.8), channel_id=1, source_target_pairs={{0,4},{1,5},{2,6},{3,7},{4,0},{5,1},{6,2},{7,3},{8,12},{9,13},{10,... | collective-permute-start | bytes 319496 | tf_op jit(solution)/shard_map/ppermute | solution.py:510
  59.3 0.0 collective-permute-done.12
  59.3 1.8 %collective-permute-start.13 = (bf16[208,256]{1,0:T(8,128)(2,1)S(1)}, bf16[208,256]{1,0:T(8,128)(2,1)S(1)}, u32[]{:S(2)}, u32[]{:S(2)}) collective-permute-start(bf16[208,256]{1,0:T(8,128)(2,1)S(1)} %add_convert_fusion.5), channel_id=1, source_target_pairs={{0,4},{1,5},{2,6},{3,7},{4,0},{5,1},{6,2},{7,3},{8,12},{9,13},{10,... | collective-permute-start | bytes 319496 | tf_op jit(solution)/shard_map/ppermute | solution.py:510
  61.1 3.0 %collective-permute-done.5 = bf16[208,256]{1,0:T(8,128)(2,1)S(1)} collective-permute-done((bf16[208,256]{1,0:T(8,128)(2,1)S(1)}, bf16[208,256]{1,0:T(8,128)(2,1)S(1)}, u32[]{:S(2)}, u32[]{:S(2)}) %collective-permute-start.5) | collective-permute-done | bytes 106528 | tf_op jit(solution)/shard_map/ppermute | solution.py:510
  64.1 1.6 %collective-permute-start.6 = (bf16[208,256]{1,0:T(8,128)(2,1)S(1)}, bf16[208,256]{1,0:T(8,128)(2,1)S(1)}, u32[]{:S(2)}, u32[]{:S(2)}) collective-permute-start(bf16[208,256]{1,0:T(8,128)(2,1)S(1)} %add_convert_fusion.7), channel_id=1, source_target_pairs={{0,1},{1,0},{2,3},{3,2},{4,5},{5,4},{6,7},{7,6},{8,24},{9,25},{10,... | collective-permute-start | bytes 319496 | tf_op jit(solution)/shard_map/ppermute | solution.py:510
  65.7 0.7 collective-permute-done.13
  66.4 1.6 %collective-permute-start.14 = (bf16[208,256]{1,0:T(8,128)(2,1)S(1)}, bf16[208,256]{1,0:T(8,128)(2,1)S(1)}, u32[]{:S(2)}, u32[]{:S(2)}) collective-permute-start(bf16[208,256]{1,0:T(8,128)(2,1)S(1)} %add_convert_fusion.4), channel_id=1, source_target_pairs={{0,1},{1,0},{2,3},{3,2},{4,5},{5,4},{6,7},{7,6},{8,24},{9,25},{10,... | collective-permute-start | bytes 319496 | tf_op jit(solution)/shard_map/ppermute | solution.py:510
  68.0 2.0 %collective-permute-done.6 = bf16[208,256]{1,0:T(8,128)(2,1)S(1)} collective-permute-done((bf16[208,256]{1,0:T(8,128)(2,1)S(1)}, bf16[208,256]{1,0:T(8,128)(2,1)S(1)}, u32[]{:S(2)}, u32[]{:S(2)}) %collective-permute-start.6) | collective-permute-done | bytes 106528 | tf_op jit(solution)/shard_map/ppermute | solution.py:510
  70.0 1.2 %collective-permute-start.7 = (bf16[416,256]{1,0:T(8,128)(2,1)S(1)}, bf16[416,256]{1,0:T(8,128)(2,1)S(1)}, u32[]{:S(2)}, u32[]{:S(2)}) collective-permute-start(bf16[416,256]{1,0:T(8,128)(2,1)S(1)} %pad_maximum_fusion.2), channel_id=1, source_target_pairs={{0,16},{1,17},{2,18},{3,19},{4,20},{5,21},{6,22},{7,23},{8,9},{9,8... | collective-permute-start | bytes 638984 | tf_op jit(solution)/shard_map/ppermute | solution.py:510
  71.3 1.1 %collective-permute-done.14 = bf16[208,256]{1,0:T(8,128)(2,1)S(1)} collective-permute-done((bf16[208,256]{1,0:T(8,128)(2,1)S(1)}, bf16[208,256]{1,0:T(8,128)(2,1)S(1)}, u32[]{:S(2)}, u32[]{:S(2)}) %collective-permute-start.14) | collective-permute-done | bytes 106528 | tf_op jit(solution)/shard_map/ppermute | solution.py:510
  72.4 1.5 %collective-permute-start.15 = (bf16[416,256]{1,0:T(8,128)(2,1)S(1)}, bf16[416,256]{1,0:T(8,128)(2,1)S(1)}, u32[]{:S(2)}, u32[]{:S(2)}) collective-permute-start(bf16[416,256]{1,0:T(8,128)(2,1)S(1)} %pad_maximum_fusion.3), channel_id=1, source_target_pairs={{0,16},{1,17},{2,18},{3,19},{4,20},{5,21},{6,22},{7,23},{8,9},{9,8... | collective-permute-start | bytes 638984 | tf_op jit(solution)/shard_map/ppermute | solution.py:510
  73.9 2.0 %collective-permute-done.7 = bf16[416,256]{1,0:T(8,128)(2,1)S(1)} collective-permute-done((bf16[416,256]{1,0:T(8,128)(2,1)S(1)}, bf16[416,256]{1,0:T(8,128)(2,1)S(1)}, u32[]{:S(2)}, u32[]{:S(2)}) %collective-permute-start.7) | collective-permute-done | bytes 213024 | tf_op jit(solution)/shard_map/ppermute | solution.py:510
  75.9 0.1 broadcast_select_fusion.3
  76.1 0.1 collective-permute-start.8
  76.1 2.2 %collective-permute-done.15 = bf16[416,256]{1,0:T(8,128)(2,1)S(1)} collective-permute-done((bf16[416,256]{1,0:T(8,128)(2,1)S(1)}, bf16[416,256]{1,0:T(8,128)(2,1)S(1)}, u32[]{:S(2)}, u32[]{:S(2)}) %collective-permute-start.15) | collective-permute-done | bytes 213024 | tf_op jit(solution)/shard_map/ppermute | solution.py:510
  78.3 0.1 broadcast_select_fusion.1
  78.4 0.0 copy-start
  78.4 0.0 copy-start.1
  78.5 0.1 collective-permute-start.16
  78.6 0.0 collective-permute-done.8.refs_1_
  78.6 1.7 %collective-permute-done.16.refs_3_ = bf16[832,256]{1,0:T(8,128)(2,1)S(1)} collective-permute-done((bf16[832,256]{1,0:T(8,128)(2,1)S(1)}, bf16[832,256]{1,0:T(8,128)(2,1)S(1)}, u32[]{:S(2)}, u32[]{:S(2)}) %collective-permute-start.16) | collective-permute-done | bytes 426016 | tf_op jit(solution)/shard_map/ppermute | solution.py:510
  80.3 0.0 copy-done
  80.3 0.0 copy-done.1
  80.3 2.5 %unpack.1 = (f32[256]{0:T(256)}, f32[256]{0:T(256)}, f32[256,256]{1,0:T(8,128)}, f32[256,256]{1,0:T(8,128)}, f32[256,256]{1,0:T(8,128)}, /*index=5*/f32[256,256]...) custom-call(s32[2]{0:T(128)S(1)} %copy-done.1, ...), custom_call_target="tpu_custom_call" | custom-call | tf_op jit(solution)/shard_map/unpack/pallas_call | solution.py:483
  (16 shorter events, 0.4 us)
Async XLA Ops:
  1.4 3.9 %collective-permute-start = (bf16[48,256]{1,0:T(8,128)(2,1)S(1)}, bf16[48,256]{1,0:T(8,128)(2,1)S(1)}, u32[]{:S(2)}, u32[]{:S(2)}) collective-permute-start(bf16[48,256]{1,0:T(8,128)(2,1)S(1)} %slice_bitcast_fusion), channel_id=1, source_target_pairs={{0,8},{8,16},{16,24},{24,0},{1,9},{9,17},{17,25},{25,1},{2,10},{10... | collective-permute-start | bytes 73736 | tf_op jit(solution)/shard_map/ppermute | solution.py:554
  5.3 0.6 copy-start.3
  36.0 2.0 %collective-permute-start.1 = (bf16[832,256]{1,0:T(8,128)(2,1)}, bf16[832,256]{1,0:T(8,128)(2,1)S(1)}, u32[]{:S(2)}, u32[]{:S(2)}) collective-permute-start(bf16[832,256]{1,0:T(8,128)(2,1)} %get-tuple-element.41), channel_id=1, source_target_pairs={{0,8},{1,9},{2,10},{3,11},{4,12},{5,13},{6,14},{7,15},{8,0},{9,1},... | collective-permute-start | bytes 1277960 | tf_op jit(solution)/shard_map/ppermute | solution.py:510
  36.2 5.4 %collective-permute-start.9 = (bf16[832,256]{1,0:T(8,128)(2,1)}, bf16[832,256]{1,0:T(8,128)(2,1)S(1)}, u32[]{:S(2)}, u32[]{:S(2)}) collective-permute-start(bf16[832,256]{1,0:T(8,128)(2,1)} %get-tuple-element.43), channel_id=1, source_target_pairs={{0,8},{1,9},{2,10},{3,11},{4,12},{5,13},{6,14},{7,15},{8,0},{9,1},... | collective-permute-start | bytes 1277960 | tf_op jit(solution)/shard_map/ppermute | solution.py:510
  39.1 2.4 %copy-start.2 = (bf16[832,256]{1,0:T(8,128)(2,1)S(1)}, bf16[832,256]{1,0:T(8,128)(2,1)}, u32[]{:S(2)}) copy-start(bf16[832,256]{1,0:T(8,128)(2,1)} %get-tuple-element.42) | copy-start | bytes 1277956
  39.2 6.2 %collective-permute-start.2 = (bf16[416,256]{1,0:T(8,128)(2,1)S(1)}, bf16[416,256]{1,0:T(8,128)(2,1)S(1)}, u32[]{:S(2)}, u32[]{:S(2)}) collective-permute-start(bf16[416,256]{1,0:T(8,128)(2,1)S(1)} %constant_dynamic-slice_fusion.3), channel_id=1, source_target_pairs={{0,16},{1,17},{2,18},{3,19},{4,20},{5,21},{6,22},{7,23},{8,9},{9,8... | collective-permute-start | bytes 638984 | tf_op jit(solution)/shard_map/ppermute | solution.py:510
  41.7 6.0 %collective-permute-start.10 = (bf16[416,256]{1,0:T(8,128)(2,1)S(1)}, bf16[416,256]{1,0:T(8,128)(2,1)S(1)}, u32[]{:S(2)}, u32[]{:S(2)}) collective-permute-start(bf16[416,256]{1,0:T(8,128)(2,1)S(1)} %constant_dynamic-slice_fusion.1), channel_id=1, source_target_pairs={{0,16},{1,17},{2,18},{3,19},{4,20},{5,21},{6,22},{7,23},{8,9},{9,8... | collective-permute-start | bytes 638984 | tf_op jit(solution)/shard_map/ppermute | solution.py:510
  45.5 4.8 %collective-permute-start.3 = (bf16[208,256]{1,0:T(8,128)(2,1)S(1)}, bf16[208,256]{1,0:T(8,128)(2,1)S(1)}, u32[]{:S(2)}, u32[]{:S(2)}) collective-permute-start(bf16[208,256]{1,0:T(8,128)(2,1)S(1)} %constant_dynamic-slice_fusion.2), channel_id=1, source_target_pairs={{0,1},{1,0},{2,3},{3,2},{4,5},{5,4},{6,7},{7,6},{8,24},{9,25},{10,... | collective-permute-start | bytes 319496 | tf_op jit(solution)/shard_map/ppermute | solution.py:510
  47.7 4.9 %collective-permute-start.11 = (bf16[208,256]{1,0:T(8,128)(2,1)S(1)}, bf16[208,256]{1,0:T(8,128)(2,1)S(1)}, u32[]{:S(2)}, u32[]{:S(2)}) collective-permute-start(bf16[208,256]{1,0:T(8,128)(2,1)S(1)} %constant_dynamic-slice_fusion), channel_id=1, source_target_pairs={{0,1},{1,0},{2,3},{3,2},{4,5},{5,4},{6,7},{7,6},{8,24},{9,25},{10,... | collective-permute-start | bytes 319496 | tf_op jit(solution)/shard_map/ppermute | solution.py:510
  50.3 5.7 %collective-permute-start.4 = (bf16[208,256]{1,0:T(8,128)(2,1)S(1)}, bf16[208,256]{1,0:T(8,128)(2,1)S(1)}, u32[]{:S(2)}, u32[]{:S(2)}) collective-permute-start(bf16[208,256]{1,0:T(8,128)(2,1)S(1)} %add_convert_fusion.9), channel_id=1, source_target_pairs={{0,2},{1,3},{2,0},{3,1},{4,6},{5,7},{6,4},{7,5},{8,10},{9,11},{10,... | collective-permute-start | bytes 319496 | tf_op jit(solution)/shard_map/ppermute | solution.py:510
  52.7 6.6 %collective-permute-start.12 = (bf16[208,256]{1,0:T(8,128)(2,1)S(1)}, bf16[208,256]{1,0:T(8,128)(2,1)S(1)}, u32[]{:S(2)}, u32[]{:S(2)}) collective-permute-start(bf16[208,256]{1,0:T(8,128)(2,1)S(1)} %add_convert_fusion.6), channel_id=1, source_target_pairs={{0,2},{1,3},{2,0},{3,1},{4,6},{5,7},{6,4},{7,5},{8,10},{9,11},{10,... | collective-permute-start | bytes 319496 | tf_op jit(solution)/shard_map/ppermute | solution.py:510
  56.0 8.1 %collective-permute-start.5 = (bf16[208,256]{1,0:T(8,128)(2,1)S(1)}, bf16[208,256]{1,0:T(8,128)(2,1)S(1)}, u32[]{:S(2)}, u32[]{:S(2)}) collective-permute-start(bf16[208,256]{1,0:T(8,128)(2,1)S(1)} %add_convert_fusion.8), channel_id=1, source_target_pairs={{0,4},{1,5},{2,6},{3,7},{4,0},{5,1},{6,2},{7,3},{8,12},{9,13},{10,... | collective-permute-start | bytes 319496 | tf_op jit(solution)/shard_map/ppermute | solution.py:510
  59.3 7.0 %collective-permute-start.13 = (bf16[208,256]{1,0:T(8,128)(2,1)S(1)}, bf16[208,256]{1,0:T(8,128)(2,1)S(1)}, u32[]{:S(2)}, u32[]{:S(2)}) collective-permute-start(bf16[208,256]{1,0:T(8,128)(2,1)S(1)} %add_convert_fusion.5), channel_id=1, source_target_pairs={{0,4},{1,5},{2,6},{3,7},{4,0},{5,1},{6,2},{7,3},{8,12},{9,13},{10,... | collective-permute-start | bytes 319496 | tf_op jit(solution)/shard_map/ppermute | solution.py:510
  64.1 5.9 %collective-permute-start.6 = (bf16[208,256]{1,0:T(8,128)(2,1)S(1)}, bf16[208,256]{1,0:T(8,128)(2,1)S(1)}, u32[]{:S(2)}, u32[]{:S(2)}) collective-permute-start(bf16[208,256]{1,0:T(8,128)(2,1)S(1)} %add_convert_fusion.7), channel_id=1, source_target_pairs={{0,1},{1,0},{2,3},{3,2},{4,5},{5,4},{6,7},{7,6},{8,24},{9,25},{10,... | collective-permute-start | bytes 319496 | tf_op jit(solution)/shard_map/ppermute | solution.py:510
  66.4 6.0 %collective-permute-start.14 = (bf16[208,256]{1,0:T(8,128)(2,1)S(1)}, bf16[208,256]{1,0:T(8,128)(2,1)S(1)}, u32[]{:S(2)}, u32[]{:S(2)}) collective-permute-start(bf16[208,256]{1,0:T(8,128)(2,1)S(1)} %add_convert_fusion.4), channel_id=1, source_target_pairs={{0,1},{1,0},{2,3},{3,2},{4,5},{5,4},{6,7},{7,6},{8,24},{9,25},{10,... | collective-permute-start | bytes 319496 | tf_op jit(solution)/shard_map/ppermute | solution.py:510
  70.0 5.9 %collective-permute-start.7 = (bf16[416,256]{1,0:T(8,128)(2,1)S(1)}, bf16[416,256]{1,0:T(8,128)(2,1)S(1)}, u32[]{:S(2)}, u32[]{:S(2)}) collective-permute-start(bf16[416,256]{1,0:T(8,128)(2,1)S(1)} %pad_maximum_fusion.2), channel_id=1, source_target_pairs={{0,16},{1,17},{2,18},{3,19},{4,20},{5,21},{6,22},{7,23},{8,9},{9,8... | collective-permute-start | bytes 638984 | tf_op jit(solution)/shard_map/ppermute | solution.py:510
  72.4 5.9 %collective-permute-start.15 = (bf16[416,256]{1,0:T(8,128)(2,1)S(1)}, bf16[416,256]{1,0:T(8,128)(2,1)S(1)}, u32[]{:S(2)}, u32[]{:S(2)}) collective-permute-start(bf16[416,256]{1,0:T(8,128)(2,1)S(1)} %pad_maximum_fusion.3), channel_id=1, source_target_pairs={{0,16},{1,17},{2,18},{3,19},{4,20},{5,21},{6,22},{7,23},{8,9},{9,8... | collective-permute-start | bytes 638984 | tf_op jit(solution)/shard_map/ppermute | solution.py:510
  76.1 2.5 %collective-permute-start.8 = (bf16[832,256]{1,0:T(8,128)(2,1)S(1)}, bf16[832,256]{1,0:T(8,128)(2,1)S(1)}, u32[]{:S(2)}, u32[]{:S(2)}) collective-permute-start(bf16[832,256]{1,0:T(8,128)(2,1)S(1)} %pad_maximum_fusion.refs_0_), channel_id=1, source_target_pairs={{0,8},{1,9},{2,10},{3,11},{4,12},{5,13},{6,14},{7,15},{8,0},{9,1},... | collective-permute-start | bytes 1277960 | tf_op jit(solution)/shard_map/ppermute | solution.py:510
  78.4 1.9 %copy-start = (bf16[256,256]{1,0:T(8,128)(2,1)S(1)}, bf16[256,256]{1,0:T(8,128)(2,1)}, u32[]{:S(2)}) copy-start(bf16[256,256]{1,0:T(8,128)(2,1)} %constant.30.clone.refs_4_) | copy-start | bytes 393220
  78.4 1.9 %copy-start.1 = (s32[2]{0:T(128)S(1)}, s32[2]{0:T(128)}, u32[]{:S(2)}) copy-start(s32[2]{0:T(128)} %pad_add_fusion.place) | copy-start | bytes 28
  78.5 1.8 %collective-permute-start.16 = (bf16[832,256]{1,0:T(8,128)(2,1)S(1)}, bf16[832,256]{1,0:T(8,128)(2,1)S(1)}, u32[]{:S(2)}, u32[]{:S(2)}) collective-permute-start(bf16[832,256]{1,0:T(8,128)(2,1)S(1)} %pad_maximum_fusion.1.refs_2_), channel_id=1, source_target_pairs={{0,8},{1,9},{2,10},{3,11},{4,12},{5,13},{6,14},{7,15},{8,0},{9,1},... | collective-permute-start | bytes 1277960 | tf_op jit(solution)/shard_map/ppermute | solution.py:510

commit v3 on v2

--- a/solution.py
+++ b/solution.py
@@ -1,5 +1,6 @@
 import functools
 import math
+import types
 
 import jax
 import jax.numpy as jnp
@@ -37,8 +38,6 @@
 BUFFER_ROWS = 3328
 PIPES = 2
 PART_ROWS = BUFFER_ROWS // (2 * PIPES)
-PAIR = 4
-PAIR_BACK = 8
 (V_CONTENT, V_POSITION, V_GAIN1, V_SHIFT1, V_GAIN2, V_SHIFT2, V_SHRINK, V_EXPAND) = range(8)
 VECTOR_ROWS = 16
 
@@ -67,6 +66,15 @@
 
 def tables():
     return jnp.asarray(position_rows()), jnp.asarray(relative_basis()[0])
+
+
+def interleave(*steps):
+    running = [[0, count, part] for count, part in steps]
+    while running:
+        slowest = min(running, key=lambda entry: entry[0] / entry[1])
+        slowest[0] += 1
+        if next(slowest[2], None) is None:
+            running.remove(slowest)
 
 
 def dot(a, b):
@@ -127,10 +135,10 @@
     for i in FIRST_COPIES + LATER_COPIES:
         moves[i].start()
     compute_layer(place, horizon, moves, *targets, *outputs, grads, *scratch)
-    core = place[1]
+    side = place[1]
     leaving = []
     for p in range(PIPES):
-        for k, half in enumerate((core, 1 - core)):
+        for k, half in enumerate((side, 1 - side)):
             at = pl.ds(pl.multiple_of((half * PIPES + p) * PART_ROWS, PART_ROWS), PART_ROWS)
             leaving.append(pltpu.make_async_copy(grads.at[at], halves[2 * p + k], half_sems.at[2 * p + k]))
     for move in leaving:
@@ -144,18 +152,12 @@
     gain2, shift2, w1, b1, w2, b2, table, basis,
     out, dx, grads,
     nl, xhat, rstd, content, placed, keys, values, relblock, raw, probs, mixed,
-    hid, n2, act, bpre, bmix, bhid, bhl, bcont, braw, kgm, kgs, vgm, vgs, vec,
+    hid, n2, act, bpre, bmix, bhid, bhl, bcont, bql, braw, kgm, kgs, vgm, vgs, vec,
 ):
     rows = x.shape[0]
     segments = rows // SEG
     position = place[0]
     vec[...] = jnp.zeros_like(vec)
-
-    def loop(count, step, unroll=1):
-        def body(i, carry):
-            step(i)
-            return carry
-        lax.fori_loop(0, count, body, 0, unroll=unroll)
 
     for i in FIRST_COPIES:
         moves[i].wait()
@@ -177,114 +179,130 @@
     normed = (unit * gain1[...] + shift1[...]).astype(BF)
     nl[0:SEG] = normed
     project(normed, 0, SEG)
-    tail = keys.shape[0] - rows - SEG
-    keys[rows + SEG :] = jnp.zeros((tail, FEATURES), BF)
-    values[rows + SEG :] = jnp.zeros((tail, 2 * FEATURES), BF)
+    block = 4 * SEG
+    for edge in range(block, rows + 1, block):
+        ahead = slice(edge + SEG, edge + LANES - SEG)
+        keys[ahead] = jnp.zeros((LANES - 2 * SEG, FEATURES), BF)
+        values[ahead] = jnp.zeros((LANES - 2 * SEG, 2 * FEATURES), BF)
     for g in range(HEADS // GROUP):
         values[:, (2 * g + 1) * LANES : (2 * g + 2) * LANES] = jnp.ones((values.shape[0], LANES), BF)
-
-    block = 4 * SEG
-
-    def first_rows(i):
-        r = pl.multiple_of(i * block, block)
-        unit, scale = normalize(x[pl.ds(r, block)].astype(F32))
-        to = pl.multiple_of(r + SEG, SEG)
-        xhat[pl.ds(to, block)] = unit
-        rstd[pl.ds(to, block)] = scale
-        normed = (unit * gain1[...] + shift1[...]).astype(BF)
-        nl[pl.ds(to, block)] = normed
-        project(normed, to, block)
-        query = dot(normed, wq[...])
-        content[pl.ds(r, block)] = (query + cbias[...]).astype(BF)
-        low = (query + pbias[...]).astype(BF)
-        placed[pl.ds(r, block)] = low
-        raw[pl.ds(r, block)] = dot_t(low, relblock[...])
-
-    loop(rows // block, first_rows)
-
+    blocks = rows // block
     lane_head = lax.broadcasted_iota(jnp.int32, (SEG, LANES), 1) // HEAD_DIM
     head_masks = [(lane_head == h).astype(F32).astype(BF) for h in range(GROUP)]
     key_at = lax.broadcasted_iota(jnp.int32, (SEG, LANES), 1)
     query_at = lax.broadcasted_iota(jnp.int32, (SEG, LANES), 0) + SEG
-
     low_row = 7 - (query_at & 7)
     row_bits = [(step, (low_row & step) != 0) for step in (1, 2, 4)]
+    upper = (key_at & (HEAD_DIM // 2)) != 0
+
+    def first(i):
+        at = pl.ds(i * block, block)
+        to = pl.ds(i * block + SEG, block)
+        unit, scale = normalize(x[at].astype(F32))
+        xhat[to] = unit
+        rstd[to] = scale
+        normed = (unit * gain1[...] + shift1[...]).astype(BF)
+        nl[to] = normed
+        yield 1
+        project(normed, i * block + SEG, block)
+        yield 1
+        query = dot(normed, wq[...])
+        content[at] = (query + cbias[...]).astype(BF)
+        low = (query + pbias[...]).astype(BF)
+        placed[at] = low
+        yield 1
+        for f in range(HEADS * LANES // FEATURES):
+            cols = slice(f * FEATURES, (f + 1) * FEATURES)
+            raw[at, cols] = dot_t(low, relblock[cols])
+            yield 1
+
+    def units_of(i):
+        units = []
+        for s in range(i * block // SEG, (i + 1) * block // SEG):
+            for g in range(HEADS // GROUP):
+                u = types.SimpleNamespace()
+                u.s, u.g, u.at, u.window = s, g, pl.ds(s * SEG, SEG), pl.ds(s * SEG, LANES)
+                u.lanes = slice(g * LANES, (g + 1) * LANES)
+                u.beside = slice(2 * g * LANES, (2 * g + 2) * LANES)
+                u.heads = pl.ds((s * HEADS + g * GROUP) * SEG, GROUP * SEG)
+                units.append(u)
+        return units
+
+    def allow(s):
+        number = position * segments + s
+        current = horizon[0, number]
+        previous = jnp.where(number == 0, SEG // STEP, horizon[0, jnp.maximum(number - 1, 0)])
+        live = key_at < jnp.where(key_at < SEG, STEP * previous, SEG + STEP * current)
+        return (key_at <= query_at) & (live | (key_at == query_at))
+
+    def score(u):
+        u.direct = dot_t(stack_heads(content[u.at, u.lanes], head_masks), keys[u.window, u.lanes])
+
+    def mask(u):
+        allowed = allow(u.s)
+        u.scores = []
+        for h in range(GROUP):
+            head = u.g * GROUP + h
+            shifted = pltpu.roll(
+                raw[u.at, head * LANES : (head + 1) * LANES], LANES - SEG + 1, 1, stride=1, stride_axis=0
+            )
+            u.scores.append(jnp.where(allowed, u.direct[h * SEG : (h + 1) * SEG] + shifted, MASKED))
+        u.tops = [jnp.max(v, axis=-1, keepdims=True) for v in u.scores]
+
+    def exponentiate(u):
+        u.low = jnp.concatenate(
+            [jnp.exp2((v - top) * SCALING_BITS).astype(BF) for v, top in zip(u.scores, u.tops)], axis=0
+        )
+
+    def mix(u):
+        u.both = dot(u.low, values[u.window, u.beside])
+
+    def finish(u):
+        inverse = 1.0 / u.both[:, LANES:]
+        mx = pick_heads(u.both[:, :LANES] * inverse, lane_head)
+        mixed[u.at, u.lanes] = mx.astype(BF)
+        bcont[u.at, u.lanes] = mx
+        probs[u.heads] = u.low.astype(F32) * inverse
+
+    def staged(i, stages):
+        units = units_of(i)
+        for t in range(len(units) + len(stages) - 1):
+            for k in reversed(range(len(stages))):
+                if 0 <= t - k < len(units):
+                    stages[k](units[t - k])
+                    yield 1
 
     def attend(i):
-        units = []
-        for k in range(PAIR):
-            s = i * PAIR + k
-            r = pl.multiple_of(s * SEG, SEG)
-            number = position * segments + s
-            current = horizon[0, number]
-            previous = jnp.where(number == 0, SEG // STEP, horizon[0, jnp.maximum(number - 1, 0)])
-            live = key_at < jnp.where(key_at < SEG, STEP * previous, SEG + STEP * current)
-            allowed = (key_at <= query_at) & (live | (key_at == query_at))
-            units += [(s, r, allowed, g, slice(g * LANES, (g + 1) * LANES)) for g in range(HEADS // GROUP)]
-        direct = [
-            dot_t(stack_heads(content[pl.ds(r, SEG), lanes], head_masks), keys[pl.ds(r, LANES), lanes])
-            for s, r, allowed, g, lanes in units
-        ]
-        scores = [
-            [
-                jnp.where(
-                    allowed,
-                    d[h * SEG : (h + 1) * SEG]
-                    + pltpu.roll(
-                        raw[pl.ds(r, SEG), (g * GROUP + h) * LANES : (g * GROUP + h + 1) * LANES],
-                        LANES - SEG + 1, 1, stride=1, stride_axis=0,
-                    ),
-                    MASKED,
-                )
-                for h in range(GROUP)
-            ]
-            for d, (s, r, allowed, g, lanes) in zip(direct, units)
-        ]
-        tops = [[jnp.max(v, axis=-1, keepdims=True) for v in vs] for vs in scores]
-        lows = [
-            jnp.concatenate([jnp.exp2((v - t) * SCALING_BITS).astype(BF) for v, t in zip(vs, ts)], axis=0)
-            for vs, ts in zip(scores, tops)
-        ]
-        boths = [
-            dot(low, values[pl.ds(r, LANES), 2 * g * LANES : (2 * g + 2) * LANES])
-            for low, (s, r, allowed, g, lanes) in zip(lows, units)
-        ]
-        for low, both, (s, r, allowed, g, lanes) in zip(lows, boths, units):
-            inverse = 1.0 / both[:, LANES:]
-            mx = pick_heads(both[:, :LANES] * inverse, lane_head)
-            mixed[pl.ds(r, SEG), lanes] = mx.astype(BF)
-            bcont[pl.ds(r, SEG), lanes] = mx
-            for h in range(GROUP):
-                at = pl.ds(pl.multiple_of((s * HEADS + g * GROUP + h) * SEG, SEG), SEG)
-                probs[at] = low[h * SEG : (h + 1) * SEG].astype(F32) * inverse[h * SEG : (h + 1) * SEG]
-
-    loop(segments // PAIR, attend)
-
-    for i in LATER_COPIES:
-        moves[i].wait()
+        return staged(i, (score, mask, exponentiate, mix, finish))
 
     def feed(i):
-        r = pl.multiple_of(i * block, block)
-        at = pl.ds(r, block)
+        at = pl.ds(i * block, block)
         hidden = x[at].astype(F32) + dot(mixed[at], wo[...])
+        yield 1
         unit, scale = normalize(hidden)
         low = (unit * gain2[...] + shift2[...]).astype(BF)
         n2[at] = low
+        yield 1
         back = cot[at]
         for f in range(HIDDEN // FEATURES):
             cols = slice(f * FEATURES, (f + 1) * FEATURES)
             v = dot(low, w1[:, cols]) + b1[:, cols]
+            grad = dot_t(back, w2[cols])
+            yield 1
             square = v * v
             half = 0.5 + 0.5 * jnp.tanh(v * (GELU_A + GELU_B * square))
             active = v * half
             act[at, cols] = active.astype(BF)
             slope = half + (2.0 * active) * (1.0 - half) * (GELU_A + (3.0 * GELU_B) * square)
-            grad = dot_t(back, w2[cols]) * slope
+            grad = grad * slope
             vec[V_EXPAND + f : V_EXPAND + f + 1] += column_sum(grad)
             bpre[at, cols] = grad.astype(BF)
+            yield 1
         out[at] = (hidden + dot(act[at], w2[...]) + b2[...]).astype(BF)
+        yield 1
+        bn = dot_t(bpre[at], w1[...])
+        yield 1
         back = back.astype(F32)
-        bn = dot_t(bpre[at], w1[...])
         vec[V_SHRINK : V_SHRINK + 1] += column_sum(back)
         vec[V_GAIN2 : V_GAIN2 + 1] += column_sum(bn * unit)
         vec[V_SHIFT2 : V_SHIFT2 + 1] += column_sum(bn)
@@ -294,94 +312,117 @@
         bhid[at] = bh
         bl = bh.astype(BF)
         bhl[at] = bl
+        yield 1
         bmix[at] = dot_t(bl, wo[...]).astype(BF)
-
-    loop(rows // block, feed)
-
-    for f in range(HIDDEN // FEATURES):
-        cols = slice(f * FEATURES, (f + 1) * FEATURES)
-        grads[EXPAND_AT + f * FEATURES : EXPAND_AT + (f + 1) * FEATURES] = t_dot(n2[...], bpre[:, cols]).astype(BF)
-        grads[SHRINK_AT + f * FEATURES : SHRINK_AT + (f + 1) * FEATURES] = t_dot(act[:, cols], cot[...]).astype(BF)
-    grads[OUTPUT_AT : OUTPUT_AT + FEATURES] = t_dot(mixed[...], bhl[...]).astype(BF)
+        yield 1
+
+    def feed_weights():
+        for f in range(HIDDEN // FEATURES):
+            cols = slice(f * FEATURES, (f + 1) * FEATURES)
+            grads[EXPAND_AT + f * FEATURES : EXPAND_AT + (f + 1) * FEATURES] = t_dot(n2[...], bpre[:, cols]).astype(BF)
+            yield 1
+            grads[SHRINK_AT + f * FEATURES : SHRINK_AT + (f + 1) * FEATURES] = t_dot(act[:, cols], cot[...]).astype(BF)
+            yield 1
+        grads[OUTPUT_AT : OUTPUT_AT + FEATURES] = t_dot(mixed[...], bhl[...]).astype(BF)
+        yield 1
+
+    def spread(u):
+        rows = bmix[u.at, u.lanes]
+        u.back = stack_heads(rows, head_masks)
+        product = rows.astype(F32) * -bcont[u.at, u.lanes]
+        left = product + pltpu.roll(product, LANES - HEAD_DIM // 2, 1)
+        right = product + pltpu.roll(product, HEAD_DIM // 2, 1)
+        along = jnp.where(upper, right, left - left.astype(BF).astype(F32)).astype(BF)
+        u.along = jnp.concatenate([u.back, stack_heads(along, head_masks)], axis=1)
+
+    def widen(u):
+        u.wide = dot_t(u.along, values[u.window, u.beside])
+
+    def differentiate(u):
+        prob = probs[u.heads]
+        bs = prob * u.wide
+        u.low, u.grad_low = prob.astype(BF), bs.astype(BF)
+        for h in range(GROUP):
+            head = u.g * GROUP + h
+            braw[u.at, head * LANES : (head + 1) * LANES] = unshift(bs[h * SEG : (h + 1) * SEG], row_bits).astype(BF)
+
+    def collect_values(u):
+        vg = t_dot(u.low, u.back).astype(BF)
+        vgm[u.at, u.lanes] = vg[0:SEG]
+        vgs[u.at, u.lanes] = vg[SEG : 2 * SEG]
+
+    def collect_keys(u):
+        kg = (t_dot(u.grad_low, stack_heads(content[u.at, u.lanes], head_masks)) * SCALING).astype(BF)
+        kgm[u.at, u.lanes] = kg[0:SEG]
+        kgs[u.at, u.lanes] = kg[SEG : 2 * SEG]
+
+    def collect_queries(u):
+        bcont[u.at, u.lanes] = pick_heads(dot(u.grad_low, keys[u.window, u.lanes]), lane_head) * SCALING
 
     def attend_back(i):
-        units = []
-        for k in range(PAIR_BACK):
-            s = i * PAIR_BACK + k
-            r = pl.multiple_of(s * SEG, SEG)
-            units += [
-                (s, pl.ds(r, SEG), pl.ds(r, LANES), g, slice(g * LANES, (g + 1) * LANES)) for g in range(HEADS // GROUP)
-            ]
-        backs, wides = [], []
-        for s, at, window, g, lanes in units:
-            rows = bmix[at, lanes]
-            back = stack_heads(rows, head_masks)
-            product = rows.astype(F32) * -bcont[at, lanes]
-            high = product.astype(BF)
-            rest = (product - high.astype(F32)).astype(BF)
-            along = jnp.concatenate([back, stack_heads(high, head_masks)], axis=1)
-            wide = dot_t(along, values[window, 2 * g * LANES : (2 * g + 2) * LANES])
-            wide += dot_t(stack_heads(rest, head_masks), values[window, (2 * g + 1) * LANES : (2 * g + 2) * LANES])
-            backs.append(back)
-            wides.append(wide)
-        lows, grads_low = [], []
-        for wide, (s, at, window, g, lanes) in zip(wides, units):
-            prob = probs[pl.ds(pl.multiple_of((s * HEADS + g * GROUP) * SEG, SEG), GROUP * SEG)]
-            bs = prob * wide
-            lows.append(prob.astype(BF))
-            grads_low.append(bs.astype(BF))
-            for h in range(GROUP):
-                head = g * GROUP + h
-                braw[at, head * LANES : (head + 1) * LANES] = unshift(
-                    bs[h * SEG : (h + 1) * SEG], row_bits
-                ).astype(BF)
-        for low, grad_low, back, (s, at, window, g, lanes) in zip(lows, grads_low, backs, units):
-            vg = t_dot(low, back).astype(BF)
-            vgm[at, lanes] = vg[0:SEG]
-            vgs[at, lanes] = vg[SEG : 2 * SEG]
-            kg = (t_dot(grad_low, stack_heads(content[at, lanes], head_masks)) * SCALING).astype(BF)
-            kgm[at, lanes] = kg[0:SEG]
-            kgs[at, lanes] = kg[SEG : 2 * SEG]
-            bcont[at, lanes] = pick_heads(dot(grad_low, keys[window, lanes]), lane_head) * SCALING
-
-    loop(segments // PAIR_BACK, attend_back)
-
-    def last_rows(i):
-        r = pl.multiple_of(i * block, block)
-        at = pl.ds(r, block)
-        to = pl.ds(pl.multiple_of(r + SEG, SEG), block)
+        return staged(i, (spread, widen, differentiate, collect_values, collect_keys, collect_queries))
+
+    def last(i):
+        at = pl.ds(i * block, block)
+        to = pl.ds(i * block + SEG, block)
         bplace = dot(braw[at], relblock[...]) * SCALING
+        yield 1
         bc = bcont[at]
         vec[V_CONTENT : V_CONTENT + 1] += column_sum(bc)
         vec[V_POSITION : V_POSITION + 1] += column_sum(bplace)
         bq = (bc + bplace).astype(BF)
-        bhl[at] = bq
+        bql[at] = bq
+        yield 1
         bn = dot_t(bq, wq[...]) + dot_t(kgs[at], wk[...]) + dot_t(vgs[at], wv[...])
+        yield 1
         bm = dot_t(kgm[at], wk[...]) + dot_t(vgm[at], wv[...])
+        yield 1
         unit = xhat[to]
         vec[V_GAIN1 : V_GAIN1 + 1] += column_sum(bn * unit) + column_sum(bm * xhat[at])
         vec[V_SHIFT1 : V_SHIFT1 + 1] += column_sum(bn) + column_sum(bm)
         u = bn * gain1[...]
         inner = u - jnp.mean(u, axis=-1, keepdims=True) - unit * jnp.mean(u * unit, axis=-1, keepdims=True)
         dx[at] = (bhid[at] + inner * rstd[to]).astype(BF)
-
-    loop(rows // block, last_rows)
-
-    segment_rows = nl[SEG : SEG + rows]
-    memory_rows = nl[0:rows]
-    grads[QUERY_AT : QUERY_AT + FEATURES] = t_dot(segment_rows, bhl[...]).astype(BF)
-    grads[KEY_AT : KEY_AT + FEATURES] = (t_dot(segment_rows, kgs[...]) + t_dot(memory_rows, kgm[...])).astype(BF)
-    grads[VALUE_AT : VALUE_AT + FEATURES] = (t_dot(segment_rows, vgs[...]) + t_dot(memory_rows, vgm[...])).astype(BF)
-    for g in range(HEADS // GROUP):
-        lanes = slice(g * LANES, (g + 1) * LANES)
-        across = t_dot(placed[:, lanes], braw[:, g * GROUP * LANES : (g + 1) * GROUP * LANES])
-        back = jnp.concatenate(
-            [across[h * HEAD_DIM : (h + 1) * HEAD_DIM, h * LANES : (h + 1) * LANES] for h in range(GROUP)], axis=0
-        ) * SCALING
-        high = back.astype(BF)
-        low = (back - high.astype(F32)).astype(BF)
-        cosines = dot_t(basis[0:LANES], high) + (dot_t(basis[LANES:], high) + dot_t(basis[0:LANES], low))
-        grads[RELATIVE_AT : RELATIVE_AT + LANES, lanes] = cosines.astype(BF)
+        yield 1
+
+    def attention_weights():
+        segment_rows = nl[SEG : SEG + rows]
+        memory_rows = nl[0:rows]
+        grads[QUERY_AT : QUERY_AT + FEATURES] = t_dot(segment_rows, bql[...]).astype(BF)
+        yield 1
+        grads[KEY_AT : KEY_AT + FEATURES] = (t_dot(segment_rows, kgs[...]) + t_dot(memory_rows, kgm[...])).astype(BF)
+        yield 1
+        grads[VALUE_AT : VALUE_AT + FEATURES] = (t_dot(segment_rows, vgs[...]) + t_dot(memory_rows, vgm[...])).astype(BF)
+        yield 1
+        for g in range(HEADS // GROUP):
+            lanes = slice(g * LANES, (g + 1) * LANES)
+            across = t_dot(placed[:, lanes], braw[:, g * GROUP * LANES : (g + 1) * GROUP * LANES])
+            back = jnp.concatenate(
+                [across[h * HEAD_DIM : (h + 1) * HEAD_DIM, h * LANES : (h + 1) * LANES] for h in range(GROUP)], axis=0
+            ) * SCALING
+            high = back.astype(BF)
+            low = (back - high.astype(F32)).astype(BF)
+            cosines = dot_t(basis[0:LANES], high) + (dot_t(basis[LANES:], high) + dot_t(basis[0:LANES], low))
+            grads[RELATIVE_AT : RELATIVE_AT + LANES, lanes] = cosines.astype(BF)
+            yield 1
+
+    phases = {
+        "first": (8, first), "attend": (40, attend), "feed": (14, feed), "back": (48, attend_back), "last": (5, last),
+    }
+    for t in range(blocks + 4):
+        if t == 2:
+            for i in LATER_COPIES:
+                moves[i].wait()
+        steps = []
+        for lag, (count, phase) in enumerate(phases.values()):
+            if 0 <= t - lag < blocks:
+                steps.append((count, phase(t - lag)))
+        if t == blocks + 2:
+            steps.append((9, feed_weights()))
+        if t == blocks + 3:
+            pass
+        interleave(*steps)
+    interleave((5, attention_weights()))
     grads[VECTOR_AT : VECTOR_AT + VECTOR_ROWS] = vec[...].astype(BF)
     grads[VECTOR_AT + VECTOR_ROWS :] = jnp.zeros((BUFFER_ROWS - VECTOR_AT - VECTOR_ROWS, FEATURES), BF)
 
@@ -413,6 +454,7 @@
         pltpu.VMEM((rows, FEATURES), F32),
         pltpu.VMEM((rows, FEATURES), BF),
         pltpu.VMEM((rows, FEATURES), F32),
+        pltpu.VMEM((rows, FEATURES), BF),
         pltpu.VMEM((rows, HEADS * LANES), BF),
         pltpu.VMEM((rows, FEATURES), BF),
         pltpu.VMEM((rows, FEATURES), BF),
@@ -444,9 +486,9 @@
 def unpack_kernel(place, *refs):
     parts, turned = refs[: 2 * PIPES], refs[2 * PIPES]
     gain1, shift1, wq, wk, wv, wr, cbias, pbias, wo, gain2, shift2, w1, b1, w2, b2, whole = refs[2 * PIPES + 1 :]
-    core = place[1]
+    side = place[1]
     for p in range(PIPES):
-        for k, half in enumerate((core, 1 - core)):
+        for k, half in enumerate((side, 1 - side)):
             at = pl.ds(pl.multiple_of((half * PIPES + p) * PART_ROWS, PART_ROWS), PART_ROWS)
             whole[at] = parts[2 * p + k][...]
     for f in range(HIDDEN // FEATURES):
@@ -501,43 +543,47 @@
     rolls = list(range(roll_bits))
     even = high + rolls
     odd = rolls[:1] + high + rolls[1:]
-    return [(roll_bits, roll_bits)] + list(zip(even, odd))
-
-
-def swap(value, bits, roll_count, count):
-    even, odd = bits
-    pairs = [(d, d ^ (1 << (odd if (d // roll_count) & 1 else even))) for d in range(count)]
-    return lax.ppermute(value, AXES, pairs)
+    return roll_bits, list(zip(even, odd))
+
+
+def side_of(device):
+    return bin(device).count("1") & 1
+
+
+def swap_cores(value, core, count):
+    return lax.ppermute(value, AXES, [(d, d ^ (1 << core)) for d in range(count)])
+
+
+def swap(value, bits, core, count):
+    return lax.ppermute(value, AXES, [(d, d ^ (1 << bits[side_of(d)]) ^ (1 << core)) for d in range(count)])
 
 
 def add_low(a, b):
     return (a.astype(F32) + b.astype(F32)).astype(BF)
 
 
-def sum_everywhere(halves, core):
+def sum_everywhere(halves, me, side):
     roll_count, tm_count = lax.axis_size("roll"), lax.axis_size("tm")
     count = roll_count * tm_count
-    me = lax.axis_index("tm") * roll_count + lax.axis_index("roll")
-    cores, *stages = exchange_plan(roll_count, tm_count)
-    halving = 2
+    core, stages = exchange_plan(roll_count, tm_count)
+    halving = 3
 
     def chain(kept, sent):
-        buffer = add_low(kept, swap(sent, cores, roll_count, count))
-        bits = []
-        for even, odd in stages[:halving]:
-            bit = jnp.where(core == 0, (me >> even) & 1, (me >> odd) & 1)
+        buffer = add_low(kept, swap_cores(sent, core, count))
+        firsts = []
+        for bits in stages[:halving]:
+            bit = jnp.where(side == 0, (me >> bits[0]) & 1, (me >> bits[1]) & 1)
             half = buffer.shape[0] // 2
             sent = lax.dynamic_slice_in_dim(buffer, (1 - bit) * half, half, 0)
             kept = lax.dynamic_slice_in_dim(buffer, bit * half, half, 0)
-            buffer = add_low(kept, swap(sent, (even, odd), roll_count, count))
-            bits.append(bit)
-        for even, odd in stages[halving:]:
-            buffer = add_low(buffer, swap(buffer, (even, odd), roll_count, count))
-        for (even, odd), bit in list(zip(stages, bits))[::-1]:
-            other = swap(buffer, (even, odd), roll_count, count)
-            first = bit == 0
+            buffer = add_low(kept, swap(sent, bits, core, count))
+            firsts.append(bit == 0)
+        for bits in stages[halving:]:
+            buffer = add_low(buffer, swap(buffer, bits, core, count))
+        for bits, first in list(zip(stages, firsts))[::-1]:
+            other = swap(buffer, bits, core, count)
             buffer = jnp.concatenate([jnp.where(first, buffer, other), jnp.where(first, other, buffer)], axis=0)
-        return [buffer, swap(buffer, cores, roll_count, count)]
+        return [buffer, swap_cores(buffer, core, count)]
 
     return sum([chain(*halves[2 * p : 2 * p + 2]) for p in range(PIPES)], [])
 
@@ -552,8 +598,12 @@
     position = lax.axis_index("tm")
     tm_count = lax.axis_size("tm")
     arrived = lax.ppermute(x[-SEG:], "tm", [(i, (i + 1) % tm_count) for i in range(tm_count)])
-    core = position & 1
-    place = jnp.stack([position, core]).astype(jnp.int32)
+    me = position * lax.axis_size("roll") + lax.axis_index("roll")
+    side = me
+    for shift in (16, 8, 4, 2, 1):
+        side = side ^ (side >> shift)
+    side = side & 1
+    place = jnp.stack([position, side]).astype(jnp.int32)
     table = jnp.asarray(position_rows())
     basis, turned = (jnp.asarray(part) for part in relative_basis())
 
@@ -569,7 +619,7 @@
         place, horizon, x, start_memory.reshape(SEG, features), arrived,
         cotangent.reshape(rollouts * columns, features), table, basis, params,
     )
-    summed = unpack(place, sum_everywhere(halves, core), turned)
+    summed = unpack(place, sum_everywhere(halves, me, side), turned)
     return (out.reshape(layer_input.shape), dx.reshape(layer_input.shape)) + tuple(summed)
 
 

time: 83.1 us -> 74.2 us (0.89)
  waiting for transfers between devices: 21.5 us -> 14.4 us
  Pallas kernels: 32.6 us -> 26 us
  starting transfers between devices: 24.1 us -> 28.7 us
    ppermute x16 -> x18, waiting for transfers between devices: 18.7 us -> 11.6 us  [the longest x14 8.43 us: swap(): lax.ppermute(value, AXES, [(d, d ^ 1 << bits[side_of(d)] ^ 1 << core) for...]
    pallas_call x1, Pallas kernels: 30.1 us -> 23.4 us  [run_layer(): pl.pallas_call(layer_kernel, out_shape=(jax.ShapeDtypeStruct((rows, FEATU...]
    ppermute x16 -> x18, starting transfers between devices: 23.6 us -> 28.3 us  [the longest x14 27.3 us: swap(): lax.ppermute(value, AXES, [(d, d ^ 1 << bits[side_of(d)] ^ 1 << core) for...]
  transfers between devices with their start and end apart: 17 -> 19, of which waited for: 14 -> 12; matrix products, arithmetic and copies ran while one was open for 3% -> 3% of each run, Pallas kernels for 0% -> 0%
where the time goes in v3:
time: 74.2 us; the launch traced here: 74 us
  starting transfers between devices  28.7 us (39%)
  Pallas kernels  26 us (35%)
  waiting for transfers between devices  14.4 us (19%)
  other arithmetic  2.41 us (3%)
  local copies, waits for them, and re-layouts  1.48 us (2%)
  between operations  0.97 us (1%)
    ppermute x14, starting transfers between devices, swap(): lax.ppermute(value, AXES, [(d, d ^ 1 << bits[side_of(d)] ^ 1 << core) for...  27.3 us
    pallas_call x1, Pallas kernels, run_layer(): pl.pallas_call(layer_kernel, out_shape=(jax.ShapeDtypeStruct((rows, FEATU...  23.4 us
    ppermute x14, waiting for transfers between devices, swap(): lax.ppermute(value, AXES, [(d, d ^ 1 << bits[side_of(d)] ^ 1 << core) for...  8.43 us
    ppermute x4, waiting for transfers between devices, swap_cores(): return lax.ppermute(value, AXES, [(d, d ^ 1 << core) for d in range(count)])  3.13 us
    ppermute x1, waiting for transfers between devices, body(): lax.ppermute(x[-SEG:], 'tm', [(i, (i + 1) % tm_count) for i in range(tm_c...  2.88 us
    pallas_call x1, Pallas kernels, unpack(): pl.pallas_call(unpack_kernel, out_shape=shapes, in_specs=[smem] + [vmem]...  2.55 us
  transfers between devices with their start and end apart: 19, of which 12 were waited for; matrix products, arithmetic and copies ran while one was open for 3% of the time, Pallas kernels for 0%

profile of v3, /device:TPU:0, one launch (start us, length us, event | category | flops | bytes accessed | tf_op | source)
XLA Modules:
  0.0 74.0 jit_solution(5276128091280741308)
XLA Ops:
  0.7 0.7 %slice_bitcast_fusion = bf16[48,256]{1,0:T(8,128)(2,1)S(1)} fusion(bf16[1,768,256]{2,1,0:T(8,128)(2,1)} %param.22), kind=kLoop, calls=%fused_computation.28 | loop fusion | bytes 49152 | tf_op jit(solution)/shard_map/slice | solution.py:600
  1.4 0.5 collective-permute-start
  1.9 0.6 pad_add_fusion.place
  2.4 2.9 %collective-permute-done.refs_2_ = bf16[48,256]{1,0:T(8,128)(2,1)S(1)} collective-permute-done((bf16[48,256]{1,0:T(8,128)(2,1)S(1)}, bf16[48,256]{1,0:T(8,128)(2,1)S(1)}, u32[]{:S(2)}, u32[]{:S(2)}) %collective-permute-start) | collective-permute-done | bytes 24608 | tf_op jit(solution)/shard_map/ppermute | solution.py:600
  5.3 0.0 copy-start.3
  5.3 0.6 copy-done.3
  5.9 23.4 %layer.1 = (bf16[768,256]{1,0:T(8,128)(2,1)}, bf16[768,256]{1,0:T(8,128)(2,1)}, bf16[832,256]{1,0:T(8,128)(2,1)}, bf16[832,256]{1,0:T(8,128)(2,1)}, bf16[832,256]{1,0:T(8,128)(2,1)}, /*index=5*/bf16[832,256]{1,0:T(8,128)(2,1)}) custom-call(s32[2]{0:T(128)} %pad_add_fusion.place, s32[1,64]{1,0:T(1,128)} %horizon.1, bf16[768,256]{1,0:T(8,128)(2,1)} %bitcast.17, ...), custom_call_target="tpu_custom_call" | custom-call | tf_op jit(solution)/shard_map/layer/pallas_call | solution.py:465
  29.3 0.2 collective-permute-start.1
  29.5 0.4 collective-permute-start.10
  29.9 1.5 %collective-permute-done.1 = bf16[832,256]{1,0:T(8,128)(2,1)S(1)} collective-permute-done((bf16[832,256]{1,0:T(8,128)(2,1)}, bf16[832,256]{1,0:T(8,128)(2,1)S(1)}, u32[]{:S(2)}, u32[]{:S(2)}) %collective-permute-start.1) | collective-permute-done | bytes 426016 | tf_op jit(solution)/shard_map/ppermute | solution.py:554
  31.4 1.1 %add_convert_fusion.1 = bf16[832,256]{1,0:T(8,128)(2,1)S(1)} fusion(bf16[832,256]{1,0:T(8,128)(2,1)S(1)} %collective-permute-done.1, bf16[832,256]{1,0:T(8,128)(2,1)} %get-tuple-element.40), kind=kLoop, calls=%fused_computation.1 | loop fusion | flops 851968 | bytes 1277952 | tf_op jit(solution)/shard_map/convert_element_type | solution.py:562
  32.5 0.0 copy-start.2
  32.6 2.1 %collective-permute-start.2 = (bf16[416,256]{1,0:T(8,128)(2,1)S(1)}, bf16[416,256]{1,0:T(8,128)(2,1)S(1)}, u32[]{:S(2)}, u32[]{:S(2)}) collective-permute-start(bf16[416,256]{1,0:T(8,128)(2,1)S(1)} %constant_dynamic-slice_fusion.5), channel_id=1, source_target_pairs={{0,24},{1,8},{2,11},{3,27},{4,13},{5,29},{6,30},{7,14},{8,1},{9,17... | collective-permute-start | bytes 638984 | tf_op jit(solution)/shard_map/ppermute | solution.py:558
  34.7 0.0 collective-permute-done.10
  34.7 0.0 copy-done.2
  34.7 0.1 add_convert_fusion
  34.8 1.0 %collective-permute-start.11 = (bf16[416,256]{1,0:T(8,128)(2,1)S(1)}, bf16[416,256]{1,0:T(8,128)(2,1)S(1)}, u32[]{:S(2)}, u32[]{:S(2)}) collective-permute-start(bf16[416,256]{1,0:T(8,128)(2,1)S(1)} %constant_dynamic-slice_fusion.2), channel_id=1, source_target_pairs={{0,24},{1,8},{2,11},{3,27},{4,13},{5,29},{6,30},{7,14},{8,1},{9,17... | collective-permute-start | bytes 638984 | tf_op jit(solution)/shard_map/ppermute | solution.py:558
  35.8 2.4 %collective-permute-done.2 = bf16[416,256]{1,0:T(8,128)(2,1)S(1)} collective-permute-done((bf16[416,256]{1,0:T(8,128)(2,1)S(1)}, bf16[416,256]{1,0:T(8,128)(2,1)S(1)}, u32[]{:S(2)}, u32[]{:S(2)}) %collective-permute-start.2) | collective-permute-done | bytes 213024 | tf_op jit(solution)/shard_map/ppermute | solution.py:558
  38.2 0.1 add_convert_fusion.3
  38.3 2.1 %collective-permute-start.3 = (bf16[208,256]{1,0:T(8,128)(2,1)S(1)}, bf16[208,256]{1,0:T(8,128)(2,1)S(1)}, u32[]{:S(2)}, u32[]{:S(2)}) collective-permute-start(bf16[208,256]{1,0:T(8,128)(2,1)S(1)} %constant_dynamic-slice_fusion.4), channel_id=1, source_target_pairs={{0,9},{1,25},{2,26},{3,10},{4,28},{5,12},{6,15},{7,31},{8,16},{9,0... | collective-permute-start | bytes 319496 | tf_op jit(solution)/shard_map/ppermute | solution.py:558
  40.3 0.1 collective-permute-done.11
  40.5 0.1 add_convert_fusion.2
  40.6 1.8 %collective-permute-start.12 = (bf16[208,256]{1,0:T(8,128)(2,1)S(1)}, bf16[208,256]{1,0:T(8,128)(2,1)S(1)}, u32[]{:S(2)}, u32[]{:S(2)}) collective-permute-start(bf16[208,256]{1,0:T(8,128)(2,1)S(1)} %constant_dynamic-slice_fusion.1), channel_id=1, source_target_pairs={{0,9},{1,25},{2,26},{3,10},{4,28},{5,12},{6,15},{7,31},{8,16},{9,0... | collective-permute-start | bytes 319496 | tf_op jit(solution)/shard_map/ppermute | solution.py:558
  42.3 0.4 collective-permute-done.3
  42.8 1.9 %collective-permute-start.4 = (bf16[104,256]{1,0:T(8,128)(2,1)S(1)}, bf16[104,256]{1,0:T(8,128)(2,1)S(1)}, u32[]{:S(2)}, u32[]{:S(2)}) collective-permute-start(bf16[104,256]{1,0:T(8,128)(2,1)S(1)} %constant_dynamic-slice_fusion.3), channel_id=1, source_target_pairs={{0,10},{1,11},{2,8},{3,9},{4,14},{5,15},{6,12},{7,13},{8,2},{9,3},... | collective-permute-start | bytes 159752 | tf_op jit(solution)/shard_map/ppermute | solution.py:558
  44.7 0.1 collective-permute-done.12
  44.8 1.9 %collective-permute-start.13 = (bf16[104,256]{1,0:T(8,128)(2,1)S(1)}, bf16[104,256]{1,0:T(8,128)(2,1)S(1)}, u32[]{:S(2)}, u32[]{:S(2)}) collective-permute-start(bf16[104,256]{1,0:T(8,128)(2,1)S(1)} %constant_dynamic-slice_fusion), channel_id=1, source_target_pairs={{0,10},{1,11},{2,8},{3,9},{4,14},{5,15},{6,12},{7,13},{8,2},{9,3},... | collective-permute-start | bytes 159752 | tf_op jit(solution)/shard_map/ppermute | solution.py:558
  46.7 0.0 collective-permute-done.4
  46.7 2.7 %collective-permute-start.5 = (bf16[104,256]{1,0:T(8,128)(2,1)S(1)}, bf16[104,256]{1,0:T(8,128)(2,1)S(1)}, u32[]{:S(2)}, u32[]{:S(2)}) collective-permute-start(bf16[104,256]{1,0:T(8,128)(2,1)S(1)} %add_convert_fusion.9), channel_id=1, source_target_pairs={{0,12},{1,13},{2,14},{3,15},{4,8},{5,9},{6,10},{7,11},{8,4},{9,5},... | collective-permute-start | bytes 159752 | tf_op jit(solution)/shard_map/ppermute | solution.py:558
  49.4 0.0 collective-permute-done.13
  49.4 2.2 %collective-permute-start.14 = (bf16[104,256]{1,0:T(8,128)(2,1)S(1)}, bf16[104,256]{1,0:T(8,128)(2,1)S(1)}, u32[]{:S(2)}, u32[]{:S(2)}) collective-permute-start(bf16[104,256]{1,0:T(8,128)(2,1)S(1)} %add_convert_fusion.7), channel_id=1, source_target_pairs={{0,12},{1,13},{2,14},{3,15},{4,8},{5,9},{6,10},{7,11},{8,4},{9,5},... | collective-permute-start | bytes 159752 | tf_op jit(solution)/shard_map/ppermute | solution.py:558
  51.6 0.0 collective-permute-done.5
  51.6 1.7 %collective-permute-start.6 = (bf16[104,256]{1,0:T(8,128)(2,1)S(1)}, bf16[104,256]{1,0:T(8,128)(2,1)S(1)}, u32[]{:S(2)}, u32[]{:S(2)}) collective-permute-start(bf16[104,256]{1,0:T(8,128)(2,1)S(1)} %add_convert_fusion.8), channel_id=1, source_target_pairs={{0,10},{1,11},{2,8},{3,9},{4,14},{5,15},{6,12},{7,13},{8,2},{9,3},... | collective-permute-start | bytes 159752 | tf_op jit(solution)/shard_map/ppermute | solution.py:558
  53.3 0.9 %collective-permute-done.14 = bf16[104,256]{1,0:T(8,128)(2,1)S(1)} collective-permute-done((bf16[104,256]{1,0:T(8,128)(2,1)S(1)}, bf16[104,256]{1,0:T(8,128)(2,1)S(1)}, u32[]{:S(2)}, u32[]{:S(2)}) %collective-permute-start.14) | collective-permute-done | bytes 53280 | tf_op jit(solution)/shard_map/ppermute | solution.py:558
  54.2 1.6 %collective-permute-start.15 = (bf16[104,256]{1,0:T(8,128)(2,1)S(1)}, bf16[104,256]{1,0:T(8,128)(2,1)S(1)}, u32[]{:S(2)}, u32[]{:S(2)}) collective-permute-start(bf16[104,256]{1,0:T(8,128)(2,1)S(1)} %add_convert_fusion.6), channel_id=1, source_target_pairs={{0,10},{1,11},{2,8},{3,9},{4,14},{5,15},{6,12},{7,13},{8,2},{9,3},... | collective-permute-start | bytes 159752 | tf_op jit(solution)/shard_map/ppermute | solution.py:558
  55.9 0.0 collective-permute-done.6
  55.9 1.7 %collective-permute-start.7 = (bf16[208,256]{1,0:T(8,128)(2,1)S(1)}, bf16[208,256]{1,0:T(8,128)(2,1)S(1)}, u32[]{:S(2)}, u32[]{:S(2)}) collective-permute-start(bf16[208,256]{1,0:T(8,128)(2,1)S(1)} %pad_maximum_fusion.4), channel_id=1, source_target_pairs={{0,9},{1,25},{2,26},{3,10},{4,28},{5,12},{6,15},{7,31},{8,16},{9,0... | collective-permute-start | bytes 319496 | tf_op jit(solution)/shard_map/ppermute | solution.py:558
  57.6 0.2 collective-permute-done.15
  57.9 2.7 %collective-permute-start.16 = (bf16[208,256]{1,0:T(8,128)(2,1)S(1)}, bf16[208,256]{1,0:T(8,128)(2,1)S(1)}, u32[]{:S(2)}, u32[]{:S(2)}) collective-permute-start(bf16[208,256]{1,0:T(8,128)(2,1)S(1)} %pad_maximum_fusion.5), channel_id=1, source_target_pairs={{0,9},{1,25},{2,26},{3,10},{4,28},{5,12},{6,15},{7,31},{8,16},{9,0... | collective-permute-start | bytes 319496 | tf_op jit(solution)/shard_map/ppermute | solution.py:558
  60.6 0.0 collective-permute-done.7
  60.6 1.3 %collective-permute-start.8 = (bf16[416,256]{1,0:T(8,128)(2,1)S(1)}, bf16[416,256]{1,0:T(8,128)(2,1)S(1)}, u32[]{:S(2)}, u32[]{:S(2)}) collective-permute-start(bf16[416,256]{1,0:T(8,128)(2,1)S(1)} %pad_maximum_fusion.2), channel_id=1, source_target_pairs={{0,24},{1,8},{2,11},{3,27},{4,13},{5,29},{6,30},{7,14},{8,1},{9,17... | collective-permute-start | bytes 638984 | tf_op jit(solution)/shard_map/ppermute | solution.py:558
  61.9 1.0 %collective-permute-done.16 = bf16[208,256]{1,0:T(8,128)(2,1)S(1)} collective-permute-done((bf16[208,256]{1,0:T(8,128)(2,1)S(1)}, bf16[208,256]{1,0:T(8,128)(2,1)S(1)}, u32[]{:S(2)}, u32[]{:S(2)}) %collective-permute-start.16) | collective-permute-done | bytes 106528 | tf_op jit(solution)/shard_map/ppermute | solution.py:558
  63.0 2.8 %collective-permute-start.17 = (bf16[416,256]{1,0:T(8,128)(2,1)S(1)}, bf16[416,256]{1,0:T(8,128)(2,1)S(1)}, u32[]{:S(2)}, u32[]{:S(2)}) collective-permute-start(bf16[416,256]{1,0:T(8,128)(2,1)S(1)} %pad_maximum_fusion.3), channel_id=1, source_target_pairs={{0,24},{1,8},{2,11},{3,27},{4,13},{5,29},{6,30},{7,14},{8,1},{9,17... | collective-permute-start | bytes 638984 | tf_op jit(solution)/shard_map/ppermute | solution.py:558
  65.8 0.3 collective-permute-done.8
  66.1 0.1 broadcast_select_fusion.3
  66.2 0.2 collective-permute-start.9
  66.4 3.0 %collective-permute-done.17 = bf16[416,256]{1,0:T(8,128)(2,1)S(1)} collective-permute-done((bf16[416,256]{1,0:T(8,128)(2,1)S(1)}, bf16[416,256]{1,0:T(8,128)(2,1)S(1)}, u32[]{:S(2)}, u32[]{:S(2)}) %collective-permute-start.17) | collective-permute-done | bytes 213024 | tf_op jit(solution)/shard_map/ppermute | solution.py:558
  69.3 0.1 broadcast_select_fusion.1
  69.4 0.0 copy-start
  69.4 0.0 copy-start.1
  69.5 0.2 collective-permute-start.18
  69.7 0.0 collective-permute-done.9.refs_1_
  69.7 1.7 %collective-permute-done.18.refs_3_ = bf16[832,256]{1,0:T(8,128)(2,1)S(1)} collective-permute-done((bf16[832,256]{1,0:T(8,128)(2,1)S(1)}, bf16[832,256]{1,0:T(8,128)(2,1)S(1)}, u32[]{:S(2)}, u32[]{:S(2)}) %collective-permute-start.18) | collective-permute-done | bytes 426016 | tf_op jit(solution)/shard_map/ppermute | solution.py:554
  71.3 0.0 copy-done
  71.3 0.0 copy-done.1
  71.3 2.6 %unpack.1 = (f32[256]{0:T(256)}, f32[256]{0:T(256)}, f32[256,256]{1,0:T(8,128)}, f32[256,256]{1,0:T(8,128)}, f32[256,256]{1,0:T(8,128)}, /*index=5*/f32[256,256]...) custom-call(s32[2]{0:T(128)S(1)} %copy-done.1, ...), custom_call_target="tpu_custom_call" | custom-call | tf_op jit(solution)/shard_map/unpack/pallas_call | solution.py:525
  (22 shorter events, 0.5 us)
Async XLA Ops:
  1.4 3.9 %collective-permute-start = (bf16[48,256]{1,0:T(8,128)(2,1)S(1)}, bf16[48,256]{1,0:T(8,128)(2,1)S(1)}, u32[]{:S(2)}, u32[]{:S(2)}) collective-permute-start(bf16[48,256]{1,0:T(8,128)(2,1)S(1)} %slice_bitcast_fusion), channel_id=1, source_target_pairs={{0,8},{8,16},{16,24},{24,0},{1,9},{9,17},{17,25},{25,1},{2,10},{10... | collective-permute-start | bytes 73736 | tf_op jit(solution)/shard_map/ppermute | solution.py:600
  5.3 0.6 copy-start.3
  29.3 2.0 %collective-permute-start.1 = (bf16[832,256]{1,0:T(8,128)(2,1)}, bf16[832,256]{1,0:T(8,128)(2,1)S(1)}, u32[]{:S(2)}, u32[]{:S(2)}) collective-permute-start(bf16[832,256]{1,0:T(8,128)(2,1)} %get-tuple-element.41), channel_id=1, source_target_pairs={{0,8},{1,9},{2,10},{3,11},{4,12},{5,13},{6,14},{7,15},{8,0},{9,1},... | collective-permute-start | bytes 1277960 | tf_op jit(solution)/shard_map/ppermute | solution.py:554
  29.5 5.1 %collective-permute-start.10 = (bf16[832,256]{1,0:T(8,128)(2,1)}, bf16[832,256]{1,0:T(8,128)(2,1)S(1)}, u32[]{:S(2)}, u32[]{:S(2)}) collective-permute-start(bf16[832,256]{1,0:T(8,128)(2,1)} %get-tuple-element.43), channel_id=1, source_target_pairs={{0,8},{1,9},{2,10},{3,11},{4,12},{5,13},{6,14},{7,15},{8,0},{9,1},... | collective-permute-start | bytes 1277960 | tf_op jit(solution)/shard_map/ppermute | solution.py:554
  32.5 2.2 %copy-start.2 = (bf16[832,256]{1,0:T(8,128)(2,1)S(1)}, bf16[832,256]{1,0:T(8,128)(2,1)}, u32[]{:S(2)}) copy-start(bf16[832,256]{1,0:T(8,128)(2,1)} %get-tuple-element.42) | copy-start | bytes 1277956
  32.6 5.6 %collective-permute-start.2 = (bf16[416,256]{1,0:T(8,128)(2,1)S(1)}, bf16[416,256]{1,0:T(8,128)(2,1)S(1)}, u32[]{:S(2)}, u32[]{:S(2)}) collective-permute-start(bf16[416,256]{1,0:T(8,128)(2,1)S(1)} %constant_dynamic-slice_fusion.5), channel_id=1, source_target_pairs={{0,24},{1,8},{2,11},{3,27},{4,13},{5,29},{6,30},{7,14},{8,1},{9,17... | collective-permute-start | bytes 638984 | tf_op jit(solution)/shard_map/ppermute | solution.py:558
  34.8 5.7 %collective-permute-start.11 = (bf16[416,256]{1,0:T(8,128)(2,1)S(1)}, bf16[416,256]{1,0:T(8,128)(2,1)S(1)}, u32[]{:S(2)}, u32[]{:S(2)}) collective-permute-start(bf16[416,256]{1,0:T(8,128)(2,1)S(1)} %constant_dynamic-slice_fusion.2), channel_id=1, source_target_pairs={{0,24},{1,8},{2,11},{3,27},{4,13},{5,29},{6,30},{7,14},{8,1},{9,17... | collective-permute-start | bytes 638984 | tf_op jit(solution)/shard_map/ppermute | solution.py:558
  38.3 4.5 %collective-permute-start.3 = (bf16[208,256]{1,0:T(8,128)(2,1)S(1)}, bf16[208,256]{1,0:T(8,128)(2,1)S(1)}, u32[]{:S(2)}, u32[]{:S(2)}) collective-permute-start(bf16[208,256]{1,0:T(8,128)(2,1)S(1)} %constant_dynamic-slice_fusion.4), channel_id=1, source_target_pairs={{0,9},{1,25},{2,26},{3,10},{4,28},{5,12},{6,15},{7,31},{8,16},{9,0... | collective-permute-start | bytes 319496 | tf_op jit(solution)/shard_map/ppermute | solution.py:558
  40.6 4.2 %collective-permute-start.12 = (bf16[208,256]{1,0:T(8,128)(2,1)S(1)}, bf16[208,256]{1,0:T(8,128)(2,1)S(1)}, u32[]{:S(2)}, u32[]{:S(2)}) collective-permute-start(bf16[208,256]{1,0:T(8,128)(2,1)S(1)} %constant_dynamic-slice_fusion.1), channel_id=1, source_target_pairs={{0,9},{1,25},{2,26},{3,10},{4,28},{5,12},{6,15},{7,31},{8,16},{9,0... | collective-permute-start | bytes 319496 | tf_op jit(solution)/shard_map/ppermute | solution.py:558
  42.8 3.9 %collective-permute-start.4 = (bf16[104,256]{1,0:T(8,128)(2,1)S(1)}, bf16[104,256]{1,0:T(8,128)(2,1)S(1)}, u32[]{:S(2)}, u32[]{:S(2)}) collective-permute-start(bf16[104,256]{1,0:T(8,128)(2,1)S(1)} %constant_dynamic-slice_fusion.3), channel_id=1, source_target_pairs={{0,10},{1,11},{2,8},{3,9},{4,14},{5,15},{6,12},{7,13},{8,2},{9,3},... | collective-permute-start | bytes 159752 | tf_op jit(solution)/shard_map/ppermute | solution.py:558
  44.8 4.6 %collective-permute-start.13 = (bf16[104,256]{1,0:T(8,128)(2,1)S(1)}, bf16[104,256]{1,0:T(8,128)(2,1)S(1)}, u32[]{:S(2)}, u32[]{:S(2)}) collective-permute-start(bf16[104,256]{1,0:T(8,128)(2,1)S(1)} %constant_dynamic-slice_fusion), channel_id=1, source_target_pairs={{0,10},{1,11},{2,8},{3,9},{4,14},{5,15},{6,12},{7,13},{8,2},{9,3},... | collective-permute-start | bytes 159752 | tf_op jit(solution)/shard_map/ppermute | solution.py:558
  46.7 4.9 %collective-permute-start.5 = (bf16[104,256]{1,0:T(8,128)(2,1)S(1)}, bf16[104,256]{1,0:T(8,128)(2,1)S(1)}, u32[]{:S(2)}, u32[]{:S(2)}) collective-permute-start(bf16[104,256]{1,0:T(8,128)(2,1)S(1)} %add_convert_fusion.9), channel_id=1, source_target_pairs={{0,12},{1,13},{2,14},{3,15},{4,8},{5,9},{6,10},{7,11},{8,4},{9,5},... | collective-permute-start | bytes 159752 | tf_op jit(solution)/shard_map/ppermute | solution.py:558
  49.4 4.8 %collective-permute-start.14 = (bf16[104,256]{1,0:T(8,128)(2,1)S(1)}, bf16[104,256]{1,0:T(8,128)(2,1)S(1)}, u32[]{:S(2)}, u32[]{:S(2)}) collective-permute-start(bf16[104,256]{1,0:T(8,128)(2,1)S(1)} %add_convert_fusion.7), channel_id=1, source_target_pairs={{0,12},{1,13},{2,14},{3,15},{4,8},{5,9},{6,10},{7,11},{8,4},{9,5},... | collective-permute-start | bytes 159752 | tf_op jit(solution)/shard_map/ppermute | solution.py:558
  51.6 4.3 %collective-permute-start.6 = (bf16[104,256]{1,0:T(8,128)(2,1)S(1)}, bf16[104,256]{1,0:T(8,128)(2,1)S(1)}, u32[]{:S(2)}, u32[]{:S(2)}) collective-permute-start(bf16[104,256]{1,0:T(8,128)(2,1)S(1)} %add_convert_fusion.8), channel_id=1, source_target_pairs={{0,10},{1,11},{2,8},{3,9},{4,14},{5,15},{6,12},{7,13},{8,2},{9,3},... | collective-permute-start | bytes 159752 | tf_op jit(solution)/shard_map/ppermute | solution.py:558
  54.2 3.6 %collective-permute-start.15 = (bf16[104,256]{1,0:T(8,128)(2,1)S(1)}, bf16[104,256]{1,0:T(8,128)(2,1)S(1)}, u32[]{:S(2)}, u32[]{:S(2)}) collective-permute-start(bf16[104,256]{1,0:T(8,128)(2,1)S(1)} %add_convert_fusion.6), channel_id=1, source_target_pairs={{0,10},{1,11},{2,8},{3,9},{4,14},{5,15},{6,12},{7,13},{8,2},{9,3},... | collective-permute-start | bytes 159752 | tf_op jit(solution)/shard_map/ppermute | solution.py:558
  55.9 4.7 %collective-permute-start.7 = (bf16[208,256]{1,0:T(8,128)(2,1)S(1)}, bf16[208,256]{1,0:T(8,128)(2,1)S(1)}, u32[]{:S(2)}, u32[]{:S(2)}) collective-permute-start(bf16[208,256]{1,0:T(8,128)(2,1)S(1)} %pad_maximum_fusion.4), channel_id=1, source_target_pairs={{0,9},{1,25},{2,26},{3,10},{4,28},{5,12},{6,15},{7,31},{8,16},{9,0... | collective-permute-start | bytes 319496 | tf_op jit(solution)/shard_map/ppermute | solution.py:558
  57.9 5.0 %collective-permute-start.16 = (bf16[208,256]{1,0:T(8,128)(2,1)S(1)}, bf16[208,256]{1,0:T(8,128)(2,1)S(1)}, u32[]{:S(2)}, u32[]{:S(2)}) collective-permute-start(bf16[208,256]{1,0:T(8,128)(2,1)S(1)} %pad_maximum_fusion.5), channel_id=1, source_target_pairs={{0,9},{1,25},{2,26},{3,10},{4,28},{5,12},{6,15},{7,31},{8,16},{9,0... | collective-permute-start | bytes 319496 | tf_op jit(solution)/shard_map/ppermute | solution.py:558
  60.6 5.4 %collective-permute-start.8 = (bf16[416,256]{1,0:T(8,128)(2,1)S(1)}, bf16[416,256]{1,0:T(8,128)(2,1)S(1)}, u32[]{:S(2)}, u32[]{:S(2)}) collective-permute-start(bf16[416,256]{1,0:T(8,128)(2,1)S(1)} %pad_maximum_fusion.2), channel_id=1, source_target_pairs={{0,24},{1,8},{2,11},{3,27},{4,13},{5,29},{6,30},{7,14},{8,1},{9,17... | collective-permute-start | bytes 638984 | tf_op jit(solution)/shard_map/ppermute | solution.py:558
  63.0 6.3 %collective-permute-start.17 = (bf16[416,256]{1,0:T(8,128)(2,1)S(1)}, bf16[416,256]{1,0:T(8,128)(2,1)S(1)}, u32[]{:S(2)}, u32[]{:S(2)}) collective-permute-start(bf16[416,256]{1,0:T(8,128)(2,1)S(1)} %pad_maximum_fusion.3), channel_id=1, source_target_pairs={{0,24},{1,8},{2,11},{3,27},{4,13},{5,29},{6,30},{7,14},{8,1},{9,17... | collective-permute-start | bytes 638984 | tf_op jit(solution)/shard_map/ppermute | solution.py:558
  66.2 3.5 %collective-permute-start.9 = (bf16[832,256]{1,0:T(8,128)(2,1)S(1)}, bf16[832,256]{1,0:T(8,128)(2,1)S(1)}, u32[]{:S(2)}, u32[]{:S(2)}) collective-permute-start(bf16[832,256]{1,0:T(8,128)(2,1)S(1)} %pad_maximum_fusion.refs_0_), channel_id=1, source_target_pairs={{0,8},{1,9},{2,10},{3,11},{4,12},{5,13},{6,14},{7,15},{8,0},{9,1},... | collective-permute-start | bytes 1277960 | tf_op jit(solution)/shard_map/ppermute | solution.py:554
  69.4 1.9 %copy-start = (bf16[256,256]{1,0:T(8,128)(2,1)S(1)}, bf16[256,256]{1,0:T(8,128)(2,1)}, u32[]{:S(2)}) copy-start(bf16[256,256]{1,0:T(8,128)(2,1)} %constant.36.clone.refs_4_) | copy-start | bytes 393220
  69.4 1.9 %copy-start.1 = (s32[2]{0:T(128)S(1)}, s32[2]{0:T(128)}, u32[]{:S(2)}) copy-start(s32[2]{0:T(128)} %pad_add_fusion.place) | copy-start | bytes 28
  69.5 1.8 %collective-permute-start.18 = (bf16[832,256]{1,0:T(8,128)(2,1)S(1)}, bf16[832,256]{1,0:T(8,128)(2,1)S(1)}, u32[]{:S(2)}, u32[]{:S(2)}) collective-permute-start(bf16[832,256]{1,0:T(8,128)(2,1)S(1)} %pad_maximum_fusion.1.refs_2_), channel_id=1, source_target_pairs={{0,8},{1,9},{2,10},{3,11},{4,12},{5,13},{6,14},{7,15},{8,0},{9,1},... | collective-permute-start | bytes 1277960 | tf_op jit(solution)/shard_map/ppermute | solution.py:554

commit v4 on v3

v4 whole, which is shorter than its diff:
```python
import functools
import math
import types

import jax
import jax.numpy as jnp
import numpy as np
from jax import lax
from jax.experimental import pallas as pl
from jax.experimental.pallas import tpu as pltpu
from jax.sharding import PartitionSpec as P

HEADS = 8
HEAD_DIM = 32
SEG = 48
STEP = 3
FEATURES = 256
HIDDEN = 1024
LANES = 128
GROUP = LANES // HEAD_DIM
EPSILON = 1e-05
MASKED = -4000000000.0
SCALING = 1.0 / math.sqrt(HEAD_DIM)
SCALING_BITS = SCALING / math.log(2.0)
GELU_A = 0.7978845608028654
GELU_B = 0.044715 * GELU_A
BF = jnp.bfloat16
F32 = jnp.float32

PIPES = 2
PART_ROWS = 832
EARLY_ROWS = (832, 320)
LATE_ROWS = 512
EXPAND_AT = (0, 256, 512, 1664)
SHRINK_AT = (832, 1088, 1344, 1984)
OUTPUT_AT = (768, 1600, 1920, 2240)
OUTPUT_PIECE = 64
QUERY_AT, KEY_AT, VALUE_AT, RELATIVE_AT, VECTOR_AT = 0, 256, 512, 768, 896
(V_CONTENT, V_POSITION, V_GAIN1, V_SHIFT1, V_GAIN2, V_SHIFT2, V_SHRINK, V_EXPAND) = range(8)
VECTOR_ROWS = 16


def position_rows():
    distance = (2 * SEG - 1 - np.arange(2 * SEG)).astype(np.float32)
    freqs = 10000.0 ** (-(2.0 * np.arange(FEATURES // 2)) / FEATURES)
    angles = distance[:, None] * freqs.astype(np.float32)[None, :]
    table = np.concatenate([np.sin(angles), np.cos(angles)], axis=-1)
    return np.pad(table, ((0, LANES - 2 * SEG), (0, 0))).astype(BF)


def relative_basis():
    count = 2 * SEG
    k, c = np.arange(count)[:, None], np.arange(count)[None, :]
    basis = np.cos(np.pi * k * (2 * c + 1) / (2 * count)) * np.where(k == 0, np.sqrt(1.0 / count), np.sqrt(2.0 / count))
    basis = np.pad(basis, ((0, LANES - count), (0, LANES - count)))

    def parts(values):
        high = values.astype(BF)
        low = (values - high.astype(np.float64)).astype(BF)
        return np.concatenate([high, low], axis=0)

    return parts(basis), parts(basis @ position_rows().astype(np.float64))


def tables():
    return jnp.asarray(position_rows()), jnp.asarray(relative_basis()[0])


def interleave(*steps):
    running = [[0, count, part] for count, part in steps]
    while running:
        slowest = min(running, key=lambda entry: entry[0] / entry[1])
        slowest[0] += 1
        if next(slowest[2], None) is None:
            running.remove(slowest)


def dot(a, b):
    return lax.dot_general(a, b, (((1,), (0,)), ((), ())), preferred_element_type=F32)


def dot_t(a, b):
    return lax.dot_general(a, b, (((1,), (1,)), ((), ())), preferred_element_type=F32)


def t_dot(a, b):
    return lax.dot_general(a, b, (((0,), (0,)), ((), ())), preferred_element_type=F32)


def normalize(rows):
    center = rows - jnp.mean(rows, axis=-1, keepdims=True)
    spread = jnp.mean(center * center, axis=-1, keepdims=True)
    scale = lax.rsqrt(spread + EPSILON)
    return center * scale, scale


def column_sum(rows):
    return jnp.sum(rows, axis=0, keepdims=True)


def stack_heads(rows, head_masks):
    return jnp.concatenate([rows * mask for mask in head_masks], axis=0)


def unshift(rows, row_bits):
    rolled = jnp.concatenate(
        [pltpu.roll(rows[a : a + 8], SEG - 8 - a, 1) for a in range(0, SEG - 8, 8)] + [rows[SEG - 8 :]], axis=0
    )
    for step, bit in row_bits:
        rolled = jnp.where(bit, pltpu.roll(rolled, step, 1), rolled)
    return rolled


def pick_heads(rows, lane_head):
    picked = rows[0:SEG]
    for h in range(1, GROUP):
        picked = jnp.where(lane_head == h, rows[h * SEG : (h + 1) * SEG], picked)
    return picked


COPIES = 21
(C_X, C_START, C_ARRIVED, C_COT, C_GAIN1, C_SHIFT1, C_WQ, C_WK, C_WV, C_WR, C_CBIAS, C_PBIAS, C_WO,
 C_GAIN2, C_SHIFT2, C_W1, C_B1, C_W2, C_B2, C_TABLE, C_BASIS) = range(COPIES)
FIRST_COPIES = (C_TABLE, C_WR, C_X, C_GAIN1, C_SHIFT1, C_START, C_ARRIVED, C_WK, C_WV, C_WQ, C_CBIAS, C_PBIAS)
LATER_COPIES = (C_WO, C_GAIN2, C_SHIFT2, C_W1, C_B1, C_COT, C_W2, C_B2, C_BASIS)


def own_place():
    position = lax.axis_index("tm")
    me = position * lax.axis_size("roll") + lax.axis_index("roll")
    side = me
    for shift in (16, 8, 4, 2, 1):
        side = side ^ (side >> shift)
    return position, me, side & 1


def layer_kernel(horizon_source, *refs):
    sources, refs = refs[:COPIES], refs[COPIES:]
    (out_target, dx_target, *halves), refs = refs[: 2 + 2 * PIPES], refs[2 + 2 * PIPES :]
    targets, (sems, out_sems, half_sems, horizon, out, dx, early, late, *scratch) = refs[:COPIES], refs[COPIES:]
    position, _, side = own_place()
    lengths = pltpu.make_async_copy(horizon_source, horizon, sems.at[COPIES])
    lengths.start()
    moves = [pltpu.make_async_copy(a, b, sems.at[i]) for i, (a, b) in enumerate(zip(sources, targets))]
    for i in FIRST_COPIES + LATER_COPIES:
        moves[i].start()
    leaving = []

    def leave(move):
        move.start()
        leaving.append(move)

    def send_rows(which, at):
        source, target = ((out, out_target), (dx, dx_target))[which]
        leave(pltpu.make_async_copy(source.at[at], target.at[at], out_sems.at[len(leaving)]))

    def send_early():
        start = 0
        for p in range(PIPES):
            for k, half in enumerate((side, 1 - side)):
                at = pl.ds(pl.multiple_of(start + half * EARLY_ROWS[p], 64), EARLY_ROWS[p])
                to = halves[2 * p + k].at[0 : EARLY_ROWS[p]]
                leave(pltpu.make_async_copy(early.at[at], to, half_sems.at[2 * p + k]))
            start += 2 * EARLY_ROWS[p]

    def send_late():
        for k, half in enumerate((side, 1 - side)):
            at = pl.ds(pl.multiple_of(half * LATE_ROWS, LATE_ROWS), LATE_ROWS)
            to = halves[2 + k].at[EARLY_ROWS[1] : PART_ROWS]
            leave(pltpu.make_async_copy(late.at[at], to, half_sems.at[2 * PIPES + k]))

    compute_layer(
        position, horizon, lengths, moves, (send_rows, send_early, send_late), *targets, out, dx, early, late, *scratch
    )
    for move in leaving:
        move.wait()


def compute_layer(
    position, horizon, lengths, moves, sends, x, start, arrived, cot, gain1, shift1, wq, wk, wv, wr, cbias, pbias, wo,
    gain2, shift2, w1, b1, w2, b2, table, basis,
    out, dx, early, late,
    nl, xhat, rstd, content, placed, keys_even, keys_odd, values_even, values_odd, relblock, raw, lows, inverses, mixed,
    hid, n2, act, bpre, bmix, bhid, bhl, bcont, bql, braw, kgm, kgs, vgm, vgs, vec,
):
    rows = x.shape[0]
    segments = rows // SEG
    send_rows, send_early, send_late = sends
    vec[...] = jnp.zeros_like(vec)

    def wait_for(*names):
        for i in names:
            moves[i].wait()

    wait_for(C_TABLE, C_WR)
    rel = dot(table[...], wr[...])
    wide_head = lax.broadcasted_iota(jnp.int32, (LANES, FEATURES), 1) // HEAD_DIM
    for h in range(HEADS):
        relblock[h * LANES : (h + 1) * LANES] = jnp.where(wide_head == h, rel, 0.0).astype(BF)

    wait_for(C_X, C_GAIN1, C_SHIFT1, C_START, C_ARRIVED, C_WK, C_WV)
    odd_lane = (lax.broadcasted_iota(jnp.int32, (1, LANES), 1) // HEAD_DIM) & 1
    parity_masks = [(odd_lane == q).astype(F32) for q in range(2)]

    def project(normed, at, count):
        key, value = dot(normed, wk[...]), dot(normed, wv[...])
        for q, (ks, vs) in enumerate(((keys_even, values_even), (keys_odd, values_odd))):
            for g in range(HEADS // GROUP):
                lanes = slice(g * LANES, (g + 1) * LANES)
                ks[pl.ds(at, count), lanes] = (key[:, lanes] * parity_masks[q]).astype(BF)
                vs[pl.ds(at, count), 2 * g * LANES : (2 * g + 1) * LANES] = (value[:, lanes] * parity_masks[q]).astype(BF)

    memory = jnp.where(position == 0, start[...].astype(F32), arrived[...].astype(F32))
    unit, scale = normalize(memory)
    xhat[0:SEG] = unit
    rstd[0:SEG] = scale
    normed = (unit * gain1[...] + shift1[...]).astype(BF)
    nl[0:SEG] = normed
    project(normed, 0, SEG)
    wait_for(C_WQ, C_CBIAS, C_PBIAS)
    lengths.wait()
    block = 8 * SEG
    for edge in range(block, rows + 1, block):
        ahead = slice(edge + SEG, edge + LANES - SEG)
        for ref in (keys_even, keys_odd, values_even, values_odd):
            ref[ahead] = jnp.zeros((LANES - 2 * SEG, ref.shape[1]), BF)
    for q, ref in enumerate((values_even, values_odd)):
        ones = jnp.broadcast_to(parity_masks[q], (ref.shape[0], LANES)).astype(BF)
        for g in range(HEADS // GROUP):
            ref[:, (2 * g + 1) * LANES : (2 * g + 2) * LANES] = ones
    blocks = rows // block
    lane_head = lax.broadcasted_iota(jnp.int32, (SEG, LANES), 1) // HEAD_DIM
    head_masks = [(lane_head == h).astype(F32).astype(BF) for h in range(GROUP)]
    key_at = lax.broadcasted_iota(jnp.int32, (SEG, LANES), 1)
    query_at = lax.broadcasted_iota(jnp.int32, (SEG, LANES), 0) + SEG
    low_row = 7 - (query_at & 7)
    row_bits = [(step, (low_row & step) != 0) for step in (1, 2, 4)]
    upper = (lax.broadcasted_iota(jnp.int32, (SEG, FEATURES), 1) & (HEAD_DIM // 2)) != 0
    first_pair = key_at < 2 * HEAD_DIM
    pair_masks = [first_pair.astype(F32).astype(BF), (key_at >= 2 * HEAD_DIM).astype(F32).astype(BF)]
    blank = jnp.zeros((SEG, LANES), BF)

    def first(i):
        at = pl.ds(i * block, block)
        to = pl.ds(i * block + SEG, block)
        unit, scale = normalize(x[at].astype(F32))
        xhat[to] = unit
        rstd[to] = scale
        normed = (unit * gain1[...] + shift1[...]).astype(BF)
        nl[to] = normed
        yield 1
        project(normed, i * block + SEG, block)
        yield 1
        query = dot(normed, wq[...])
        content[at] = (query + cbias[...]).astype(BF)
        low = (query + pbias[...]).astype(BF)
        placed[at] = low
        yield 1
        for f in range(HEADS * LANES // FEATURES):
            cols = slice(f * FEATURES, (f + 1) * FEATURES)
            raw[at, cols] = dot_t(low, relblock[cols])
            yield 1

    def units_of(i):
        units = []
        for s in range(i * block // SEG, (i + 1) * block // SEG):
            u = types.SimpleNamespace()
            u.s, u.at, u.window = s, pl.ds(s * SEG, SEG), pl.ds(s * SEG, LANES)
            u.pairs = [pl.ds((s * HEADS // 2 + p) * SEG, SEG) for p in range(HEADS // 2)]
            units.append(u)
        return units

    def window_keys(u):
        return jnp.concatenate([keys_even[u.window], keys_odd[u.window]], axis=0)

    def window_values(u, g):
        lanes = slice(2 * g * LANES, (2 * g + 2) * LANES)
        return jnp.concatenate([values_even[u.window, lanes], values_odd[u.window, lanes]], axis=0)

    def group_lanes(g):
        return slice(g * LANES, (g + 1) * LANES)

    def allow(s):
        number = position * segments + s
        current = horizon[0, number]
        previous = jnp.where(number == 0, SEG // STEP, horizon[0, jnp.maximum(number - 1, 0)])
        live = key_at < jnp.where(key_at < SEG, STEP * previous, SEG + STEP * current)
        return (key_at <= query_at) & (live | (key_at == query_at))

    def score(u):
        parts = []
        for p in range(HEADS // 2):
            g = p // 2
            part = content[u.at, group_lanes(g)] * pair_masks[p % 2]
            parts.append(jnp.concatenate([part, blank] if g == 0 else [blank, part], axis=1))
        u.direct = dot_t(jnp.concatenate(parts, axis=0), window_keys(u))

    def mask(u):
        allowed = allow(u.s)
        u.scores = []
        for head in range(HEADS):
            p, q = head // 2, head % 2
            shifted = pltpu.roll(
                raw[u.at, head * LANES : (head + 1) * LANES], LANES - SEG + 1, 1, stride=1, stride_axis=0
            )
            direct = u.direct[p * SEG : (p + 1) * SEG, q * LANES : (q + 1) * LANES]
            u.scores.append(jnp.where(allowed, direct + shifted, MASKED))
        u.tops = [jnp.max(v, axis=-1, keepdims=True) for v in u.scores]

    def exponentiate(u):
        u.low = [jnp.exp2((v - top) * SCALING_BITS).astype(BF) for v, top in zip(u.scores, u.tops)]
        u.low = [jnp.concatenate(u.low[2 * p : 2 * p + 2], axis=1) for p in range(HEADS // 2)]
        for p in range(HEADS // 2):
            lows[u.pairs[p]] = u.low[p]

    def mix(u):
        u.both = [
            dot(jnp.concatenate(u.low[2 * g : 2 * g + 2], axis=0), window_values(u, g)) for g in range(HEADS // GROUP)
        ]

    def finish(u):
        for g in range(HEADS // GROUP):
            both = u.both[g]
            total = jnp.where(first_pair, both[:SEG, LANES:], both[SEG:, LANES:])
            inverse = 1.0 / total
            mx = jnp.where(first_pair, both[:SEG, :LANES], both[SEG:, :LANES]) * inverse
            mixed[u.at, group_lanes(g)] = mx.astype(BF)
            bcont[u.at, group_lanes(g)] = mx
            inverses[u.at, group_lanes(g)] = inverse

    def staged(i, stages):
        units = units_of(i)
        for stage in stages:
            for u in units:
                stage(u)
                yield 1

    def attend(i):
        return staged(i, (score, mask, exponentiate, mix, finish))

    def feed(i):
        at = pl.ds(i * block, block)
        hidden = x[at].astype(F32) + dot(mixed[at], wo[...])
        yield 1
        unit, scale = normalize(hidden)
        low = (unit * gain2[...] + shift2[...]).astype(BF)
        n2[at] = low
        yield 1
        back = cot[at]
        for f in range(HIDDEN // FEATURES):
            cols = slice(f * FEATURES, (f + 1) * FEATURES)
            v = dot(low, w1[:, cols]) + b1[:, cols]
            grad = dot_t(back, w2[cols])
            yield 1
            square = v * v
            half = 0.5 + 0.5 * jnp.tanh(v * (GELU_A + GELU_B * square))
            active = v * half
            act[at, cols] = active.astype(BF)
            slope = half + (2.0 * active) * (1.0 - half) * (GELU_A + (3.0 * GELU_B) * square)
            grad = grad * slope
            vec[V_EXPAND + f : V_EXPAND + f + 1] += column_sum(grad)
            bpre[at, cols] = grad.astype(BF)
            yield 1
        out[at] = (hidden + dot(act[at], w2[...]) + b2[...]).astype(BF)
        send_rows(0, at)
        yield 1
        bn = dot_t(bpre[at], w1[...])
        yield 1
        back = back.astype(F32)
        vec[V_SHRINK : V_SHRINK + 1] += column_sum(back)
        vec[V_GAIN2 : V_GAIN2 + 1] += column_sum(bn * unit)
        vec[V_SHIFT2 : V_SHIFT2 + 1] += column_sum(bn)
        u = bn * gain2[...]
        inner = u - jnp.mean(u, axis=-1, keepdims=True) - unit * jnp.mean(u * unit, axis=-1, keepdims=True)
        bh = back + inner * scale
        bhid[at] = bh
        bl = bh.astype(BF)
        bhl[at] = bl
        yield 1
        bmix[at] = dot_t(bl, wo[...]).astype(BF)
        yield 1

    def feed_weights():
        for f in range(HIDDEN // FEATURES):
            cols = slice(f * FEATURES, (f + 1) * FEATURES)
            early[EXPAND_AT[f] : EXPAND_AT[f] + FEATURES] = t_dot(n2[...], bpre[:, cols]).astype(BF)
            yield 1
            early[SHRINK_AT[f] : SHRINK_AT[f] + FEATURES] = t_dot(act[:, cols], cot[...]).astype(BF)
            yield 1
        weight = t_dot(mixed[...], bhl[...]).astype(BF)
        for k, to in enumerate(OUTPUT_AT):
            early[to : to + OUTPUT_PIECE] = weight[k * OUTPUT_PIECE : (k + 1) * OUTPUT_PIECE]
        send_early()
        yield 1

    def spread(u):
        u.back = (bmix[u.at].astype(F32) * inverses[u.at]).astype(BF)
        product = u.back.astype(F32) * -bcont[u.at]
        left, right = [], []
        for g in range(HEADS // GROUP):
            part = product[:, group_lanes(g)]
            left.append(part + pltpu.roll(part, LANES - HEAD_DIM // 2, 1))
            right.append(part + pltpu.roll(part, HEAD_DIM // 2, 1))
        left, right = jnp.concatenate(left, axis=1), jnp.concatenate(right, axis=1)
        u.along = jnp.where(upper, right, left - left.astype(BF).astype(F32)).astype(BF)

    def widen(u):
        u.wide = []
        for g in range(HEADS // GROUP):
            rows_in = [
                jnp.concatenate([u.back[:, group_lanes(g)] * m, u.along[:, group_lanes(g)] * m], axis=1)
                for m in pair_masks
            ]
            u.wide.append(dot_t(jnp.concatenate(rows_in, axis=0), window_values(u, g)))

    def differentiate(u):
        u.low, u.grad_low = [], []
        for p in range(HEADS // 2):
            low = lows[u.pairs[p]]
            bs = low.astype(F32) * u.wide[p // 2][(p % 2) * SEG : (p % 2 + 1) * SEG]
            u.low.append(low)
            u.grad_low.append(bs.astype(BF))
            for q in range(2):
                head = 2 * p + q
                braw[u.at, head * LANES : (head + 1) * LANES] = unshift(
                    bs[:, q * LANES : (q + 1) * LANES], row_bits
                ).astype(BF)

    def by_head(pairs, g):
        return jnp.concatenate(
            [pairs[p][:, q * LANES : (q + 1) * LANES] for p in (2 * g, 2 * g + 1) for q in range(2)], axis=0
        )

    def collect_values(u):
        for g in range(HEADS // GROUP):
            lanes = group_lanes(g)
            vg = t_dot(by_head(u.low, g), stack_heads(u.back[:, lanes], head_masks)).astype(BF)
            vgm[u.at, lanes] = vg[0:SEG]
            vgs[u.at, lanes] = vg[SEG : 2 * SEG]

    def collect_keys(u):
        for g in range(HEADS // GROUP):
            lanes = group_lanes(g)
            kg = (t_dot(by_head(u.grad_low, g), stack_heads(content[u.at, lanes], head_masks)) * SCALING).astype(BF)
            kgm[u.at, lanes] = kg[0:SEG]
            kgs[u.at, lanes] = kg[SEG : 2 * SEG]

    def collect_queries(u):
        wide = dot(jnp.concatenate(u.grad_low, axis=0), window_keys(u))
        for g in range(HEADS // GROUP):
            lanes = group_lanes(g)
            bcont[u.at, lanes] = SCALING * jnp.where(
                first_pair, wide[2 * g * SEG : (2 * g + 1) * SEG, lanes], wide[(2 * g + 1) * SEG : (2 * g + 2) * SEG, lanes]
            )

    def attend_back(i):
        return staged(i, (spread, widen, differentiate, collect_values, collect_keys, collect_queries))

    def last(i):
        at = pl.ds(i * block, block)
        to = pl.ds(i * block + SEG, block)
        bplace = dot(braw[at], relblock[...]) * SCALING
        yield 1
        bc = bcont[at]
        vec[V_CONTENT : V_CONTENT + 1] += column_sum(bc)
        vec[V_POSITION : V_POSITION + 1] += column_sum(bplace)
        bq = (bc + bplace).astype(BF)
        bql[at] = bq
        yield 1
        bn = dot_t(bq, wq[...]) + dot_t(kgs[at], wk[...]) + dot_t(vgs[at], wv[...])
        yield 1
        bm = dot_t(kgm[at], wk[...]) + dot_t(vgm[at], wv[...])
        yield 1
        unit = xhat[to]
        vec[V_GAIN1 : V_GAIN1 + 1] += column_sum(bn * unit) + column_sum(bm * xhat[at])
        vec[V_SHIFT1 : V_SHIFT1 + 1] += column_sum(bn) + column_sum(bm)
        u = bn * gain1[...]
        inner = u - jnp.mean(u, axis=-1, keepdims=True) - unit * jnp.mean(u * unit, axis=-1, keepdims=True)
        dx[at] = (bhid[at] + inner * rstd[to]).astype(BF)
        send_rows(1, at)
        yield 1

    def attention_weights():
        segment_rows = nl[SEG : SEG + rows]
        memory_rows = nl[0:rows]
        late[QUERY_AT : QUERY_AT + FEATURES] = t_dot(segment_rows, bql[...]).astype(BF)
        yield 1
        late[KEY_AT : KEY_AT + FEATURES] = (t_dot(segment_rows, kgs[...]) + t_dot(memory_rows, kgm[...])).astype(BF)
        yield 1
        late[VALUE_AT : VALUE_AT + FEATURES] = (t_dot(segment_rows, vgs[...]) + t_dot(memory_rows, vgm[...])).astype(BF)
        yield 1
        for g in range(HEADS // GROUP):
            lanes = slice(g * LANES, (g + 1) * LANES)
            across = t_dot(placed[:, lanes], braw[:, g * GROUP * LANES : (g + 1) * GROUP * LANES])
            back = jnp.concatenate(
                [across[h * HEAD_DIM : (h + 1) * HEAD_DIM, h * LANES : (h + 1) * LANES] for h in range(GROUP)], axis=0
            ) * SCALING
            high = back.astype(BF)
            low = (back - high.astype(F32)).astype(BF)
            cosines = dot_t(basis[0:LANES], high) + (dot_t(basis[LANES:], high) + dot_t(basis[0:LANES], low))
            late[RELATIVE_AT : RELATIVE_AT + LANES, lanes] = cosines.astype(BF)
            yield 1

    phases = {
        "first": (8, first), "attend": (5 * block // SEG, attend), "feed": (14, feed), "back": (6 * block // SEG, attend_back), "last": (5, last),
    }
    for t in range(blocks + 4):
        if t == 2:
            wait_for(*LATER_COPIES)
        steps = []
        for lag, (count, phase) in enumerate(phases.values()):
            if 0 <= t - lag < blocks:
                steps.append((count, phase(t - lag)))
        if t == blocks + 2:
            steps.append((9, feed_weights()))
        if t == blocks + 3:
            pass
        interleave(*steps)
    interleave((5, attention_weights()))
    late[VECTOR_AT : VECTOR_AT + VECTOR_ROWS] = vec[...].astype(BF)
    late[VECTOR_AT + VECTOR_ROWS :] = jnp.zeros((2 * LATE_ROWS - VECTOR_AT - VECTOR_ROWS, FEATURES), BF)
    send_late()


def run_layer(horizon, x, start, arrived, cot, table, basis, params):
    rows = x.shape[0]
    operands = (x, start, arrived, cot, *params, table, basis)
    vmem = pl.BlockSpec(memory_space=pltpu.VMEM)
    hbm = pl.BlockSpec(memory_space=pltpu.HBM)
    padded = rows + SEG + LANES - 2 * SEG
    scratch = [
        pltpu.VMEM((rows + SEG, FEATURES), BF),
        pltpu.VMEM((rows + SEG, FEATURES), F32),
        pltpu.VMEM((rows + SEG, 1), F32),
        pltpu.VMEM((rows, FEATURES), BF),
        pltpu.VMEM((rows, FEATURES), BF),
        pltpu.VMEM((padded, FEATURES), BF),
        pltpu.VMEM((padded, FEATURES), BF),
        pltpu.VMEM((padded, 2 * FEATURES), BF),
        pltpu.VMEM((padded, 2 * FEATURES), BF),
        pltpu.VMEM((HEADS * LANES, FEATURES), BF),
        pltpu.VMEM((rows, HEADS * LANES), F32),
        pltpu.VMEM((rows * HEADS // 2, 2 * LANES), BF),
        pltpu.VMEM((rows, FEATURES), F32),
        pltpu.VMEM((rows, FEATURES), BF),
        pltpu.VMEM((rows, FEATURES), F32),
        pltpu.VMEM((rows, FEATURES), BF),
        pltpu.VMEM((rows, HIDDEN), BF),
        pltpu.VMEM((rows, HIDDEN), BF),
        pltpu.VMEM((rows, FEATURES), BF),
        pltpu.VMEM((rows, FEATURES), F32),
        pltpu.VMEM((rows, FEATURES), BF),
        pltpu.VMEM((rows, FEATURES), F32),
        pltpu.VMEM((rows, FEATURES), BF),
        pltpu.VMEM((rows, HEADS * LANES), BF),
        pltpu.VMEM((rows, FEATURES), BF),
        pltpu.VMEM((rows, FEATURES), BF),
        pltpu.VMEM((rows, FEATURES), BF),
        pltpu.VMEM((rows, FEATURES), BF),
        pltpu.VMEM((VECTOR_ROWS, FEATURES), F32),
    ]
    return pl.pallas_call(
        layer_kernel,
        out_shape=(
            jax.ShapeDtypeStruct((rows, FEATURES), BF),
            jax.ShapeDtypeStruct((rows, FEATURES), BF),
        )
        + (jax.ShapeDtypeStruct((PART_ROWS, FEATURES), BF),) * (2 * PIPES),
        in_specs=[hbm] * (COPIES + 1),
        out_specs=(hbm,) * (2 + 2 * PIPES),
        scratch_shapes=[pltpu.VMEM(a.shape, a.dtype) for a in operands]
        + [
            pltpu.SemaphoreType.DMA((COPIES + 1,)),
            pltpu.SemaphoreType.DMA((4 * (rows // SEG) + 2 * PIPES,)),
            pltpu.SemaphoreType.DMA((2 * PIPES + 2,)),
            pltpu.SMEM(horizon.shape, horizon.dtype),
            pltpu.VMEM((rows, FEATURES), BF),
            pltpu.VMEM((rows, FEATURES), BF),
            pltpu.VMEM((2 * sum(EARLY_ROWS), FEATURES), BF),
            pltpu.VMEM((2 * LATE_ROWS, FEATURES), BF),
        ]
        + scratch,
        compiler_params=pltpu.CompilerParams(vmem_limit_bytes=63 * 1024 * 1024),
        name="layer",
    )(horizon, *operands)


def join(own, other, whole):
    _, _, side = own_place()
    for k, part in ((side, own), (1 - side, other)):
        whole[pl.ds(pl.multiple_of(k * PART_ROWS, PART_ROWS), PART_ROWS)] = part[...]


BLOCKS = HIDDEN // FEATURES


def first_unpack_kernel(own, other, w1, w2, wo, whole, expand, shrink, output, sems):
    join(own, other, whole)
    moves = []

    def leave(source, target):
        moves.append(pltpu.make_async_copy(source, target, sems.at[len(moves)]))
        moves[-1].start()

    for f in range(BLOCKS - 1):
        cols = slice(f * FEATURES, (f + 1) * FEATURES)
        expand[f] = whole[f * FEATURES : (f + 1) * FEATURES].astype(F32)
        leave(expand.at[f], w1.at[:, cols])
        shrink[f] = whole[PART_ROWS + f * FEATURES : PART_ROWS + (f + 1) * FEATURES].astype(F32)
        leave(shrink.at[f], w2.at[cols])
    for k in range(2):
        end = (k + 1) * PART_ROWS
        output[k] = whole[end - OUTPUT_PIECE : end].astype(F32)
        leave(output.at[k], wo.at[k * OUTPUT_PIECE : (k + 1) * OUTPUT_PIECE])
    for move in moves:
        move.wait()


def second_unpack_kernel(
    w1_old, w2_old, wo_old, own, other, turned,
    w1, w2, wo, wq, wk, wv, wr, gain1, shift1, cbias, pbias, gain2, shift2, b1, b2,
    whole, expand, shrink, output, sems,
):
    join(own, other, whole)
    moves = []

    def leave(source, target):
        moves.append(pltpu.make_async_copy(source, target, sems.at[len(moves)]))
        moves[-1].start()

    cols = slice(HIDDEN - FEATURES, HIDDEN)
    expand[...] = whole[0:FEATURES].astype(F32)
    leave(expand, w1.at[:, cols])
    shrink[...] = whole[PART_ROWS : PART_ROWS + FEATURES].astype(F32)
    leave(shrink, w2.at[cols])
    for k in range(2):
        start = k * PART_ROWS + FEATURES
        output[k] = whole[start : start + OUTPUT_PIECE].astype(F32)
        leave(output.at[k], wo.at[(k + 2) * OUTPUT_PIECE : (k + 3) * OUTPUT_PIECE])

    def late(at, count):
        at += EARLY_ROWS[1] if at < LATE_ROWS else EARLY_ROWS[1] + PART_ROWS - LATE_ROWS
        return whole[at : at + count]

    for ref, at in ((wq, QUERY_AT), (wk, KEY_AT), (wv, VALUE_AT)):
        ref[...] = late(at, FEATURES).astype(F32)
    cosines = late(RELATIVE_AT, LANES)
    wr[...] = t_dot(turned[0:LANES], cosines) + t_dot(turned[LANES:], cosines)
    vectors = late(VECTOR_AT, VECTOR_ROWS).astype(F32)
    for ref, at in (
        (cbias, V_CONTENT), (pbias, V_POSITION), (gain1, V_GAIN1), (shift1, V_SHIFT1),
        (gain2, V_GAIN2), (shift2, V_SHIFT2), (b2, V_SHRINK),
    ):
        ref[...] = vectors[at]
    for f in range(BLOCKS):
        b1[f * FEATURES : (f + 1) * FEATURES] = vectors[V_EXPAND + f]
    for move in moves:
        move.wait()


def unpack_all(parts, turned):
    vmem = pl.BlockSpec(memory_space=pltpu.VMEM)
    hbm = pl.BlockSpec(memory_space=pl.ANY)
    square, vector = (FEATURES, FEATURES), (FEATURES,)
    split = ((FEATURES, HIDDEN), (HIDDEN, FEATURES), square)
    rest = (square,) * 4 + (vector,) * 6 + ((HIDDEN,), vector)

    def pieces(count):
        lead = (count,) if count > 1 else ()
        return [
            pltpu.VMEM((2 * PART_ROWS, FEATURES), BF),
            pltpu.VMEM((*lead, *square), F32),
            pltpu.VMEM((*lead, *square), F32),
            pltpu.VMEM((2, OUTPUT_PIECE, FEATURES), F32),
            pltpu.SemaphoreType.DMA((2 * count + 2,)),
        ]

    def shapes(dims):
        return tuple(jax.ShapeDtypeStruct(shape, F32) for shape in dims)

    params = pltpu.CompilerParams(vmem_limit_bytes=32 * 1024 * 1024)
    begun = pl.pallas_call(
        first_unpack_kernel,
        out_shape=shapes(split),
        in_specs=[vmem, vmem],
        out_specs=(hbm,) * 3,
        scratch_shapes=pieces(BLOCKS - 1),
        compiler_params=params,
        name="unpack_first",
    )(*parts[:2])
    w1, w2, wo, wq, wk, wv, wr, gain1, shift1, cbias, pbias, gain2, shift2, b1, b2 = pl.pallas_call(
        second_unpack_kernel,
        out_shape=shapes(split + rest),
        in_specs=[hbm] * 3 + [vmem] * 3,
        out_specs=(hbm,) * 3 + (vmem,) * len(rest),
        scratch_shapes=pieces(1),
        input_output_aliases={0: 0, 1: 1, 2: 2},
        compiler_params=params,
        name="unpack_second",
    )(*begun, *parts[2:], turned)
    return gain1, shift1, wq, wk, wv, wr, cbias, pbias, wo, gain2, shift2, w1, b1, w2, b2


AXES = ("tm", "roll")


def exchange_plan(roll_count, tm_count):
    tm_bits = tm_count.bit_length() - 1
    roll_bits = roll_count.bit_length() - 1
    high = [roll_bits + b for b in range(1, tm_bits)]
    rolls = list(range(roll_bits))
    even = high + rolls
    odd = rolls[:1] + high + rolls[1:]
    return roll_bits, list(zip(even, odd))


def side_of(device):
    return bin(device).count("1") & 1


def swap_cores(value, core, count):
    return lax.ppermute(value, AXES, [(d, d ^ (1 << core)) for d in range(count)])


def swap(value, bits, core, count):
    return lax.ppermute(value, AXES, [(d, d ^ (1 << bits[side_of(d)]) ^ (1 << core)) for d in range(count)])


def add_low(a, b):
    return (a.astype(F32) + b.astype(F32)).astype(BF)


def sum_everywhere(halves, me, side):
    roll_count, tm_count = lax.axis_size("roll"), lax.axis_size("tm")
    count = roll_count * tm_count
    core, stages = exchange_plan(roll_count, tm_count)
    halving = 3

    def chain(kept, sent):
        got = swap_cores(sent, core, count)
        firsts = []
        for number, bits in enumerate(stages[:halving]):
            bit = jnp.where(side == 0, (me >> bits[0]) & 1, (me >> bits[1]) & 1)
            half = kept.shape[0] // 2

            def cut(value, which):
                return lax.dynamic_slice_in_dim(value, which * half, half, 0)

            leaving, staying = cut(kept, 1 - bit), cut(kept, bit)
            if number == 0:
                leaving, staying = lax.optimization_barrier((leaving, staying))
            sent = add_low(leaving, cut(got, 1 - bit))
            kept = add_low(staying, cut(got, bit))
            got = swap(sent, bits, core, count)
            firsts.append(bit == 0)
        buffer = add_low(kept, got)
        for bits in stages[halving:]:
            buffer = add_low(buffer, swap(buffer, bits, core, count))
        for bits, first in list(zip(stages, firsts))[::-1]:
            other = swap(buffer, bits, core, count)
            buffer = jnp.concatenate([jnp.where(first, buffer, other), jnp.where(first, other, buffer)], axis=0)
        return [buffer, swap_cores(buffer, core, count)]

    return sum([chain(*halves[2 * p : 2 * p + 2]) for p in range(PIPES)], [])


def body(
    layer_input, start_memory, horizon, cotangent, first_gain, first_shift, query_projection_weight,
    key_projection_weight, value_projection_weight, relative_weight, content_bias, position_bias,
    output_weight, second_gain, second_shift, expand_weight, expand_bias, shrink_weight, shrink_bias,
):
    rollouts, columns, features = layer_input.shape
    x = layer_input.reshape(rollouts * columns, features)
    tm_count = lax.axis_size("tm")
    arrived = lax.ppermute(x[-SEG:], "tm", [(i, (i + 1) % tm_count) for i in range(tm_count)])
    _, me, side = own_place()
    table = jnp.asarray(position_rows())
    basis, turned = (jnp.asarray(part) for part in relative_basis())

    def row(v):
        return v.reshape(1, -1)

    params = (
        row(first_gain), row(first_shift), query_projection_weight, key_projection_weight,
        value_projection_weight, relative_weight, row(content_bias), row(position_bias), output_weight,
        row(second_gain), row(second_shift), expand_weight, row(expand_bias), shrink_weight, row(shrink_bias),
    )
    out, dx, *halves = run_layer(
        horizon, x, start_memory.reshape(SEG, features), arrived,
        cotangent.reshape(rollouts * columns, features), table, basis, params,
    )
    summed = unpack_all(sum_everywhere(halves, me, side), turned)
    return (out.reshape(layer_input.shape), dx.reshape(layer_input.shape)) + tuple(summed)


def solution(mesh):
    in_specs = (
        P("roll", "tm", None), P("roll", None, None), P("roll", None), P("roll", "tm", None),
    ) + (P(),) * 15
    out_specs = (P("roll", "tm", None), P("roll", "tm", None)) + (P(),) * 15
    return jax.shard_map(body, mesh=mesh, in_specs=in_specs, out_specs=out_specs, check_vma=False)
```

time: 74.2 us -> 68.8 us (0.927)
  Pallas kernels: 26 us -> 22.9 us
  other arithmetic: 2.41 us -> 0.81 us
  waiting for transfers between devices: 14.4 us -> 13 us
  local copies, waits for them, and re-layouts: 1.48 us -> 2.66 us
    pallas_call x1, Pallas kernels: 23.4 us -> 19.5 us  [run_layer(): pl.pallas_call(layer_kernel, out_shape=(jax.ShapeDtypeStruct((rows, FEATU...]
    ppermute x4, waiting for transfers between devices: 3.13 us -> 0.48 us  [swap_cores(): return lax.ppermute(value, AXES, [(d, d ^ 1 << core) for d in range(count)])]
    dynamic_slice x6 -> x1, local copies, waits for them, and re-layouts: 0.11 us -> 1.3 us  [cut(): return lax.dynamic_slice_in_dim(value, which * half, half, 0)]
    convert_element_type x10, other arithmetic: 1.45 us -> 0.43 us  [add_low(): return (a.astype(F32) + b.astype(F32)).astype(BF)]
    pallas_call x1 -> x2, Pallas kernels: 2.55 us -> 3.39 us  [the longest x1 2.06 us: unpack_all(): pl.pallas_call(second_unpack_kernel, out_shape=shapes(split + rest), in_s...]
  transfers between devices with their start and end apart: 19 -> 19, of which waited for: 12 -> 12; matrix products, arithmetic and copies ran while one was open for 3% -> 3% of each run, Pallas kernels for 0% -> 2%
where the time goes in v4:
time: 68.8 us; the launch traced here: 68.6 us
  starting transfers between devices  28.2 us (41%)
  Pallas kernels  22.9 us (33%)
  waiting for transfers between devices  13 us (19%)
  local copies, waits for them, and re-layouts  2.66 us (4%)
  between operations  0.97 us (1%)
  other arithmetic  0.81 us (1%)
    ppermute x14, starting transfers between devices, swap(): lax.ppermute(value, AXES, [(d, d ^ 1 << bits[side_of(d)] ^ 1 << core) for...  26.9 us
    pallas_call x1, Pallas kernels, run_layer(): pl.pallas_call(layer_kernel, out_shape=(jax.ShapeDtypeStruct((rows, FEATU...  19.5 us
    ppermute x14, waiting for transfers between devices, swap(): lax.ppermute(value, AXES, [(d, d ^ 1 << bits[side_of(d)] ^ 1 << core) for...  9.03 us
    ppermute x1, waiting for transfers between devices, body(): lax.ppermute(x[-SEG:], 'tm', [(i, (i + 1) % tm_count) for i in range(tm_c...  3.46 us
    pallas_call x1, Pallas kernels, unpack_all(): pl.pallas_call(second_unpack_kernel, out_shape=shapes(split + rest), in_s...  2.06 us
  transfers between devices with their start and end apart: 19, of which 12 were waited for; matrix products, arithmetic and copies ran while one was open for 3% of the time, Pallas kernels for 2%

profile of v4, /device:TPU:0, one launch (start us, length us, event | category | flops | bytes accessed | tf_op | source)
XLA Modules:
  0.0 68.6 jit_solution(4942922827711437379)
XLA Ops:
  0.7 0.7 %slice_bitcast_fusion = bf16[48,256]{1,0:T(8,128)(2,1)S(1)} fusion(bf16[1,768,256]{2,1,0:T(8,128)(2,1)} %param.22), kind=kLoop, calls=%fused_computation.34 | loop fusion | bytes 49152 | tf_op jit(solution)/shard_map/slice | solution.py:775
  1.4 0.5 collective-permute-start
  1.9 3.5 %collective-permute-done.refs_2_ = bf16[48,256]{1,0:T(8,128)(2,1)S(1)} collective-permute-done((bf16[48,256]{1,0:T(8,128)(2,1)S(1)}, bf16[48,256]{1,0:T(8,128)(2,1)S(1)}, u32[]{:S(2)}, u32[]{:S(2)}) %collective-permute-start) | collective-permute-done | bytes 24608 | tf_op jit(solution)/shard_map/ppermute | solution.py:775
  5.3 0.0 copy-start.1
  5.3 0.6 copy-done.1
  5.9 19.5 %layer.1 = (bf16[768,256]{1,0:T(8,128)(2,1)}, bf16[768,256]{1,0:T(8,128)(2,1)}, bf16[832,256]{1,0:T(8,128)(2,1)}, bf16[832,256]{1,0:T(8,128)(2,1)}, bf16[832,256]{1,0:T(8,128)(2,1)}, /*index=5*/bf16[832,256]{1,0:T(8,128)(2,1)}) custom-call(s32[1,64]{1,0:T(1,128)} %horizon_source.1, bf16[768,256]{1,0:T(8,128)(2,1)} %bitcast.15, bf16[48,256]{1,0:T(8,128)(2,1)} %bitcast.17, ...), custom_call_target="tpu_custom_call" | custom-call | tf_op jit(solution)/shard_map/layer/pallas_call | solution.py:562
  25.5 0.2 collective-permute-start.1
  25.6 0.4 collective-permute-start.10
  26.0 1.3 %constant_dynamic-slice_fusion = (bf16[416,256]{1,0:T(8,128)(2,1)S(1)}, bf16[416,256]{1,0:T(8,128)(2,1)S(1)}, bf16[416,256]{1,0:T(8,128)(2,1)S(1)}, bf16[416,256]{1,0:T(8,128)(2,1)S(1)}) fusion(bf16[832,256]{1,0:T(8,128)(2,1)} %get-tuple-element.54, s32[]{:T(128)S(6)} %select_n.113, s32[]{:T(128)S(6)} %select_n.112, bf16[832,256]{1,0:T(8,128)(2,1)} %get-tuple-element.47), kind=kLoop, calls=%fused_computation.35 | loop fusion | bytes 1703944 | tf_op jit(solution)/shard_map/dynamic_slice | solution.py:747
  27.3 0.2 collective-permute-done.1
  27.5 0.1 add_convert_fusion.3
  27.6 2.1 %collective-permute-start.2 = (bf16[416,256]{1,0:T(8,128)(2,1)S(1)}, bf16[416,256]{1,0:T(8,128)(2,1)S(1)}, u32[]{:S(2)}, u32[]{:S(2)}) collective-permute-start(bf16[416,256]{1,0:T(8,128)(2,1)S(1)} %get-tuple-element.86), channel_id=1, source_target_pairs={{0,24},{1,8},{2,11},{3,27},{4,13},{5,29},{6,30},{7,14},{8,1},{9,17... | collective-permute-start | bytes 638984 | tf_op jit(solution)/shard_map/ppermute | solution.py:726
  29.7 0.0 collective-permute-done.10
  29.7 0.1 add_convert_fusion.1
  29.8 0.5 collective-permute-start.11
  30.3 2.9 %collective-permute-done.2 = bf16[416,256]{1,0:T(8,128)(2,1)S(1)} collective-permute-done((bf16[416,256]{1,0:T(8,128)(2,1)S(1)}, bf16[416,256]{1,0:T(8,128)(2,1)S(1)}, u32[]{:S(2)}, u32[]{:S(2)}) %collective-permute-start.2) | collective-permute-done | bytes 213024 | tf_op jit(solution)/shard_map/ppermute | solution.py:726
  33.3 0.1 add_convert_fusion.7
  33.3 2.1 %collective-permute-start.3 = (bf16[208,256]{1,0:T(8,128)(2,1)S(1)}, bf16[208,256]{1,0:T(8,128)(2,1)S(1)}, u32[]{:S(2)}, u32[]{:S(2)}) collective-permute-start(bf16[208,256]{1,0:T(8,128)(2,1)S(1)} %get-tuple-element.84), channel_id=1, source_target_pairs={{0,9},{1,25},{2,26},{3,10},{4,28},{5,12},{6,15},{7,31},{8,16},{9,0... | collective-permute-start | bytes 319496 | tf_op jit(solution)/shard_map/ppermute | solution.py:726
  35.4 0.1 collective-permute-done.11
  35.5 0.1 add_convert_fusion.5
  35.6 1.8 %collective-permute-start.12 = (bf16[208,256]{1,0:T(8,128)(2,1)S(1)}, bf16[208,256]{1,0:T(8,128)(2,1)S(1)}, u32[]{:S(2)}, u32[]{:S(2)}) collective-permute-start(bf16[208,256]{1,0:T(8,128)(2,1)S(1)} %get-tuple-element.76), channel_id=1, source_target_pairs={{0,9},{1,25},{2,26},{3,10},{4,28},{5,12},{6,15},{7,31},{8,16},{9,0... | collective-permute-start | bytes 319496 | tf_op jit(solution)/shard_map/ppermute | solution.py:726
  37.4 0.4 collective-permute-done.3
  37.8 1.9 %collective-permute-start.4 = (bf16[104,256]{1,0:T(8,128)(2,1)S(1)}, bf16[104,256]{1,0:T(8,128)(2,1)S(1)}, u32[]{:S(2)}, u32[]{:S(2)}) collective-permute-start(bf16[104,256]{1,0:T(8,128)(2,1)S(1)} %add_convert_fusion.14), channel_id=1, source_target_pairs={{0,10},{1,11},{2,8},{3,9},{4,14},{5,15},{6,12},{7,13},{8,2},{9,3},... | collective-permute-start | bytes 159752 | tf_op jit(solution)/shard_map/ppermute | solution.py:726
  39.7 0.1 collective-permute-done.12
  39.8 1.9 %collective-permute-start.13 = (bf16[104,256]{1,0:T(8,128)(2,1)S(1)}, bf16[104,256]{1,0:T(8,128)(2,1)S(1)}, u32[]{:S(2)}, u32[]{:S(2)}) collective-permute-start(bf16[104,256]{1,0:T(8,128)(2,1)S(1)} %add_convert_fusion.10), channel_id=1, source_target_pairs={{0,10},{1,11},{2,8},{3,9},{4,14},{5,15},{6,12},{7,13},{8,2},{9,3},... | collective-permute-start | bytes 159752 | tf_op jit(solution)/shard_map/ppermute | solution.py:726
  41.7 0.0 collective-permute-done.4
  41.7 2.7 %collective-permute-start.5 = (bf16[104,256]{1,0:T(8,128)(2,1)S(1)}, bf16[104,256]{1,0:T(8,128)(2,1)S(1)}, u32[]{:S(2)}, u32[]{:S(2)}) collective-permute-start(bf16[104,256]{1,0:T(8,128)(2,1)S(1)} %add_convert_fusion.13), channel_id=1, source_target_pairs={{0,12},{1,13},{2,14},{3,15},{4,8},{5,9},{6,10},{7,11},{8,4},{9,5},... | collective-permute-start | bytes 159752 | tf_op jit(solution)/shard_map/ppermute | solution.py:726
  44.4 0.0 collective-permute-done.13
  44.4 2.2 %collective-permute-start.14 = (bf16[104,256]{1,0:T(8,128)(2,1)S(1)}, bf16[104,256]{1,0:T(8,128)(2,1)S(1)}, u32[]{:S(2)}, u32[]{:S(2)}) collective-permute-start(bf16[104,256]{1,0:T(8,128)(2,1)S(1)} %add_convert_fusion.9), channel_id=1, source_target_pairs={{0,12},{1,13},{2,14},{3,15},{4,8},{5,9},{6,10},{7,11},{8,4},{9,5},... | collective-permute-start | bytes 159752 | tf_op jit(solution)/shard_map/ppermute | solution.py:726
  46.6 0.0 collective-permute-done.5
  46.6 1.7 %collective-permute-start.6 = (bf16[104,256]{1,0:T(8,128)(2,1)S(1)}, bf16[104,256]{1,0:T(8,128)(2,1)S(1)}, u32[]{:S(2)}, u32[]{:S(2)}) collective-permute-start(bf16[104,256]{1,0:T(8,128)(2,1)S(1)} %add_convert_fusion.12), channel_id=1, source_target_pairs={{0,10},{1,11},{2,8},{3,9},{4,14},{5,15},{6,12},{7,13},{8,2},{9,3},... | collective-permute-start | bytes 159752 | tf_op jit(solution)/shard_map/ppermute | solution.py:726
  48.4 0.9 %collective-permute-done.14 = bf16[104,256]{1,0:T(8,128)(2,1)S(1)} collective-permute-done((bf16[104,256]{1,0:T(8,128)(2,1)S(1)}, bf16[104,256]{1,0:T(8,128)(2,1)S(1)}, u32[]{:S(2)}, u32[]{:S(2)}) %collective-permute-start.14) | collective-permute-done | bytes 53280 | tf_op jit(solution)/shard_map/ppermute | solution.py:726
  49.3 1.6 %collective-permute-start.15 = (bf16[104,256]{1,0:T(8,128)(2,1)S(1)}, bf16[104,256]{1,0:T(8,128)(2,1)S(1)}, u32[]{:S(2)}, u32[]{:S(2)}) collective-permute-start(bf16[104,256]{1,0:T(8,128)(2,1)S(1)} %add_convert_fusion.8), channel_id=1, source_target_pairs={{0,10},{1,11},{2,8},{3,9},{4,14},{5,15},{6,12},{7,13},{8,2},{9,3},... | collective-permute-start | bytes 159752 | tf_op jit(solution)/shard_map/ppermute | solution.py:726
  50.9 0.0 collective-permute-done.6
  50.9 1.7 %collective-permute-start.7 = (bf16[208,256]{1,0:T(8,128)(2,1)S(1)}, bf16[208,256]{1,0:T(8,128)(2,1)S(1)}, u32[]{:S(2)}, u32[]{:S(2)}) collective-permute-start(bf16[208,256]{1,0:T(8,128)(2,1)S(1)} %pad_maximum_fusion.4), channel_id=1, source_target_pairs={{0,9},{1,25},{2,26},{3,10},{4,28},{5,12},{6,15},{7,31},{8,16},{9,0... | collective-permute-start | bytes 319496 | tf_op jit(solution)/shard_map/ppermute | solution.py:726
  52.6 0.3 collective-permute-done.15
  52.9 2.7 %collective-permute-start.16 = (bf16[208,256]{1,0:T(8,128)(2,1)S(1)}, bf16[208,256]{1,0:T(8,128)(2,1)S(1)}, u32[]{:S(2)}, u32[]{:S(2)}) collective-permute-start(bf16[208,256]{1,0:T(8,128)(2,1)S(1)} %pad_maximum_fusion.5), channel_id=1, source_target_pairs={{0,9},{1,25},{2,26},{3,10},{4,28},{5,12},{6,15},{7,31},{8,16},{9,0... | collective-permute-start | bytes 319496 | tf_op jit(solution)/shard_map/ppermute | solution.py:726
  55.6 0.0 collective-permute-done.7
  55.7 1.2 %collective-permute-start.8 = (bf16[416,256]{1,0:T(8,128)(2,1)S(1)}, bf16[416,256]{1,0:T(8,128)(2,1)S(1)}, u32[]{:S(2)}, u32[]{:S(2)}) collective-permute-start(bf16[416,256]{1,0:T(8,128)(2,1)S(1)} %pad_maximum_fusion.2), channel_id=1, source_target_pairs={{0,24},{1,8},{2,11},{3,27},{4,13},{5,29},{6,30},{7,14},{8,1},{9,17... | collective-permute-start | bytes 638984 | tf_op jit(solution)/shard_map/ppermute | solution.py:726
  56.9 1.1 %collective-permute-done.16 = bf16[208,256]{1,0:T(8,128)(2,1)S(1)} collective-permute-done((bf16[208,256]{1,0:T(8,128)(2,1)S(1)}, bf16[208,256]{1,0:T(8,128)(2,1)S(1)}, u32[]{:S(2)}, u32[]{:S(2)}) %collective-permute-start.16) | collective-permute-done | bytes 106528 | tf_op jit(solution)/shard_map/ppermute | solution.py:726
  58.1 2.8 %collective-permute-start.17 = (bf16[416,256]{1,0:T(8,128)(2,1)S(1)}, bf16[416,256]{1,0:T(8,128)(2,1)S(1)}, u32[]{:S(2)}, u32[]{:S(2)}) collective-permute-start(bf16[416,256]{1,0:T(8,128)(2,1)S(1)} %pad_maximum_fusion.3), channel_id=1, source_target_pairs={{0,24},{1,8},{2,11},{3,27},{4,13},{5,29},{6,30},{7,14},{8,1},{9,17... | collective-permute-start | bytes 638984 | tf_op jit(solution)/shard_map/ppermute | solution.py:726
  60.9 0.3 collective-permute-done.8
  61.1 0.1 broadcast_select_fusion.3
  61.2 0.2 collective-permute-start.9
  61.4 3.0 %collective-permute-done.17 = bf16[416,256]{1,0:T(8,128)(2,1)S(1)} collective-permute-done((bf16[416,256]{1,0:T(8,128)(2,1)S(1)}, bf16[416,256]{1,0:T(8,128)(2,1)S(1)}, u32[]{:S(2)}, u32[]{:S(2)}) %collective-permute-start.17) | collective-permute-done | bytes 213024 | tf_op jit(solution)/shard_map/ppermute | solution.py:726
  64.4 0.1 broadcast_select_fusion.1
  64.5 0.0 copy-start
  64.5 0.2 collective-permute-start.18
  64.7 0.0 collective-permute-done.9.other
  64.7 1.3 %unpack_first.1 = (f32[256,1024]{1,0:T(8,128)}, f32[1024,256]{1,0:T(8,128)}, f32[256,256]{1,0:T(8,128)}) custom-call(bf16[832,256]{1,0:T(8,128)(2,1)S(1)} %pad_maximum_fusion.own, bf16[832,256]{1,0:T(8,128)(2,1)S(1)} %collective-permute-done.9.other), custom_call_target="tpu_custom_call" | custom-call | tf_op jit(solution)/shard_map/unpack_first/pallas_call | solution.py:682
  66.1 0.3 collective-permute-done.18.other
  66.4 0.0 copy-done
  66.4 2.1 %unpack_second.1 = (f32[256,1024]{1,0:T(8,128)}, f32[1024,256]{1,0:T(8,128)}, f32[256,256]{1,0:T(8,128)}, f32[256,256]{1,0:T(8,128)}, f32[256,256]{1,0:T(8,128)}...) custom-call(f32[256,1024]{1,0:T(8,128)} %get-tuple-element.51.w1_old, ...), custom_call_target="tpu_custom_call", output_to_operand_aliasing={{0}: (0, {}), {1}: (1, {}), {2}: (2, {})} | custom-call | tf_op jit(solution)/shard_map/unpack_second/pallas_call | solution.py:691
  (16 shorter events, 0.3 us)
Async XLA Ops:
  1.4 3.9 %collective-permute-start = (bf16[48,256]{1,0:T(8,128)(2,1)S(1)}, bf16[48,256]{1,0:T(8,128)(2,1)S(1)}, u32[]{:S(2)}, u32[]{:S(2)}) collective-permute-start(bf16[48,256]{1,0:T(8,128)(2,1)S(1)} %slice_bitcast_fusion), channel_id=1, source_target_pairs={{0,8},{8,16},{16,24},{24,0},{1,9},{9,17},{17,25},{25,1},{2,10},{10... | collective-permute-start | bytes 73736 | tf_op jit(solution)/shard_map/ppermute | solution.py:775
  5.3 0.6 copy-start.1
  25.5 2.0 %collective-permute-start.1 = (bf16[832,256]{1,0:T(8,128)(2,1)}, bf16[832,256]{1,0:T(8,128)(2,1)S(1)}, u32[]{:S(2)}, u32[]{:S(2)}) collective-permute-start(bf16[832,256]{1,0:T(8,128)(2,1)} %get-tuple-element.49), channel_id=1, source_target_pairs={{0,8},{1,9},{2,10},{3,11},{4,12},{5,13},{6,14},{7,15},{8,0},{9,1},... | collective-permute-start | bytes 1277960 | tf_op jit(solution)/shard_map/ppermute | solution.py:722
  25.6 4.1 %collective-permute-start.10 = (bf16[832,256]{1,0:T(8,128)(2,1)}, bf16[832,256]{1,0:T(8,128)(2,1)S(1)}, u32[]{:S(2)}, u32[]{:S(2)}) collective-permute-start(bf16[832,256]{1,0:T(8,128)(2,1)} %get-tuple-element.56), channel_id=1, source_target_pairs={{0,8},{1,9},{2,10},{3,11},{4,12},{5,13},{6,14},{7,15},{8,0},{9,1},... | collective-permute-start | bytes 1277960 | tf_op jit(solution)/shard_map/ppermute | solution.py:722
  27.6 5.6 %collective-permute-start.2 = (bf16[416,256]{1,0:T(8,128)(2,1)S(1)}, bf16[416,256]{1,0:T(8,128)(2,1)S(1)}, u32[]{:S(2)}, u32[]{:S(2)}) collective-permute-start(bf16[416,256]{1,0:T(8,128)(2,1)S(1)} %get-tuple-element.86), channel_id=1, source_target_pairs={{0,24},{1,8},{2,11},{3,27},{4,13},{5,29},{6,30},{7,14},{8,1},{9,17... | collective-permute-start | bytes 638984 | tf_op jit(solution)/shard_map/ppermute | solution.py:726
  29.8 5.7 %collective-permute-start.11 = (bf16[416,256]{1,0:T(8,128)(2,1)S(1)}, bf16[416,256]{1,0:T(8,128)(2,1)S(1)}, u32[]{:S(2)}, u32[]{:S(2)}) collective-permute-start(bf16[416,256]{1,0:T(8,128)(2,1)S(1)} %get-tuple-element.78), channel_id=1, source_target_pairs={{0,24},{1,8},{2,11},{3,27},{4,13},{5,29},{6,30},{7,14},{8,1},{9,17... | collective-permute-start | bytes 638984 | tf_op jit(solution)/shard_map/ppermute | solution.py:726
  33.3 4.5 %collective-permute-start.3 = (bf16[208,256]{1,0:T(8,128)(2,1)S(1)}, bf16[208,256]{1,0:T(8,128)(2,1)S(1)}, u32[]{:S(2)}, u32[]{:S(2)}) collective-permute-start(bf16[208,256]{1,0:T(8,128)(2,1)S(1)} %get-tuple-element.84), channel_id=1, source_target_pairs={{0,9},{1,25},{2,26},{3,10},{4,28},{5,12},{6,15},{7,31},{8,16},{9,0... | collective-permute-start | bytes 319496 | tf_op jit(solution)/shard_map/ppermute | solution.py:726
  35.6 4.2 %collective-permute-start.12 = (bf16[208,256]{1,0:T(8,128)(2,1)S(1)}, bf16[208,256]{1,0:T(8,128)(2,1)S(1)}, u32[]{:S(2)}, u32[]{:S(2)}) collective-permute-start(bf16[208,256]{1,0:T(8,128)(2,1)S(1)} %get-tuple-element.76), channel_id=1, source_target_pairs={{0,9},{1,25},{2,26},{3,10},{4,28},{5,12},{6,15},{7,31},{8,16},{9,0... | collective-permute-start | bytes 319496 | tf_op jit(solution)/shard_map/ppermute | solution.py:726
  37.8 3.9 %collective-permute-start.4 = (bf16[104,256]{1,0:T(8,128)(2,1)S(1)}, bf16[104,256]{1,0:T(8,128)(2,1)S(1)}, u32[]{:S(2)}, u32[]{:S(2)}) collective-permute-start(bf16[104,256]{1,0:T(8,128)(2,1)S(1)} %add_convert_fusion.14), channel_id=1, source_target_pairs={{0,10},{1,11},{2,8},{3,9},{4,14},{5,15},{6,12},{7,13},{8,2},{9,3},... | collective-permute-start | bytes 159752 | tf_op jit(solution)/shard_map/ppermute | solution.py:726
  39.8 4.6 %collective-permute-start.13 = (bf16[104,256]{1,0:T(8,128)(2,1)S(1)}, bf16[104,256]{1,0:T(8,128)(2,1)S(1)}, u32[]{:S(2)}, u32[]{:S(2)}) collective-permute-start(bf16[104,256]{1,0:T(8,128)(2,1)S(1)} %add_convert_fusion.10), channel_id=1, source_target_pairs={{0,10},{1,11},{2,8},{3,9},{4,14},{5,15},{6,12},{7,13},{8,2},{9,3},... | collective-permute-start | bytes 159752 | tf_op jit(solution)/shard_map/ppermute | solution.py:726
  41.7 4.9 %collective-permute-start.5 = (bf16[104,256]{1,0:T(8,128)(2,1)S(1)}, bf16[104,256]{1,0:T(8,128)(2,1)S(1)}, u32[]{:S(2)}, u32[]{:S(2)}) collective-permute-start(bf16[104,256]{1,0:T(8,128)(2,1)S(1)} %add_convert_fusion.13), channel_id=1, source_target_pairs={{0,12},{1,13},{2,14},{3,15},{4,8},{5,9},{6,10},{7,11},{8,4},{9,5},... | collective-permute-start | bytes 159752 | tf_op jit(solution)/shard_map/ppermute | solution.py:726
  44.4 4.8 %collective-permute-start.14 = (bf16[104,256]{1,0:T(8,128)(2,1)S(1)}, bf16[104,256]{1,0:T(8,128)(2,1)S(1)}, u32[]{:S(2)}, u32[]{:S(2)}) collective-permute-start(bf16[104,256]{1,0:T(8,128)(2,1)S(1)} %add_convert_fusion.9), channel_id=1, source_target_pairs={{0,12},{1,13},{2,14},{3,15},{4,8},{5,9},{6,10},{7,11},{8,4},{9,5},... | collective-permute-start | bytes 159752 | tf_op jit(solution)/shard_map/ppermute | solution.py:726
  46.6 4.3 %collective-permute-start.6 = (bf16[104,256]{1,0:T(8,128)(2,1)S(1)}, bf16[104,256]{1,0:T(8,128)(2,1)S(1)}, u32[]{:S(2)}, u32[]{:S(2)}) collective-permute-start(bf16[104,256]{1,0:T(8,128)(2,1)S(1)} %add_convert_fusion.12), channel_id=1, source_target_pairs={{0,10},{1,11},{2,8},{3,9},{4,14},{5,15},{6,12},{7,13},{8,2},{9,3},... | collective-permute-start | bytes 159752 | tf_op jit(solution)/shard_map/ppermute | solution.py:726
  49.3 3.6 %collective-permute-start.15 = (bf16[104,256]{1,0:T(8,128)(2,1)S(1)}, bf16[104,256]{1,0:T(8,128)(2,1)S(1)}, u32[]{:S(2)}, u32[]{:S(2)}) collective-permute-start(bf16[104,256]{1,0:T(8,128)(2,1)S(1)} %add_convert_fusion.8), channel_id=1, source_target_pairs={{0,10},{1,11},{2,8},{3,9},{4,14},{5,15},{6,12},{7,13},{8,2},{9,3},... | collective-permute-start | bytes 159752 | tf_op jit(solution)/shard_map/ppermute | solution.py:726
  50.9 4.7 %collective-permute-start.7 = (bf16[208,256]{1,0:T(8,128)(2,1)S(1)}, bf16[208,256]{1,0:T(8,128)(2,1)S(1)}, u32[]{:S(2)}, u32[]{:S(2)}) collective-permute-start(bf16[208,256]{1,0:T(8,128)(2,1)S(1)} %pad_maximum_fusion.4), channel_id=1, source_target_pairs={{0,9},{1,25},{2,26},{3,10},{4,28},{5,12},{6,15},{7,31},{8,16},{9,0... | collective-permute-start | bytes 319496 | tf_op jit(solution)/shard_map/ppermute | solution.py:726
  52.9 5.1 %collective-permute-start.16 = (bf16[208,256]{1,0:T(8,128)(2,1)S(1)}, bf16[208,256]{1,0:T(8,128)(2,1)S(1)}, u32[]{:S(2)}, u32[]{:S(2)}) collective-permute-start(bf16[208,256]{1,0:T(8,128)(2,1)S(1)} %pad_maximum_fusion.5), channel_id=1, source_target_pairs={{0,9},{1,25},{2,26},{3,10},{4,28},{5,12},{6,15},{7,31},{8,16},{9,0... | collective-permute-start | bytes 319496 | tf_op jit(solution)/shard_map/ppermute | solution.py:726
  55.7 5.4 %collective-permute-start.8 = (bf16[416,256]{1,0:T(8,128)(2,1)S(1)}, bf16[416,256]{1,0:T(8,128)(2,1)S(1)}, u32[]{:S(2)}, u32[]{:S(2)}) collective-permute-start(bf16[416,256]{1,0:T(8,128)(2,1)S(1)} %pad_maximum_fusion.2), channel_id=1, source_target_pairs={{0,24},{1,8},{2,11},{3,27},{4,13},{5,29},{6,30},{7,14},{8,1},{9,17... | collective-permute-start | bytes 638984 | tf_op jit(solution)/shard_map/ppermute | solution.py:726
  58.1 6.3 %collective-permute-start.17 = (bf16[416,256]{1,0:T(8,128)(2,1)S(1)}, bf16[416,256]{1,0:T(8,128)(2,1)S(1)}, u32[]{:S(2)}, u32[]{:S(2)}) collective-permute-start(bf16[416,256]{1,0:T(8,128)(2,1)S(1)} %pad_maximum_fusion.3), channel_id=1, source_target_pairs={{0,24},{1,8},{2,11},{3,27},{4,13},{5,29},{6,30},{7,14},{8,1},{9,17... | collective-permute-start | bytes 638984 | tf_op jit(solution)/shard_map/ppermute | solution.py:726
  61.2 3.5 %collective-permute-start.9 = (bf16[832,256]{1,0:T(8,128)(2,1)S(1)}, bf16[832,256]{1,0:T(8,128)(2,1)S(1)}, u32[]{:S(2)}, u32[]{:S(2)}) collective-permute-start(bf16[832,256]{1,0:T(8,128)(2,1)S(1)} %pad_maximum_fusion.own), channel_id=1, source_target_pairs={{0,8},{1,9},{2,10},{3,11},{4,12},{5,13},{6,14},{7,15},{8,0},{9,1},... | collective-permute-start | bytes 1277960 | tf_op jit(solution)/shard_map/ppermute | solution.py:722
  64.5 1.9 %copy-start = (bf16[256,256]{1,0:T(8,128)(2,1)S(1)}, bf16[256,256]{1,0:T(8,128)(2,1)}, u32[]{:S(2)}) copy-start(bf16[256,256]{1,0:T(8,128)(2,1)} %constant.36.clone.turned) | copy-start | bytes 393220
  64.5 1.8 %collective-permute-start.18 = (bf16[832,256]{1,0:T(8,128)(2,1)S(1)}, bf16[832,256]{1,0:T(8,128)(2,1)S(1)}, u32[]{:S(2)}, u32[]{:S(2)}) collective-permute-start(bf16[832,256]{1,0:T(8,128)(2,1)S(1)} %pad_maximum_fusion.1.own), channel_id=1, source_target_pairs={{0,8},{1,9},{2,10},{3,11},{4,12},{5,13},{6,14},{7,15},{8,0},{9,1},... | collective-permute-start | bytes 1277960 | tf_op jit(solution)/shard_map/ppermute | solution.py:722

commit v5 on v4

--- a/solution.py
+++ b/solution.py
@@ -104,7 +104,7 @@
 
 def unshift(rows, row_bits):
     rolled = jnp.concatenate(
-        [pltpu.roll(rows[a : a + 8], SEG - 8 - a, 1) for a in range(0, SEG - 8, 8)] + [rows[SEG - 8 :]], axis=0
+        [pltpu.roll(rows[a : a + 16], SEG - 16 - a, 1) for a in range(0, SEG - 16, 16)] + [rows[SEG - 16 :]], axis=0
     )
     for step, bit in row_bits:
         rolled = jnp.where(bit, pltpu.roll(rolled, step, 1), rolled)
@@ -233,8 +233,8 @@
     head_masks = [(lane_head == h).astype(F32).astype(BF) for h in range(GROUP)]
     key_at = lax.broadcasted_iota(jnp.int32, (SEG, LANES), 1)
     query_at = lax.broadcasted_iota(jnp.int32, (SEG, LANES), 0) + SEG
-    low_row = 7 - (query_at & 7)
-    row_bits = [(step, (low_row & step) != 0) for step in (1, 2, 4)]
+    low_row = 15 - (query_at & 15)
+    row_bits = [(step, (low_row & step).astype(F32).astype(BF) > 0.5) for step in (8, 4, 2, 1)]
     upper = (lax.broadcasted_iota(jnp.int32, (SEG, FEATURES), 1) & (HEAD_DIM // 2)) != 0
     first_pair = key_at < 2 * HEAD_DIM
     pair_masks = [first_pair.astype(F32).astype(BF), (key_at >= 2 * HEAD_DIM).astype(F32).astype(BF)]
@@ -423,8 +423,8 @@
             for q in range(2):
                 head = 2 * p + q
                 braw[u.at, head * LANES : (head + 1) * LANES] = unshift(
-                    bs[:, q * LANES : (q + 1) * LANES], row_bits
-                ).astype(BF)
+                    u.grad_low[p][:, q * LANES : (q + 1) * LANES], row_bits
+                )
 
     def by_head(pairs, g):
         return jnp.concatenate(
@@ -502,7 +502,7 @@
             yield 1
 
     phases = {
-        "first": (8, first), "attend": (5 * block // SEG, attend), "feed": (14, feed), "back": (6 * block // SEG, attend_back), "last": (5, last),
+        "first": (8, first), "attend": (2 * block // SEG, attend), "feed": (14, feed), "back": (6 * block // SEG, attend_back), "last": (5, last),
     }
     for t in range(blocks + 4):
         if t == 2:
@@ -617,10 +617,9 @@
 
 
 def second_unpack_kernel(
-    w1_old, w2_old, wo_old, own, other, turned,
-    w1, w2, wo, wq, wk, wv, wr, gain1, shift1, cbias, pbias, gain2, shift2, b1, b2,
-    whole, expand, shrink, output, sems,
+    w1_old, w2_old, wo_old, own, other, turned, w1, w2, wo, wq, wk, wv, wr, *refs
 ):
+    vectors, (squares, output, longer, whole, sems, *kept) = refs[: V_EXPAND + 1], refs[V_EXPAND + 1 :]
     join(own, other, whole)
     moves = []
 
@@ -628,32 +627,32 @@
         moves.append(pltpu.make_async_copy(source, target, sems.at[len(moves)]))
         moves[-1].start()
 
+    def late(at, count):
+        at += EARLY_ROWS[1] if at < LATE_ROWS else EARLY_ROWS[1] + PART_ROWS - LATE_ROWS
+        return whole[at : at + count]
+
+    cosines = late(RELATIVE_AT, LANES)
+    squares[5] = t_dot(turned[0:LANES], cosines) + t_dot(turned[LANES:], cosines)
+    rows = late(VECTOR_AT, VECTOR_ROWS).astype(F32)
+    for k in range(V_EXPAND):
+        kept[k][...] = rows[k]
+        leave(kept[k], vectors[k])
+    for f in range(BLOCKS):
+        longer[f * FEATURES : (f + 1) * FEATURES] = rows[V_EXPAND + f]
+    leave(longer, vectors[V_EXPAND])
     cols = slice(HIDDEN - FEATURES, HIDDEN)
-    expand[...] = whole[0:FEATURES].astype(F32)
-    leave(expand, w1.at[:, cols])
-    shrink[...] = whole[PART_ROWS : PART_ROWS + FEATURES].astype(F32)
-    leave(shrink, w2.at[cols])
+    squares[0] = whole[0:FEATURES].astype(F32)
+    leave(squares.at[0], w1.at[:, cols])
+    squares[1] = whole[PART_ROWS : PART_ROWS + FEATURES].astype(F32)
+    leave(squares.at[1], w2.at[cols])
+    for k, (ref, at) in enumerate(((wq, QUERY_AT), (wk, KEY_AT), (wv, VALUE_AT))):
+        squares[k + 2] = late(at, FEATURES).astype(F32)
+        leave(squares.at[k + 2], ref)
+    leave(squares.at[5], wr)
     for k in range(2):
         start = k * PART_ROWS + FEATURES
         output[k] = whole[start : start + OUTPUT_PIECE].astype(F32)
         leave(output.at[k], wo.at[(k + 2) * OUTPUT_PIECE : (k + 3) * OUTPUT_PIECE])
-
-    def late(at, count):
-        at += EARLY_ROWS[1] if at < LATE_ROWS else EARLY_ROWS[1] + PART_ROWS - LATE_ROWS
-        return whole[at : at + count]
-
-    for ref, at in ((wq, QUERY_AT), (wk, KEY_AT), (wv, VALUE_AT)):
-        ref[...] = late(at, FEATURES).astype(F32)
-    cosines = late(RELATIVE_AT, LANES)
-    wr[...] = t_dot(turned[0:LANES], cosines) + t_dot(turned[LANES:], cosines)
-    vectors = late(VECTOR_AT, VECTOR_ROWS).astype(F32)
-    for ref, at in (
-        (cbias, V_CONTENT), (pbias, V_POSITION), (gain1, V_GAIN1), (shift1, V_SHIFT1),
-        (gain2, V_GAIN2), (shift2, V_SHIFT2), (b2, V_SHRINK),
-    ):
-        ref[...] = vectors[at]
-    for f in range(BLOCKS):
-        b1[f * FEATURES : (f + 1) * FEATURES] = vectors[V_EXPAND + f]
     for move in moves:
         move.wait()
 
@@ -663,17 +662,9 @@
     hbm = pl.BlockSpec(memory_space=pl.ANY)
     square, vector = (FEATURES, FEATURES), (FEATURES,)
     split = ((FEATURES, HIDDEN), (HIDDEN, FEATURES), square)
-    rest = (square,) * 4 + (vector,) * 6 + ((HIDDEN,), vector)
-
-    def pieces(count):
-        lead = (count,) if count > 1 else ()
-        return [
-            pltpu.VMEM((2 * PART_ROWS, FEATURES), BF),
-            pltpu.VMEM((*lead, *square), F32),
-            pltpu.VMEM((*lead, *square), F32),
-            pltpu.VMEM((2, OUTPUT_PIECE, FEATURES), F32),
-            pltpu.SemaphoreType.DMA((2 * count + 2,)),
-        ]
+    rest = (square,) * 4 + (vector,) * V_EXPAND + ((HIDDEN,),)
+    whole = pltpu.VMEM((2 * PART_ROWS, FEATURES), BF)
+    output = pltpu.VMEM((2, OUTPUT_PIECE, FEATURES), F32)
 
     def shapes(dims):
         return tuple(jax.ShapeDtypeStruct(shape, F32) for shape in dims)
@@ -684,16 +675,29 @@
         out_shape=shapes(split),
         in_specs=[vmem, vmem],
         out_specs=(hbm,) * 3,
-        scratch_shapes=pieces(BLOCKS - 1),
+        scratch_shapes=[
+            whole,
+            pltpu.VMEM((BLOCKS - 1, *square), F32),
+            pltpu.VMEM((BLOCKS - 1, *square), F32),
+            output,
+            pltpu.SemaphoreType.DMA((2 * BLOCKS,)),
+        ],
         compiler_params=params,
         name="unpack_first",
     )(*parts[:2])
-    w1, w2, wo, wq, wk, wv, wr, gain1, shift1, cbias, pbias, gain2, shift2, b1, b2 = pl.pallas_call(
+    w1, w2, wo, wq, wk, wv, wr, cbias, pbias, gain1, shift1, gain2, shift2, b2, b1 = pl.pallas_call(
         second_unpack_kernel,
         out_shape=shapes(split + rest),
         in_specs=[hbm] * 3 + [vmem] * 3,
-        out_specs=(hbm,) * 3 + (vmem,) * len(rest),
-        scratch_shapes=pieces(1),
+        out_specs=(hbm,) * (3 + len(rest)),
+        scratch_shapes=[
+            pltpu.VMEM((6, *square), F32),
+            output,
+            pltpu.VMEM((HIDDEN,), F32),
+            whole,
+            pltpu.SemaphoreType.DMA((8 + V_EXPAND + 1,)),
+        ]
+        + [pltpu.VMEM(vector, F32)] * V_EXPAND,
         input_output_aliases={0: 0, 1: 1, 2: 2},
         compiler_params=params,
         name="unpack_second",

time: 68.8 us -> 66.3 us (0.964)
  Pallas kernels: 22.9 us -> 20.4 us
    pallas_call x1, Pallas kernels: 19.5 us -> 17.5 us  [run_layer(): pl.pallas_call(layer_kernel, out_shape=(jax.ShapeDtypeStruct((rows, FEATU...]
where the time goes in v5:
time: 66.3 us; the launch traced here: 66.1 us
  starting transfers between devices  28.2 us (43%)
  Pallas kernels  20.4 us (31%)
  waiting for transfers between devices  13 us (20%)
  local copies, waits for them, and re-layouts  2.66 us (4%)
  between operations  0.97 us (1%)
  other arithmetic  0.81 us (1%)
    ppermute x14, starting transfers between devices, swap(): lax.ppermute(value, AXES, [(d, d ^ 1 << bits[side_of(d)] ^ 1 << core) for...  26.9 us
    pallas_call x1, Pallas kernels, run_layer(): pl.pallas_call(layer_kernel, out_shape=(jax.ShapeDtypeStruct((rows, FEATU...  17.5 us
    ppermute x14, waiting for transfers between devices, swap(): lax.ppermute(value, AXES, [(d, d ^ 1 << bits[side_of(d)] ^ 1 << core) for...  9.04 us
    ppermute x1, waiting for transfers between devices, body(): lax.ppermute(x[-SEG:], 'tm', [(i, (i + 1) % tm_count) for i in range(tm_c...  3.46 us
    pallas_call x1, Pallas kernels, unpack_all(): pl.pallas_call(second_unpack_kernel, out_shape=shapes(split + rest), in_s...  1.62 us
    pallas_call x1, Pallas kernels, unpack_all(): pl.pallas_call(first_unpack_kernel, out_shape=shapes(split), in_specs=[vm...  1.33 us
  transfers between devices with their start and end apart: 19, of which 12 were waited for; matrix products, arithmetic and copies ran while one was open for 3% of the time, Pallas kernels for 2%

profile of v5, /device:TPU:0, one launch (start us, length us, event | category | flops | bytes accessed | tf_op | source)
XLA Modules:
  0.0 66.1 jit_solution(6222180339216303207)
XLA Ops:
  0.7 0.7 %slice_bitcast_fusion = bf16[48,256]{1,0:T(8,128)(2,1)S(1)} fusion(bf16[1,768,256]{2,1,0:T(8,128)(2,1)} %param.22), kind=kLoop, calls=%fused_computation.34 | loop fusion | bytes 49152 | tf_op jit(solution)/shard_map/slice | solution.py:779
  1.4 0.5 collective-permute-start
  1.9 3.5 %collective-permute-done.refs_2_ = bf16[48,256]{1,0:T(8,128)(2,1)S(1)} collective-permute-done((bf16[48,256]{1,0:T(8,128)(2,1)S(1)}, bf16[48,256]{1,0:T(8,128)(2,1)S(1)}, u32[]{:S(2)}, u32[]{:S(2)}) %collective-permute-start) | collective-permute-done | bytes 24608 | tf_op jit(solution)/shard_map/ppermute | solution.py:779
  5.3 0.0 copy-start.1
  5.3 0.6 copy-done.1
  5.9 17.5 %layer.1 = (bf16[768,256]{1,0:T(8,128)(2,1)}, bf16[768,256]{1,0:T(8,128)(2,1)}, bf16[832,256]{1,0:T(8,128)(2,1)}, bf16[832,256]{1,0:T(8,128)(2,1)}, bf16[832,256]{1,0:T(8,128)(2,1)}, /*index=5*/bf16[832,256]{1,0:T(8,128)(2,1)}) custom-call(s32[1,64]{1,0:T(1,128)} %horizon_source.1, bf16[768,256]{1,0:T(8,128)(2,1)} %bitcast.15, bf16[48,256]{1,0:T(8,128)(2,1)} %bitcast.17, ...), custom_call_target="tpu_custom_call" | custom-call | tf_op jit(solution)/shard_map/layer/pallas_call | solution.py:562
  23.4 0.2 collective-permute-start.1
  23.6 0.4 collective-permute-start.10
  24.0 1.3 %constant_dynamic-slice_fusion = (bf16[416,256]{1,0:T(8,128)(2,1)S(1)}, bf16[416,256]{1,0:T(8,128)(2,1)S(1)}, bf16[416,256]{1,0:T(8,128)(2,1)S(1)}, bf16[416,256]{1,0:T(8,128)(2,1)S(1)}) fusion(bf16[832,256]{1,0:T(8,128)(2,1)} %get-tuple-element.54, s32[]{:T(128)S(6)} %select_n.113, s32[]{:T(128)S(6)} %select_n.112, bf16[832,256]{1,0:T(8,128)(2,1)} %get-tuple-element.47), kind=kLoop, calls=%fused_computation.35 | loop fusion | bytes 1703944 | tf_op jit(solution)/shard_map/dynamic_slice | solution.py:751
  25.3 0.2 collective-permute-done.1
  25.5 0.1 add_convert_fusion.3
  25.6 2.1 %collective-permute-start.2 = (bf16[416,256]{1,0:T(8,128)(2,1)S(1)}, bf16[416,256]{1,0:T(8,128)(2,1)S(1)}, u32[]{:S(2)}, u32[]{:S(2)}) collective-permute-start(bf16[416,256]{1,0:T(8,128)(2,1)S(1)} %get-tuple-element.86), channel_id=1, source_target_pairs={{0,24},{1,8},{2,11},{3,27},{4,13},{5,29},{6,30},{7,14},{8,1},{9,17... | collective-permute-start | bytes 638984 | tf_op jit(solution)/shard_map/ppermute | solution.py:730
  27.7 0.0 collective-permute-done.10
  27.7 0.1 add_convert_fusion.1
  27.8 0.5 collective-permute-start.11
  28.3 2.9 %collective-permute-done.2 = bf16[416,256]{1,0:T(8,128)(2,1)S(1)} collective-permute-done((bf16[416,256]{1,0:T(8,128)(2,1)S(1)}, bf16[416,256]{1,0:T(8,128)(2,1)S(1)}, u32[]{:S(2)}, u32[]{:S(2)}) %collective-permute-start.2) | collective-permute-done | bytes 213024 | tf_op jit(solution)/shard_map/ppermute | solution.py:730
  31.2 0.1 add_convert_fusion.7
  31.3 2.1 %collective-permute-start.3 = (bf16[208,256]{1,0:T(8,128)(2,1)S(1)}, bf16[208,256]{1,0:T(8,128)(2,1)S(1)}, u32[]{:S(2)}, u32[]{:S(2)}) collective-permute-start(bf16[208,256]{1,0:T(8,128)(2,1)S(1)} %get-tuple-element.84), channel_id=1, source_target_pairs={{0,9},{1,25},{2,26},{3,10},{4,28},{5,12},{6,15},{7,31},{8,16},{9,0... | collective-permute-start | bytes 319496 | tf_op jit(solution)/shard_map/ppermute | solution.py:730
  33.3 0.1 collective-permute-done.11
  33.5 0.1 add_convert_fusion.5
  33.6 1.8 %collective-permute-start.12 = (bf16[208,256]{1,0:T(8,128)(2,1)S(1)}, bf16[208,256]{1,0:T(8,128)(2,1)S(1)}, u32[]{:S(2)}, u32[]{:S(2)}) collective-permute-start(bf16[208,256]{1,0:T(8,128)(2,1)S(1)} %get-tuple-element.76), channel_id=1, source_target_pairs={{0,9},{1,25},{2,26},{3,10},{4,28},{5,12},{6,15},{7,31},{8,16},{9,0... | collective-permute-start | bytes 319496 | tf_op jit(solution)/shard_map/ppermute | solution.py:730
  35.3 0.4 collective-permute-done.3
  35.8 1.9 %collective-permute-start.4 = (bf16[104,256]{1,0:T(8,128)(2,1)S(1)}, bf16[104,256]{1,0:T(8,128)(2,1)S(1)}, u32[]{:S(2)}, u32[]{:S(2)}) collective-permute-start(bf16[104,256]{1,0:T(8,128)(2,1)S(1)} %add_convert_fusion.14), channel_id=1, source_target_pairs={{0,10},{1,11},{2,8},{3,9},{4,14},{5,15},{6,12},{7,13},{8,2},{9,3},... | collective-permute-start | bytes 159752 | tf_op jit(solution)/shard_map/ppermute | solution.py:730
  37.7 0.1 collective-permute-done.12
  37.8 1.9 %collective-permute-start.13 = (bf16[104,256]{1,0:T(8,128)(2,1)S(1)}, bf16[104,256]{1,0:T(8,128)(2,1)S(1)}, u32[]{:S(2)}, u32[]{:S(2)}) collective-permute-start(bf16[104,256]{1,0:T(8,128)(2,1)S(1)} %add_convert_fusion.10), channel_id=1, source_target_pairs={{0,10},{1,11},{2,8},{3,9},{4,14},{5,15},{6,12},{7,13},{8,2},{9,3},... | collective-permute-start | bytes 159752 | tf_op jit(solution)/shard_map/ppermute | solution.py:730
  39.6 0.0 collective-permute-done.4
  39.7 2.7 %collective-permute-start.5 = (bf16[104,256]{1,0:T(8,128)(2,1)S(1)}, bf16[104,256]{1,0:T(8,128)(2,1)S(1)}, u32[]{:S(2)}, u32[]{:S(2)}) collective-permute-start(bf16[104,256]{1,0:T(8,128)(2,1)S(1)} %add_convert_fusion.13), channel_id=1, source_target_pairs={{0,12},{1,13},{2,14},{3,15},{4,8},{5,9},{6,10},{7,11},{8,4},{9,5},... | collective-permute-start | bytes 159752 | tf_op jit(solution)/shard_map/ppermute | solution.py:730
  42.4 0.0 collective-permute-done.13
  42.4 2.2 %collective-permute-start.14 = (bf16[104,256]{1,0:T(8,128)(2,1)S(1)}, bf16[104,256]{1,0:T(8,128)(2,1)S(1)}, u32[]{:S(2)}, u32[]{:S(2)}) collective-permute-start(bf16[104,256]{1,0:T(8,128)(2,1)S(1)} %add_convert_fusion.9), channel_id=1, source_target_pairs={{0,12},{1,13},{2,14},{3,15},{4,8},{5,9},{6,10},{7,11},{8,4},{9,5},... | collective-permute-start | bytes 159752 | tf_op jit(solution)/shard_map/ppermute | solution.py:730
  44.6 0.0 collective-permute-done.5
  44.6 1.7 %collective-permute-start.6 = (bf16[104,256]{1,0:T(8,128)(2,1)S(1)}, bf16[104,256]{1,0:T(8,128)(2,1)S(1)}, u32[]{:S(2)}, u32[]{:S(2)}) collective-permute-start(bf16[104,256]{1,0:T(8,128)(2,1)S(1)} %add_convert_fusion.12), channel_id=1, source_target_pairs={{0,10},{1,11},{2,8},{3,9},{4,14},{5,15},{6,12},{7,13},{8,2},{9,3},... | collective-permute-start | bytes 159752 | tf_op jit(solution)/shard_map/ppermute | solution.py:730
  46.3 0.9 %collective-permute-done.14 = bf16[104,256]{1,0:T(8,128)(2,1)S(1)} collective-permute-done((bf16[104,256]{1,0:T(8,128)(2,1)S(1)}, bf16[104,256]{1,0:T(8,128)(2,1)S(1)}, u32[]{:S(2)}, u32[]{:S(2)}) %collective-permute-start.14) | collective-permute-done | bytes 53280 | tf_op jit(solution)/shard_map/ppermute | solution.py:730
  47.2 1.6 %collective-permute-start.15 = (bf16[104,256]{1,0:T(8,128)(2,1)S(1)}, bf16[104,256]{1,0:T(8,128)(2,1)S(1)}, u32[]{:S(2)}, u32[]{:S(2)}) collective-permute-start(bf16[104,256]{1,0:T(8,128)(2,1)S(1)} %add_convert_fusion.8), channel_id=1, source_target_pairs={{0,10},{1,11},{2,8},{3,9},{4,14},{5,15},{6,12},{7,13},{8,2},{9,3},... | collective-permute-start | bytes 159752 | tf_op jit(solution)/shard_map/ppermute | solution.py:730
  48.8 0.0 collective-permute-done.6
  48.9 1.7 %collective-permute-start.7 = (bf16[208,256]{1,0:T(8,128)(2,1)S(1)}, bf16[208,256]{1,0:T(8,128)(2,1)S(1)}, u32[]{:S(2)}, u32[]{:S(2)}) collective-permute-start(bf16[208,256]{1,0:T(8,128)(2,1)S(1)} %pad_maximum_fusion.4), channel_id=1, source_target_pairs={{0,9},{1,25},{2,26},{3,10},{4,28},{5,12},{6,15},{7,31},{8,16},{9,0... | collective-permute-start | bytes 319496 | tf_op jit(solution)/shard_map/ppermute | solution.py:730
  50.6 0.3 collective-permute-done.15
  50.9 2.7 %collective-permute-start.16 = (bf16[208,256]{1,0:T(8,128)(2,1)S(1)}, bf16[208,256]{1,0:T(8,128)(2,1)S(1)}, u32[]{:S(2)}, u32[]{:S(2)}) collective-permute-start(bf16[208,256]{1,0:T(8,128)(2,1)S(1)} %pad_maximum_fusion.5), channel_id=1, source_target_pairs={{0,9},{1,25},{2,26},{3,10},{4,28},{5,12},{6,15},{7,31},{8,16},{9,0... | collective-permute-start | bytes 319496 | tf_op jit(solution)/shard_map/ppermute | solution.py:730
  53.6 0.0 collective-permute-done.7
  53.6 1.2 %collective-permute-start.8 = (bf16[416,256]{1,0:T(8,128)(2,1)S(1)}, bf16[416,256]{1,0:T(8,128)(2,1)S(1)}, u32[]{:S(2)}, u32[]{:S(2)}) collective-permute-start(bf16[416,256]{1,0:T(8,128)(2,1)S(1)} %pad_maximum_fusion.2), channel_id=1, source_target_pairs={{0,24},{1,8},{2,11},{3,27},{4,13},{5,29},{6,30},{7,14},{8,1},{9,17... | collective-permute-start | bytes 638984 | tf_op jit(solution)/shard_map/ppermute | solution.py:730
  54.9 1.1 %collective-permute-done.16 = bf16[208,256]{1,0:T(8,128)(2,1)S(1)} collective-permute-done((bf16[208,256]{1,0:T(8,128)(2,1)S(1)}, bf16[208,256]{1,0:T(8,128)(2,1)S(1)}, u32[]{:S(2)}, u32[]{:S(2)}) %collective-permute-start.16) | collective-permute-done | bytes 106528 | tf_op jit(solution)/shard_map/ppermute | solution.py:730
  56.0 2.8 %collective-permute-start.17 = (bf16[416,256]{1,0:T(8,128)(2,1)S(1)}, bf16[416,256]{1,0:T(8,128)(2,1)S(1)}, u32[]{:S(2)}, u32[]{:S(2)}) collective-permute-start(bf16[416,256]{1,0:T(8,128)(2,1)S(1)} %pad_maximum_fusion.3), channel_id=1, source_target_pairs={{0,24},{1,8},{2,11},{3,27},{4,13},{5,29},{6,30},{7,14},{8,1},{9,17... | collective-permute-start | bytes 638984 | tf_op jit(solution)/shard_map/ppermute | solution.py:730
  58.8 0.3 collective-permute-done.8
  59.1 0.1 broadcast_select_fusion.3
  59.2 0.2 collective-permute-start.9
  59.4 3.0 %collective-permute-done.17 = bf16[416,256]{1,0:T(8,128)(2,1)S(1)} collective-permute-done((bf16[416,256]{1,0:T(8,128)(2,1)S(1)}, bf16[416,256]{1,0:T(8,128)(2,1)S(1)}, u32[]{:S(2)}, u32[]{:S(2)}) %collective-permute-start.17) | collective-permute-done | bytes 213024 | tf_op jit(solution)/shard_map/ppermute | solution.py:730
  62.4 0.1 broadcast_select_fusion.1
  62.5 0.0 copy-start
  62.5 0.2 collective-permute-start.18
  62.7 0.0 collective-permute-done.9.other
  62.7 1.3 %unpack_first.1 = (f32[256,1024]{1,0:T(8,128)}, f32[1024,256]{1,0:T(8,128)}, f32[256,256]{1,0:T(8,128)}) custom-call(bf16[832,256]{1,0:T(8,128)(2,1)S(1)} %pad_maximum_fusion.own, bf16[832,256]{1,0:T(8,128)(2,1)S(1)} %collective-permute-done.9.other), custom_call_target="tpu_custom_call" | custom-call | tf_op jit(solution)/shard_map/unpack_first/pallas_call | solution.py:673
  64.0 0.3 collective-permute-done.18.other
  64.3 0.0 copy-done
  64.3 1.6 %unpack_second.1 = (f32[256,1024]{1,0:T(8,128)}, f32[1024,256]{1,0:T(8,128)}, f32[256,256]{1,0:T(8,128)}, f32[256,256]{1,0:T(8,128)}, f32[256,256]{1,0:T(8,128)}...) custom-call(f32[256,1024]{1,0:T(8,128)} %get-tuple-element.51.w1_old, ...), custom_call_target="tpu_custom_call", output_to_operand_aliasing={{0}: (0, {}), {1}: (1, {}), {2}: (2, {})} | custom-call | tf_op jit(solution)/shard_map/unpack_second/pallas_call | solution.py:688
  (16 shorter events, 0.3 us)
Async XLA Ops:
  1.4 3.9 %collective-permute-start = (bf16[48,256]{1,0:T(8,128)(2,1)S(1)}, bf16[48,256]{1,0:T(8,128)(2,1)S(1)}, u32[]{:S(2)}, u32[]{:S(2)}) collective-permute-start(bf16[48,256]{1,0:T(8,128)(2,1)S(1)} %slice_bitcast_fusion), channel_id=1, source_target_pairs={{0,8},{8,16},{16,24},{24,0},{1,9},{9,17},{17,25},{25,1},{2,10},{10... | collective-permute-start | bytes 73736 | tf_op jit(solution)/shard_map/ppermute | solution.py:779
  5.3 0.6 copy-start.1
  23.4 2.0 %collective-permute-start.1 = (bf16[832,256]{1,0:T(8,128)(2,1)}, bf16[832,256]{1,0:T(8,128)(2,1)S(1)}, u32[]{:S(2)}, u32[]{:S(2)}) collective-permute-start(bf16[832,256]{1,0:T(8,128)(2,1)} %get-tuple-element.49), channel_id=1, source_target_pairs={{0,8},{1,9},{2,10},{3,11},{4,12},{5,13},{6,14},{7,15},{8,0},{9,1},... | collective-permute-start | bytes 1277960 | tf_op jit(solution)/shard_map/ppermute | solution.py:726
  23.6 4.1 %collective-permute-start.10 = (bf16[832,256]{1,0:T(8,128)(2,1)}, bf16[832,256]{1,0:T(8,128)(2,1)S(1)}, u32[]{:S(2)}, u32[]{:S(2)}) collective-permute-start(bf16[832,256]{1,0:T(8,128)(2,1)} %get-tuple-element.56), channel_id=1, source_target_pairs={{0,8},{1,9},{2,10},{3,11},{4,12},{5,13},{6,14},{7,15},{8,0},{9,1},... | collective-permute-start | bytes 1277960 | tf_op jit(solution)/shard_map/ppermute | solution.py:726
  25.6 5.6 %collective-permute-start.2 = (bf16[416,256]{1,0:T(8,128)(2,1)S(1)}, bf16[416,256]{1,0:T(8,128)(2,1)S(1)}, u32[]{:S(2)}, u32[]{:S(2)}) collective-permute-start(bf16[416,256]{1,0:T(8,128)(2,1)S(1)} %get-tuple-element.86), channel_id=1, source_target_pairs={{0,24},{1,8},{2,11},{3,27},{4,13},{5,29},{6,30},{7,14},{8,1},{9,17... | collective-permute-start | bytes 638984 | tf_op jit(solution)/shard_map/ppermute | solution.py:730
  27.8 5.7 %collective-permute-start.11 = (bf16[416,256]{1,0:T(8,128)(2,1)S(1)}, bf16[416,256]{1,0:T(8,128)(2,1)S(1)}, u32[]{:S(2)}, u32[]{:S(2)}) collective-permute-start(bf16[416,256]{1,0:T(8,128)(2,1)S(1)} %get-tuple-element.78), channel_id=1, source_target_pairs={{0,24},{1,8},{2,11},{3,27},{4,13},{5,29},{6,30},{7,14},{8,1},{9,17... | collective-permute-start | bytes 638984 | tf_op jit(solution)/shard_map/ppermute | solution.py:730
  31.3 4.5 %collective-permute-start.3 = (bf16[208,256]{1,0:T(8,128)(2,1)S(1)}, bf16[208,256]{1,0:T(8,128)(2,1)S(1)}, u32[]{:S(2)}, u32[]{:S(2)}) collective-permute-start(bf16[208,256]{1,0:T(8,128)(2,1)S(1)} %get-tuple-element.84), channel_id=1, source_target_pairs={{0,9},{1,25},{2,26},{3,10},{4,28},{5,12},{6,15},{7,31},{8,16},{9,0... | collective-permute-start | bytes 319496 | tf_op jit(solution)/shard_map/ppermute | solution.py:730
  33.6 4.2 %collective-permute-start.12 = (bf16[208,256]{1,0:T(8,128)(2,1)S(1)}, bf16[208,256]{1,0:T(8,128)(2,1)S(1)}, u32[]{:S(2)}, u32[]{:S(2)}) collective-permute-start(bf16[208,256]{1,0:T(8,128)(2,1)S(1)} %get-tuple-element.76), channel_id=1, source_target_pairs={{0,9},{1,25},{2,26},{3,10},{4,28},{5,12},{6,15},{7,31},{8,16},{9,0... | collective-permute-start | bytes 319496 | tf_op jit(solution)/shard_map/ppermute | solution.py:730
  35.8 3.9 %collective-permute-start.4 = (bf16[104,256]{1,0:T(8,128)(2,1)S(1)}, bf16[104,256]{1,0:T(8,128)(2,1)S(1)}, u32[]{:S(2)}, u32[]{:S(2)}) collective-permute-start(bf16[104,256]{1,0:T(8,128)(2,1)S(1)} %add_convert_fusion.14), channel_id=1, source_target_pairs={{0,10},{1,11},{2,8},{3,9},{4,14},{5,15},{6,12},{7,13},{8,2},{9,3},... | collective-permute-start | bytes 159752 | tf_op jit(solution)/shard_map/ppermute | solution.py:730
  37.8 4.6 %collective-permute-start.13 = (bf16[104,256]{1,0:T(8,128)(2,1)S(1)}, bf16[104,256]{1,0:T(8,128)(2,1)S(1)}, u32[]{:S(2)}, u32[]{:S(2)}) collective-permute-start(bf16[104,256]{1,0:T(8,128)(2,1)S(1)} %add_convert_fusion.10), channel_id=1, source_target_pairs={{0,10},{1,11},{2,8},{3,9},{4,14},{5,15},{6,12},{7,13},{8,2},{9,3},... | collective-permute-start | bytes 159752 | tf_op jit(solution)/shard_map/ppermute | solution.py:730
  39.7 4.9 %collective-permute-start.5 = (bf16[104,256]{1,0:T(8,128)(2,1)S(1)}, bf16[104,256]{1,0:T(8,128)(2,1)S(1)}, u32[]{:S(2)}, u32[]{:S(2)}) collective-permute-start(bf16[104,256]{1,0:T(8,128)(2,1)S(1)} %add_convert_fusion.13), channel_id=1, source_target_pairs={{0,12},{1,13},{2,14},{3,15},{4,8},{5,9},{6,10},{7,11},{8,4},{9,5},... | collective-permute-start | bytes 159752 | tf_op jit(solution)/shard_map/ppermute | solution.py:730
  42.4 4.8 %collective-permute-start.14 = (bf16[104,256]{1,0:T(8,128)(2,1)S(1)}, bf16[104,256]{1,0:T(8,128)(2,1)S(1)}, u32[]{:S(2)}, u32[]{:S(2)}) collective-permute-start(bf16[104,256]{1,0:T(8,128)(2,1)S(1)} %add_convert_fusion.9), channel_id=1, source_target_pairs={{0,12},{1,13},{2,14},{3,15},{4,8},{5,9},{6,10},{7,11},{8,4},{9,5},... | collective-permute-start | bytes 159752 | tf_op jit(solution)/shard_map/ppermute | solution.py:730
  44.6 4.3 %collective-permute-start.6 = (bf16[104,256]{1,0:T(8,128)(2,1)S(1)}, bf16[104,256]{1,0:T(8,128)(2,1)S(1)}, u32[]{:S(2)}, u32[]{:S(2)}) collective-permute-start(bf16[104,256]{1,0:T(8,128)(2,1)S(1)} %add_convert_fusion.12), channel_id=1, source_target_pairs={{0,10},{1,11},{2,8},{3,9},{4,14},{5,15},{6,12},{7,13},{8,2},{9,3},... | collective-permute-start | bytes 159752 | tf_op jit(solution)/shard_map/ppermute | solution.py:730
  47.2 3.6 %collective-permute-start.15 = (bf16[104,256]{1,0:T(8,128)(2,1)S(1)}, bf16[104,256]{1,0:T(8,128)(2,1)S(1)}, u32[]{:S(2)}, u32[]{:S(2)}) collective-permute-start(bf16[104,256]{1,0:T(8,128)(2,1)S(1)} %add_convert_fusion.8), channel_id=1, source_target_pairs={{0,10},{1,11},{2,8},{3,9},{4,14},{5,15},{6,12},{7,13},{8,2},{9,3},... | collective-permute-start | bytes 159752 | tf_op jit(solution)/shard_map/ppermute | solution.py:730
  48.9 4.7 %collective-permute-start.7 = (bf16[208,256]{1,0:T(8,128)(2,1)S(1)}, bf16[208,256]{1,0:T(8,128)(2,1)S(1)}, u32[]{:S(2)}, u32[]{:S(2)}) collective-permute-start(bf16[208,256]{1,0:T(8,128)(2,1)S(1)} %pad_maximum_fusion.4), channel_id=1, source_target_pairs={{0,9},{1,25},{2,26},{3,10},{4,28},{5,12},{6,15},{7,31},{8,16},{9,0... | collective-permute-start | bytes 319496 | tf_op jit(solution)/shard_map/ppermute | solution.py:730
  50.9 5.1 %collective-permute-start.16 = (bf16[208,256]{1,0:T(8,128)(2,1)S(1)}, bf16[208,256]{1,0:T(8,128)(2,1)S(1)}, u32[]{:S(2)}, u32[]{:S(2)}) collective-permute-start(bf16[208,256]{1,0:T(8,128)(2,1)S(1)} %pad_maximum_fusion.5), channel_id=1, source_target_pairs={{0,9},{1,25},{2,26},{3,10},{4,28},{5,12},{6,15},{7,31},{8,16},{9,0... | collective-permute-start | bytes 319496 | tf_op jit(solution)/shard_map/ppermute | solution.py:730
  53.6 5.4 %collective-permute-start.8 = (bf16[416,256]{1,0:T(8,128)(2,1)S(1)}, bf16[416,256]{1,0:T(8,128)(2,1)S(1)}, u32[]{:S(2)}, u32[]{:S(2)}) collective-permute-start(bf16[416,256]{1,0:T(8,128)(2,1)S(1)} %pad_maximum_fusion.2), channel_id=1, source_target_pairs={{0,24},{1,8},{2,11},{3,27},{4,13},{5,29},{6,30},{7,14},{8,1},{9,17... | collective-permute-start | bytes 638984 | tf_op jit(solution)/shard_map/ppermute | solution.py:730
  56.0 6.3 %collective-permute-start.17 = (bf16[416,256]{1,0:T(8,128)(2,1)S(1)}, bf16[416,256]{1,0:T(8,128)(2,1)S(1)}, u32[]{:S(2)}, u32[]{:S(2)}) collective-permute-start(bf16[416,256]{1,0:T(8,128)(2,1)S(1)} %pad_maximum_fusion.3), channel_id=1, source_target_pairs={{0,24},{1,8},{2,11},{3,27},{4,13},{5,29},{6,30},{7,14},{8,1},{9,17... | collective-permute-start | bytes 638984 | tf_op jit(solution)/shard_map/ppermute | solution.py:730
  59.2 3.5 %collective-permute-start.9 = (bf16[832,256]{1,0:T(8,128)(2,1)S(1)}, bf16[832,256]{1,0:T(8,128)(2,1)S(1)}, u32[]{:S(2)}, u32[]{:S(2)}) collective-permute-start(bf16[832,256]{1,0:T(8,128)(2,1)S(1)} %pad_maximum_fusion.own), channel_id=1, source_target_pairs={{0,8},{1,9},{2,10},{3,11},{4,12},{5,13},{6,14},{7,15},{8,0},{9,1},... | collective-permute-start | bytes 1277960 | tf_op jit(solution)/shard_map/ppermute | solution.py:726
  62.5 1.9 %copy-start = (bf16[256,256]{1,0:T(8,128)(2,1)S(1)}, bf16[256,256]{1,0:T(8,128)(2,1)}, u32[]{:S(2)}) copy-start(bf16[256,256]{1,0:T(8,128)(2,1)} %constant.36.clone.turned) | copy-start | bytes 393220
  62.5 1.8 %collective-permute-start.18 = (bf16[832,256]{1,0:T(8,128)(2,1)S(1)}, bf16[832,256]{1,0:T(8,128)(2,1)S(1)}, u32[]{:S(2)}, u32[]{:S(2)}) collective-permute-start(bf16[832,256]{1,0:T(8,128)(2,1)S(1)} %pad_maximum_fusion.1.own), channel_id=1, source_target_pairs={{0,8},{1,9},{2,10},{3,11},{4,12},{5,13},{6,14},{7,15},{8,0},{9,1},... | collective-permute-start | bytes 1277960 | tf_op jit(solution)/shard_map/ppermute | solution.py:726

commit v6 on v5

--- a/solution.py
+++ b/solution.py
@@ -163,11 +163,11 @@
                 leave(pltpu.make_async_copy(early.at[at], to, half_sems.at[2 * p + k]))
             start += 2 * EARLY_ROWS[p]
 
-    def send_late():
+    def send_late(piece):
         for k, half in enumerate((side, 1 - side)):
-            at = pl.ds(pl.multiple_of(half * LATE_ROWS, LATE_ROWS), LATE_ROWS)
-            to = halves[2 + k].at[EARLY_ROWS[1] : PART_ROWS]
-            leave(pltpu.make_async_copy(late.at[at], to, half_sems.at[2 * PIPES + k]))
+            at = pl.ds(pl.multiple_of(half * LATE_ROWS + piece * FEATURES, FEATURES), FEATURES)
+            to = halves[2 + k].at[EARLY_ROWS[1] + piece * FEATURES : EARLY_ROWS[1] + (piece + 1) * FEATURES]
+            leave(pltpu.make_async_copy(late.at[at], to, half_sems.at[2 * PIPES + 2 * piece + k]))
 
     compute_layer(
         position, horizon, lengths, moves, (send_rows, send_early, send_late), *targets, out, dx, early, late, *scratch
@@ -485,9 +485,10 @@
         memory_rows = nl[0:rows]
         late[QUERY_AT : QUERY_AT + FEATURES] = t_dot(segment_rows, bql[...]).astype(BF)
         yield 1
+        late[VALUE_AT : VALUE_AT + FEATURES] = (t_dot(segment_rows, vgs[...]) + t_dot(memory_rows, vgm[...])).astype(BF)
+        send_late(0)
+        yield 1
         late[KEY_AT : KEY_AT + FEATURES] = (t_dot(segment_rows, kgs[...]) + t_dot(memory_rows, kgm[...])).astype(BF)
-        yield 1
-        late[VALUE_AT : VALUE_AT + FEATURES] = (t_dot(segment_rows, vgs[...]) + t_dot(memory_rows, vgm[...])).astype(BF)
         yield 1
         for g in range(HEADS // GROUP):
             lanes = slice(g * LANES, (g + 1) * LANES)
@@ -512,14 +513,14 @@
             if 0 <= t - lag < blocks:
                 steps.append((count, phase(t - lag)))
         if t == blocks + 2:
-            steps.append((9, feed_weights()))
+            steps.append((18, feed_weights()))
         if t == blocks + 3:
             pass
         interleave(*steps)
     interleave((5, attention_weights()))
     late[VECTOR_AT : VECTOR_AT + VECTOR_ROWS] = vec[...].astype(BF)
     late[VECTOR_AT + VECTOR_ROWS :] = jnp.zeros((2 * LATE_ROWS - VECTOR_AT - VECTOR_ROWS, FEATURES), BF)
-    send_late()
+    send_late(1)
 
 
 def run_layer(horizon, x, start, arrived, cot, table, basis, params):
@@ -572,7 +573,7 @@
         + [
             pltpu.SemaphoreType.DMA((COPIES + 1,)),
             pltpu.SemaphoreType.DMA((4 * (rows // SEG) + 2 * PIPES,)),
-            pltpu.SemaphoreType.DMA((2 * PIPES + 2,)),
+            pltpu.SemaphoreType.DMA((2 * PIPES + 4,)),
             pltpu.SMEM(horizon.shape, horizon.dtype),
             pltpu.VMEM((rows, FEATURES), BF),
             pltpu.VMEM((rows, FEATURES), BF),

time: 66.3 us -> 66.1 us (level)
  no operation moved by 1% of the time
where the time goes in v6:
time: 66.1 us; the launch traced here: 65.8 us
  starting transfers between devices  28.2 us (43%)
  Pallas kernels  20.2 us (31%)
  waiting for transfers between devices  13 us (20%)
  local copies, waits for them, and re-layouts  2.66 us (4%)
  between operations  0.97 us (1%)
  other arithmetic  0.81 us (1%)
    ppermute x14, starting transfers between devices, swap(): lax.ppermute(value, AXES, [(d, d ^ 1 << bits[side_of(d)] ^ 1 << core) for...  26.8 us
    pallas_call x1, Pallas kernels, run_layer(): pl.pallas_call(layer_kernel, out_shape=(jax.ShapeDtypeStruct((rows, FEATU...  17.2 us
    ppermute x14, waiting for transfers between devices, swap(): lax.ppermute(value, AXES, [(d, d ^ 1 << bits[side_of(d)] ^ 1 << core) for...  9.05 us
    ppermute x1, waiting for transfers between devices, body(): lax.ppermute(x[-SEG:], 'tm', [(i, (i + 1) % tm_count) for i in range(tm_c...  3.46 us
    pallas_call x1, Pallas kernels, unpack_all(): pl.pallas_call(second_unpack_kernel, out_shape=shapes(split + rest), in_s...  1.62 us
    pallas_call x1, Pallas kernels, unpack_all(): pl.pallas_call(first_unpack_kernel, out_shape=shapes(split), in_specs=[vm...  1.33 us
  transfers between devices with their start and end apart: 19, of which 12 were waited for; matrix products, arithmetic and copies ran while one was open for 3% of the time, Pallas kernels for 2%

profile of v6, /device:TPU:0, one launch (start us, length us, event | category | flops | bytes accessed | tf_op | source)
XLA Modules:
  0.0 65.8 jit_solution(11542560669640910310)
XLA Ops:
  0.7 0.7 %slice_bitcast_fusion = bf16[48,256]{1,0:T(8,128)(2,1)S(1)} fusion(bf16[1,768,256]{2,1,0:T(8,128)(2,1)} %param.22), kind=kLoop, calls=%fused_computation.34 | loop fusion | bytes 49152 | tf_op jit(solution)/shard_map/slice | solution.py:780
  1.4 0.5 collective-permute-start
  1.9 3.5 %collective-permute-done.refs_2_ = bf16[48,256]{1,0:T(8,128)(2,1)S(1)} collective-permute-done((bf16[48,256]{1,0:T(8,128)(2,1)S(1)}, bf16[48,256]{1,0:T(8,128)(2,1)S(1)}, u32[]{:S(2)}, u32[]{:S(2)}) %collective-permute-start) | collective-permute-done | bytes 24608 | tf_op jit(solution)/shard_map/ppermute | solution.py:780
  5.3 0.0 copy-start.1
  5.3 0.6 copy-done.1
  5.9 17.2 %layer.1 = (bf16[768,256]{1,0:T(8,128)(2,1)}, bf16[768,256]{1,0:T(8,128)(2,1)}, bf16[832,256]{1,0:T(8,128)(2,1)}, bf16[832,256]{1,0:T(8,128)(2,1)}, bf16[832,256]{1,0:T(8,128)(2,1)}, /*index=5*/bf16[832,256]{1,0:T(8,128)(2,1)}) custom-call(s32[1,64]{1,0:T(1,128)} %horizon_source.1, bf16[768,256]{1,0:T(8,128)(2,1)} %bitcast.15, bf16[48,256]{1,0:T(8,128)(2,1)} %bitcast.17, ...), custom_call_target="tpu_custom_call" | custom-call | tf_op jit(solution)/shard_map/layer/pallas_call | solution.py:563
  23.2 0.2 collective-permute-start.1
  23.3 0.4 collective-permute-start.10
  23.7 1.3 %constant_dynamic-slice_fusion = (bf16[416,256]{1,0:T(8,128)(2,1)S(1)}, bf16[416,256]{1,0:T(8,128)(2,1)S(1)}, bf16[416,256]{1,0:T(8,128)(2,1)S(1)}, bf16[416,256]{1,0:T(8,128)(2,1)S(1)}) fusion(bf16[832,256]{1,0:T(8,128)(2,1)} %get-tuple-element.54, s32[]{:T(128)S(6)} %select_n.113, s32[]{:T(128)S(6)} %select_n.112, bf16[832,256]{1,0:T(8,128)(2,1)} %get-tuple-element.47), kind=kLoop, calls=%fused_computation.35 | loop fusion | bytes 1703944 | tf_op jit(solution)/shard_map/dynamic_slice | solution.py:752
  25.0 0.2 collective-permute-done.1
  25.2 0.1 add_convert_fusion.3
  25.3 2.1 %collective-permute-start.2 = (bf16[416,256]{1,0:T(8,128)(2,1)S(1)}, bf16[416,256]{1,0:T(8,128)(2,1)S(1)}, u32[]{:S(2)}, u32[]{:S(2)}) collective-permute-start(bf16[416,256]{1,0:T(8,128)(2,1)S(1)} %get-tuple-element.86), channel_id=1, source_target_pairs={{0,24},{1,8},{2,11},{3,27},{4,13},{5,29},{6,30},{7,14},{8,1},{9,17... | collective-permute-start | bytes 638984 | tf_op jit(solution)/shard_map/ppermute | solution.py:731
  27.4 0.0 collective-permute-done.10
  27.4 0.1 add_convert_fusion.1
  27.5 0.5 collective-permute-start.11
  28.0 2.9 %collective-permute-done.2 = bf16[416,256]{1,0:T(8,128)(2,1)S(1)} collective-permute-done((bf16[416,256]{1,0:T(8,128)(2,1)S(1)}, bf16[416,256]{1,0:T(8,128)(2,1)S(1)}, u32[]{:S(2)}, u32[]{:S(2)}) %collective-permute-start.2) | collective-permute-done | bytes 213024 | tf_op jit(solution)/shard_map/ppermute | solution.py:731
  31.0 0.1 add_convert_fusion.7
  31.0 2.1 %collective-permute-start.3 = (bf16[208,256]{1,0:T(8,128)(2,1)S(1)}, bf16[208,256]{1,0:T(8,128)(2,1)S(1)}, u32[]{:S(2)}, u32[]{:S(2)}) collective-permute-start(bf16[208,256]{1,0:T(8,128)(2,1)S(1)} %get-tuple-element.84), channel_id=1, source_target_pairs={{0,9},{1,25},{2,26},{3,10},{4,28},{5,12},{6,15},{7,31},{8,16},{9,0... | collective-permute-start | bytes 319496 | tf_op jit(solution)/shard_map/ppermute | solution.py:731
  33.1 0.2 collective-permute-done.11
  33.2 0.1 add_convert_fusion.5
  33.3 1.8 %collective-permute-start.12 = (bf16[208,256]{1,0:T(8,128)(2,1)S(1)}, bf16[208,256]{1,0:T(8,128)(2,1)S(1)}, u32[]{:S(2)}, u32[]{:S(2)}) collective-permute-start(bf16[208,256]{1,0:T(8,128)(2,1)S(1)} %get-tuple-element.76), channel_id=1, source_target_pairs={{0,9},{1,25},{2,26},{3,10},{4,28},{5,12},{6,15},{7,31},{8,16},{9,0... | collective-permute-start | bytes 319496 | tf_op jit(solution)/shard_map/ppermute | solution.py:731
  35.1 0.4 collective-permute-done.3
  35.5 1.9 %collective-permute-start.4 = (bf16[104,256]{1,0:T(8,128)(2,1)S(1)}, bf16[104,256]{1,0:T(8,128)(2,1)S(1)}, u32[]{:S(2)}, u32[]{:S(2)}) collective-permute-start(bf16[104,256]{1,0:T(8,128)(2,1)S(1)} %add_convert_fusion.14), channel_id=1, source_target_pairs={{0,10},{1,11},{2,8},{3,9},{4,14},{5,15},{6,12},{7,13},{8,2},{9,3},... | collective-permute-start | bytes 159752 | tf_op jit(solution)/shard_map/ppermute | solution.py:731
  37.4 0.1 collective-permute-done.12
  37.5 1.9 %collective-permute-start.13 = (bf16[104,256]{1,0:T(8,128)(2,1)S(1)}, bf16[104,256]{1,0:T(8,128)(2,1)S(1)}, u32[]{:S(2)}, u32[]{:S(2)}) collective-permute-start(bf16[104,256]{1,0:T(8,128)(2,1)S(1)} %add_convert_fusion.10), channel_id=1, source_target_pairs={{0,10},{1,11},{2,8},{3,9},{4,14},{5,15},{6,12},{7,13},{8,2},{9,3},... | collective-permute-start | bytes 159752 | tf_op jit(solution)/shard_map/ppermute | solution.py:731
  39.4 0.0 collective-permute-done.4
  39.4 2.7 %collective-permute-start.5 = (bf16[104,256]{1,0:T(8,128)(2,1)S(1)}, bf16[104,256]{1,0:T(8,128)(2,1)S(1)}, u32[]{:S(2)}, u32[]{:S(2)}) collective-permute-start(bf16[104,256]{1,0:T(8,128)(2,1)S(1)} %add_convert_fusion.13), channel_id=1, source_target_pairs={{0,12},{1,13},{2,14},{3,15},{4,8},{5,9},{6,10},{7,11},{8,4},{9,5},... | collective-permute-start | bytes 159752 | tf_op jit(solution)/shard_map/ppermute | solution.py:731
  42.1 0.0 collective-permute-done.13
  42.1 2.2 %collective-permute-start.14 = (bf16[104,256]{1,0:T(8,128)(2,1)S(1)}, bf16[104,256]{1,0:T(8,128)(2,1)S(1)}, u32[]{:S(2)}, u32[]{:S(2)}) collective-permute-start(bf16[104,256]{1,0:T(8,128)(2,1)S(1)} %add_convert_fusion.9), channel_id=1, source_target_pairs={{0,12},{1,13},{2,14},{3,15},{4,8},{5,9},{6,10},{7,11},{8,4},{9,5},... | collective-permute-start | bytes 159752 | tf_op jit(solution)/shard_map/ppermute | solution.py:731
  44.3 0.0 collective-permute-done.5
  44.3 1.7 %collective-permute-start.6 = (bf16[104,256]{1,0:T(8,128)(2,1)S(1)}, bf16[104,256]{1,0:T(8,128)(2,1)S(1)}, u32[]{:S(2)}, u32[]{:S(2)}) collective-permute-start(bf16[104,256]{1,0:T(8,128)(2,1)S(1)} %add_convert_fusion.12), channel_id=1, source_target_pairs={{0,10},{1,11},{2,8},{3,9},{4,14},{5,15},{6,12},{7,13},{8,2},{9,3},... | collective-permute-start | bytes 159752 | tf_op jit(solution)/shard_map/ppermute | solution.py:731
  46.1 0.9 %collective-permute-done.14 = bf16[104,256]{1,0:T(8,128)(2,1)S(1)} collective-permute-done((bf16[104,256]{1,0:T(8,128)(2,1)S(1)}, bf16[104,256]{1,0:T(8,128)(2,1)S(1)}, u32[]{:S(2)}, u32[]{:S(2)}) %collective-permute-start.14) | collective-permute-done | bytes 53280 | tf_op jit(solution)/shard_map/ppermute | solution.py:731
  47.0 1.6 %collective-permute-start.15 = (bf16[104,256]{1,0:T(8,128)(2,1)S(1)}, bf16[104,256]{1,0:T(8,128)(2,1)S(1)}, u32[]{:S(2)}, u32[]{:S(2)}) collective-permute-start(bf16[104,256]{1,0:T(8,128)(2,1)S(1)} %add_convert_fusion.8), channel_id=1, source_target_pairs={{0,10},{1,11},{2,8},{3,9},{4,14},{5,15},{6,12},{7,13},{8,2},{9,3},... | collective-permute-start | bytes 159752 | tf_op jit(solution)/shard_map/ppermute | solution.py:731
  48.6 0.0 collective-permute-done.6
  48.6 1.7 %collective-permute-start.7 = (bf16[208,256]{1,0:T(8,128)(2,1)S(1)}, bf16[208,256]{1,0:T(8,128)(2,1)S(1)}, u32[]{:S(2)}, u32[]{:S(2)}) collective-permute-start(bf16[208,256]{1,0:T(8,128)(2,1)S(1)} %pad_maximum_fusion.4), channel_id=1, source_target_pairs={{0,9},{1,25},{2,26},{3,10},{4,28},{5,12},{6,15},{7,31},{8,16},{9,0... | collective-permute-start | bytes 319496 | tf_op jit(solution)/shard_map/ppermute | solution.py:731
  50.3 0.3 collective-permute-done.15
  50.6 2.7 %collective-permute-start.16 = (bf16[208,256]{1,0:T(8,128)(2,1)S(1)}, bf16[208,256]{1,0:T(8,128)(2,1)S(1)}, u32[]{:S(2)}, u32[]{:S(2)}) collective-permute-start(bf16[208,256]{1,0:T(8,128)(2,1)S(1)} %pad_maximum_fusion.5), channel_id=1, source_target_pairs={{0,9},{1,25},{2,26},{3,10},{4,28},{5,12},{6,15},{7,31},{8,16},{9,0... | collective-permute-start | bytes 319496 | tf_op jit(solution)/shard_map/ppermute | solution.py:731
  53.3 0.0 collective-permute-done.7
  53.4 1.2 %collective-permute-start.8 = (bf16[416,256]{1,0:T(8,128)(2,1)S(1)}, bf16[416,256]{1,0:T(8,128)(2,1)S(1)}, u32[]{:S(2)}, u32[]{:S(2)}) collective-permute-start(bf16[416,256]{1,0:T(8,128)(2,1)S(1)} %pad_maximum_fusion.2), channel_id=1, source_target_pairs={{0,24},{1,8},{2,11},{3,27},{4,13},{5,29},{6,30},{7,14},{8,1},{9,17... | collective-permute-start | bytes 638984 | tf_op jit(solution)/shard_map/ppermute | solution.py:731
  54.6 1.1 %collective-permute-done.16 = bf16[208,256]{1,0:T(8,128)(2,1)S(1)} collective-permute-done((bf16[208,256]{1,0:T(8,128)(2,1)S(1)}, bf16[208,256]{1,0:T(8,128)(2,1)S(1)}, u32[]{:S(2)}, u32[]{:S(2)}) %collective-permute-start.16) | collective-permute-done | bytes 106528 | tf_op jit(solution)/shard_map/ppermute | solution.py:731
  55.8 2.8 %collective-permute-start.17 = (bf16[416,256]{1,0:T(8,128)(2,1)S(1)}, bf16[416,256]{1,0:T(8,128)(2,1)S(1)}, u32[]{:S(2)}, u32[]{:S(2)}) collective-permute-start(bf16[416,256]{1,0:T(8,128)(2,1)S(1)} %pad_maximum_fusion.3), channel_id=1, source_target_pairs={{0,24},{1,8},{2,11},{3,27},{4,13},{5,29},{6,30},{7,14},{8,1},{9,17... | collective-permute-start | bytes 638984 | tf_op jit(solution)/shard_map/ppermute | solution.py:731
  58.6 0.3 collective-permute-done.8
  58.8 0.1 broadcast_select_fusion.3
  58.9 0.2 collective-permute-start.9
  59.1 3.0 %collective-permute-done.17 = bf16[416,256]{1,0:T(8,128)(2,1)S(1)} collective-permute-done((bf16[416,256]{1,0:T(8,128)(2,1)S(1)}, bf16[416,256]{1,0:T(8,128)(2,1)S(1)}, u32[]{:S(2)}, u32[]{:S(2)}) %collective-permute-start.17) | collective-permute-done | bytes 213024 | tf_op jit(solution)/shard_map/ppermute | solution.py:731
  62.1 0.1 broadcast_select_fusion.1
  62.2 0.0 copy-start
  62.2 0.2 collective-permute-start.18
  62.4 0.0 collective-permute-done.9.other
  62.4 1.3 %unpack_first.1 = (f32[256,1024]{1,0:T(8,128)}, f32[1024,256]{1,0:T(8,128)}, f32[256,256]{1,0:T(8,128)}) custom-call(bf16[832,256]{1,0:T(8,128)(2,1)S(1)} %pad_maximum_fusion.own, bf16[832,256]{1,0:T(8,128)(2,1)S(1)} %collective-permute-done.9.other), custom_call_target="tpu_custom_call" | custom-call | tf_op jit(solution)/shard_map/unpack_first/pallas_call | solution.py:674
  63.8 0.3 collective-permute-done.18.other
  64.1 0.0 copy-done
  64.1 1.6 %unpack_second.1 = (f32[256,1024]{1,0:T(8,128)}, f32[1024,256]{1,0:T(8,128)}, f32[256,256]{1,0:T(8,128)}, f32[256,256]{1,0:T(8,128)}, f32[256,256]{1,0:T(8,128)}...) custom-call(f32[256,1024]{1,0:T(8,128)} %get-tuple-element.51.w1_old, ...), custom_call_target="tpu_custom_call", output_to_operand_aliasing={{0}: (0, {}), {1}: (1, {}), {2}: (2, {})} | custom-call | tf_op jit(solution)/shard_map/unpack_second/pallas_call | solution.py:689
  (16 shorter events, 0.3 us)
Async XLA Ops:
  1.4 3.9 %collective-permute-start = (bf16[48,256]{1,0:T(8,128)(2,1)S(1)}, bf16[48,256]{1,0:T(8,128)(2,1)S(1)}, u32[]{:S(2)}, u32[]{:S(2)}) collective-permute-start(bf16[48,256]{1,0:T(8,128)(2,1)S(1)} %slice_bitcast_fusion), channel_id=1, source_target_pairs={{0,8},{8,16},{16,24},{24,0},{1,9},{9,17},{17,25},{25,1},{2,10},{10... | collective-permute-start | bytes 73736 | tf_op jit(solution)/shard_map/ppermute | solution.py:780
  5.3 0.6 copy-start.1
  23.2 2.0 %collective-permute-start.1 = (bf16[832,256]{1,0:T(8,128)(2,1)}, bf16[832,256]{1,0:T(8,128)(2,1)S(1)}, u32[]{:S(2)}, u32[]{:S(2)}) collective-permute-start(bf16[832,256]{1,0:T(8,128)(2,1)} %get-tuple-element.49), channel_id=1, source_target_pairs={{0,8},{1,9},{2,10},{3,11},{4,12},{5,13},{6,14},{7,15},{8,0},{9,1},... | collective-permute-start | bytes 1277960 | tf_op jit(solution)/shard_map/ppermute | solution.py:727
  23.3 4.1 %collective-permute-start.10 = (bf16[832,256]{1,0:T(8,128)(2,1)}, bf16[832,256]{1,0:T(8,128)(2,1)S(1)}, u32[]{:S(2)}, u32[]{:S(2)}) collective-permute-start(bf16[832,256]{1,0:T(8,128)(2,1)} %get-tuple-element.56), channel_id=1, source_target_pairs={{0,8},{1,9},{2,10},{3,11},{4,12},{5,13},{6,14},{7,15},{8,0},{9,1},... | collective-permute-start | bytes 1277960 | tf_op jit(solution)/shard_map/ppermute | solution.py:727
  25.3 5.6 %collective-permute-start.2 = (bf16[416,256]{1,0:T(8,128)(2,1)S(1)}, bf16[416,256]{1,0:T(8,128)(2,1)S(1)}, u32[]{:S(2)}, u32[]{:S(2)}) collective-permute-start(bf16[416,256]{1,0:T(8,128)(2,1)S(1)} %get-tuple-element.86), channel_id=1, source_target_pairs={{0,24},{1,8},{2,11},{3,27},{4,13},{5,29},{6,30},{7,14},{8,1},{9,17... | collective-permute-start | bytes 638984 | tf_op jit(solution)/shard_map/ppermute | solution.py:731
  27.5 5.7 %collective-permute-start.11 = (bf16[416,256]{1,0:T(8,128)(2,1)S(1)}, bf16[416,256]{1,0:T(8,128)(2,1)S(1)}, u32[]{:S(2)}, u32[]{:S(2)}) collective-permute-start(bf16[416,256]{1,0:T(8,128)(2,1)S(1)} %get-tuple-element.78), channel_id=1, source_target_pairs={{0,24},{1,8},{2,11},{3,27},{4,13},{5,29},{6,30},{7,14},{8,1},{9,17... | collective-permute-start | bytes 638984 | tf_op jit(solution)/shard_map/ppermute | solution.py:731
  31.0 4.5 %collective-permute-start.3 = (bf16[208,256]{1,0:T(8,128)(2,1)S(1)}, bf16[208,256]{1,0:T(8,128)(2,1)S(1)}, u32[]{:S(2)}, u32[]{:S(2)}) collective-permute-start(bf16[208,256]{1,0:T(8,128)(2,1)S(1)} %get-tuple-element.84), channel_id=1, source_target_pairs={{0,9},{1,25},{2,26},{3,10},{4,28},{5,12},{6,15},{7,31},{8,16},{9,0... | collective-permute-start | bytes 319496 | tf_op jit(solution)/shard_map/ppermute | solution.py:731
  33.3 4.2 %collective-permute-start.12 = (bf16[208,256]{1,0:T(8,128)(2,1)S(1)}, bf16[208,256]{1,0:T(8,128)(2,1)S(1)}, u32[]{:S(2)}, u32[]{:S(2)}) collective-permute-start(bf16[208,256]{1,0:T(8,128)(2,1)S(1)} %get-tuple-element.76), channel_id=1, source_target_pairs={{0,9},{1,25},{2,26},{3,10},{4,28},{5,12},{6,15},{7,31},{8,16},{9,0... | collective-permute-start | bytes 319496 | tf_op jit(solution)/shard_map/ppermute | solution.py:731
  35.5 3.9 %collective-permute-start.4 = (bf16[104,256]{1,0:T(8,128)(2,1)S(1)}, bf16[104,256]{1,0:T(8,128)(2,1)S(1)}, u32[]{:S(2)}, u32[]{:S(2)}) collective-permute-start(bf16[104,256]{1,0:T(8,128)(2,1)S(1)} %add_convert_fusion.14), channel_id=1, source_target_pairs={{0,10},{1,11},{2,8},{3,9},{4,14},{5,15},{6,12},{7,13},{8,2},{9,3},... | collective-permute-start | bytes 159752 | tf_op jit(solution)/shard_map/ppermute | solution.py:731
  37.5 4.6 %collective-permute-start.13 = (bf16[104,256]{1,0:T(8,128)(2,1)S(1)}, bf16[104,256]{1,0:T(8,128)(2,1)S(1)}, u32[]{:S(2)}, u32[]{:S(2)}) collective-permute-start(bf16[104,256]{1,0:T(8,128)(2,1)S(1)} %add_convert_fusion.10), channel_id=1, source_target_pairs={{0,10},{1,11},{2,8},{3,9},{4,14},{5,15},{6,12},{7,13},{8,2},{9,3},... | collective-permute-start | bytes 159752 | tf_op jit(solution)/shard_map/ppermute | solution.py:731
  39.4 4.9 %collective-permute-start.5 = (bf16[104,256]{1,0:T(8,128)(2,1)S(1)}, bf16[104,256]{1,0:T(8,128)(2,1)S(1)}, u32[]{:S(2)}, u32[]{:S(2)}) collective-permute-start(bf16[104,256]{1,0:T(8,128)(2,1)S(1)} %add_convert_fusion.13), channel_id=1, source_target_pairs={{0,12},{1,13},{2,14},{3,15},{4,8},{5,9},{6,10},{7,11},{8,4},{9,5},... | collective-permute-start | bytes 159752 | tf_op jit(solution)/shard_map/ppermute | solution.py:731
  42.1 4.8 %collective-permute-start.14 = (bf16[104,256]{1,0:T(8,128)(2,1)S(1)}, bf16[104,256]{1,0:T(8,128)(2,1)S(1)}, u32[]{:S(2)}, u32[]{:S(2)}) collective-permute-start(bf16[104,256]{1,0:T(8,128)(2,1)S(1)} %add_convert_fusion.9), channel_id=1, source_target_pairs={{0,12},{1,13},{2,14},{3,15},{4,8},{5,9},{6,10},{7,11},{8,4},{9,5},... | collective-permute-start | bytes 159752 | tf_op jit(solution)/shard_map/ppermute | solution.py:731
  44.3 4.3 %collective-permute-start.6 = (bf16[104,256]{1,0:T(8,128)(2,1)S(1)}, bf16[104,256]{1,0:T(8,128)(2,1)S(1)}, u32[]{:S(2)}, u32[]{:S(2)}) collective-permute-start(bf16[104,256]{1,0:T(8,128)(2,1)S(1)} %add_convert_fusion.12), channel_id=1, source_target_pairs={{0,10},{1,11},{2,8},{3,9},{4,14},{5,15},{6,12},{7,13},{8,2},{9,3},... | collective-permute-start | bytes 159752 | tf_op jit(solution)/shard_map/ppermute | solution.py:731
  47.0 3.6 %collective-permute-start.15 = (bf16[104,256]{1,0:T(8,128)(2,1)S(1)}, bf16[104,256]{1,0:T(8,128)(2,1)S(1)}, u32[]{:S(2)}, u32[]{:S(2)}) collective-permute-start(bf16[104,256]{1,0:T(8,128)(2,1)S(1)} %add_convert_fusion.8), channel_id=1, source_target_pairs={{0,10},{1,11},{2,8},{3,9},{4,14},{5,15},{6,12},{7,13},{8,2},{9,3},... | collective-permute-start | bytes 159752 | tf_op jit(solution)/shard_map/ppermute | solution.py:731
  48.6 4.7 %collective-permute-start.7 = (bf16[208,256]{1,0:T(8,128)(2,1)S(1)}, bf16[208,256]{1,0:T(8,128)(2,1)S(1)}, u32[]{:S(2)}, u32[]{:S(2)}) collective-permute-start(bf16[208,256]{1,0:T(8,128)(2,1)S(1)} %pad_maximum_fusion.4), channel_id=1, source_target_pairs={{0,9},{1,25},{2,26},{3,10},{4,28},{5,12},{6,15},{7,31},{8,16},{9,0... | collective-permute-start | bytes 319496 | tf_op jit(solution)/shard_map/ppermute | solution.py:731
  50.6 5.1 %collective-permute-start.16 = (bf16[208,256]{1,0:T(8,128)(2,1)S(1)}, bf16[208,256]{1,0:T(8,128)(2,1)S(1)}, u32[]{:S(2)}, u32[]{:S(2)}) collective-permute-start(bf16[208,256]{1,0:T(8,128)(2,1)S(1)} %pad_maximum_fusion.5), channel_id=1, source_target_pairs={{0,9},{1,25},{2,26},{3,10},{4,28},{5,12},{6,15},{7,31},{8,16},{9,0... | collective-permute-start | bytes 319496 | tf_op jit(solution)/shard_map/ppermute | solution.py:731
  53.4 5.4 %collective-permute-start.8 = (bf16[416,256]{1,0:T(8,128)(2,1)S(1)}, bf16[416,256]{1,0:T(8,128)(2,1)S(1)}, u32[]{:S(2)}, u32[]{:S(2)}) collective-permute-start(bf16[416,256]{1,0:T(8,128)(2,1)S(1)} %pad_maximum_fusion.2), channel_id=1, source_target_pairs={{0,24},{1,8},{2,11},{3,27},{4,13},{5,29},{6,30},{7,14},{8,1},{9,17... | collective-permute-start | bytes 638984 | tf_op jit(solution)/shard_map/ppermute | solution.py:731
  55.8 6.3 %collective-permute-start.17 = (bf16[416,256]{1,0:T(8,128)(2,1)S(1)}, bf16[416,256]{1,0:T(8,128)(2,1)S(1)}, u32[]{:S(2)}, u32[]{:S(2)}) collective-permute-start(bf16[416,256]{1,0:T(8,128)(2,1)S(1)} %pad_maximum_fusion.3), channel_id=1, source_target_pairs={{0,24},{1,8},{2,11},{3,27},{4,13},{5,29},{6,30},{7,14},{8,1},{9,17... | collective-permute-start | bytes 638984 | tf_op jit(solution)/shard_map/ppermute | solution.py:731
  58.9 3.5 %collective-permute-start.9 = (bf16[832,256]{1,0:T(8,128)(2,1)S(1)}, bf16[832,256]{1,0:T(8,128)(2,1)S(1)}, u32[]{:S(2)}, u32[]{:S(2)}) collective-permute-start(bf16[832,256]{1,0:T(8,128)(2,1)S(1)} %pad_maximum_fusion.own), channel_id=1, source_target_pairs={{0,8},{1,9},{2,10},{3,11},{4,12},{5,13},{6,14},{7,15},{8,0},{9,1},... | collective-permute-start | bytes 1277960 | tf_op jit(solution)/shard_map/ppermute | solution.py:727
  62.2 1.9 %copy-start = (bf16[256,256]{1,0:T(8,128)(2,1)S(1)}, bf16[256,256]{1,0:T(8,128)(2,1)}, u32[]{:S(2)}) copy-start(bf16[256,256]{1,0:T(8,128)(2,1)} %constant.36.clone.turned) | copy-start | bytes 393220
  62.2 1.8 %collective-permute-start.18 = (bf16[832,256]{1,0:T(8,128)(2,1)S(1)}, bf16[832,256]{1,0:T(8,128)(2,1)S(1)}, u32[]{:S(2)}, u32[]{:S(2)}) collective-permute-start(bf16[832,256]{1,0:T(8,128)(2,1)S(1)} %pad_maximum_fusion.1.own), channel_id=1, source_target_pairs={{0,8},{1,9},{2,10},{3,11},{4,12},{5,13},{6,14},{7,15},{8,0},{9,1},... | collective-permute-start | bytes 1277960 | tf_op jit(solution)/shard_map/ppermute | solution.py:727

commit v7 on v5

--- a/solution.py
+++ b/solution.py
@@ -752,7 +752,7 @@
 
             leaving, staying = cut(kept, 1 - bit), cut(kept, bit)
             if number == 0:
-                leaving, staying = lax.optimization_barrier((leaving, staying))
+                leaving = lax.optimization_barrier(leaving)
             sent = add_low(leaving, cut(got, 1 - bit))
             kept = add_low(staying, cut(got, bit))
             got = swap(sent, bits, core, count)

time: 66.3 us -> 66.4 us (level)
  no operation moved by 1% of the time
where the time goes in v7:
time: 66.4 us; the launch traced here: 66.1 us
  starting transfers between devices  28.2 us (42%)
  Pallas kernels  20.4 us (31%)
  waiting for transfers between devices  13.2 us (20%)
  local copies, waits for them, and re-layouts  2.41 us (4%)
  between operations  1 us (2%)
  other arithmetic  0.86 us (1%)
    ppermute x14, starting transfers between devices, swap(): lax.ppermute(value, AXES, [(d, d ^ 1 << bits[side_of(d)] ^ 1 << core) for...  26.8 us
    pallas_call x1, Pallas kernels, run_layer(): pl.pallas_call(layer_kernel, out_shape=(jax.ShapeDtypeStruct((rows, FEATU...  17.5 us
    ppermute x14, waiting for transfers between devices, swap(): lax.ppermute(value, AXES, [(d, d ^ 1 << bits[side_of(d)] ^ 1 << core) for...  9.04 us
    ppermute x1, waiting for transfers between devices, body(): lax.ppermute(x[-SEG:], 'tm', [(i, (i + 1) % tm_count) for i in range(tm_c...  3.46 us
    pallas_call x1, Pallas kernels, unpack_all(): pl.pallas_call(second_unpack_kernel, out_shape=shapes(split + rest), in_s...  1.62 us
    pallas_call x1, Pallas kernels, unpack_all(): pl.pallas_call(first_unpack_kernel, out_shape=shapes(split), in_specs=[vm...  1.33 us
  transfers between devices with their start and end apart: 19, of which 12 were waited for; matrix products, arithmetic and copies ran while one was open for 3% of the time, Pallas kernels for 2%

profile of v7, /device:TPU:0, one launch (start us, length us, event | category | flops | bytes accessed | tf_op | source)
XLA Modules:
  0.0 66.1 jit_solution(15725868077708727941)
XLA Ops:
  0.7 0.7 %slice_bitcast_fusion = bf16[48,256]{1,0:T(8,128)(2,1)S(1)} fusion(bf16[1,768,256]{2,1,0:T(8,128)(2,1)} %param.22), kind=kLoop, calls=%fused_computation.34 | loop fusion | bytes 49152 | tf_op jit(solution)/shard_map/slice | solution.py:779
  1.4 0.5 collective-permute-start
  1.9 3.5 %collective-permute-done.refs_2_ = bf16[48,256]{1,0:T(8,128)(2,1)S(1)} collective-permute-done((bf16[48,256]{1,0:T(8,128)(2,1)S(1)}, bf16[48,256]{1,0:T(8,128)(2,1)S(1)}, u32[]{:S(2)}, u32[]{:S(2)}) %collective-permute-start) | collective-permute-done | bytes 24608 | tf_op jit(solution)/shard_map/ppermute | solution.py:779
  5.3 0.0 copy-start.3
  5.3 0.6 copy-done.3
  5.9 17.5 %layer.1 = (bf16[768,256]{1,0:T(8,128)(2,1)}, bf16[768,256]{1,0:T(8,128)(2,1)}, bf16[832,256]{1,0:T(8,128)(2,1)}, bf16[832,256]{1,0:T(8,128)(2,1)}, bf16[832,256]{1,0:T(8,128)(2,1)}, /*index=5*/bf16[832,256]{1,0:T(8,128)(2,1)}) custom-call(s32[1,64]{1,0:T(1,128)} %horizon_source.1, bf16[768,256]{1,0:T(8,128)(2,1)} %bitcast.15, bf16[48,256]{1,0:T(8,128)(2,1)} %bitcast.17, ...), custom_call_target="tpu_custom_call" | custom-call | tf_op jit(solution)/shard_map/layer/pallas_call | solution.py:562
  23.4 0.0 copy-start.1
  23.4 0.2 collective-permute-start.1
  23.6 0.4 collective-permute-start.10
  24.0 0.0 copy-start.2
  24.0 1.0 %constant_dynamic-slice_fusion.1 = bf16[416,256]{1,0:T(8,128)(2,1)S(1)} fusion(bf16[832,256]{1,0:T(8,128)(2,1)} %get-tuple-element.43, s32[]{:T(128)S(6)} %select_n.114), kind=kLoop, calls=%fused_computation.36 | loop fusion | bytes 425988 | tf_op jit(solution)/shard_map/dynamic_slice | solution.py:751
  25.0 0.0 copy-done.1
  25.1 0.4 collective-permute-done.1
  25.5 0.0 copy-done.2
  25.5 0.1 add_convert_fusion.3
  25.6 2.1 %collective-permute-start.2 = (bf16[416,256]{1,0:T(8,128)(2,1)S(1)}, bf16[416,256]{1,0:T(8,128)(2,1)S(1)}, u32[]{:S(2)}, u32[]{:S(2)}) collective-permute-start(bf16[416,256]{1,0:T(8,128)(2,1)S(1)} %get-tuple-element.76), channel_id=1, source_target_pairs={{0,24},{1,8},{2,11},{3,27},{4,13},{5,29},{6,30},{7,14},{8,1},{9,17... | collective-permute-start | bytes 638984 | tf_op jit(solution)/shard_map/ppermute | solution.py:730
  27.7 0.0 collective-permute-done.10
  27.7 0.1 add_convert_fusion.1
  27.9 0.5 collective-permute-start.11
  28.3 2.9 %collective-permute-done.2 = bf16[416,256]{1,0:T(8,128)(2,1)S(1)} collective-permute-done((bf16[416,256]{1,0:T(8,128)(2,1)S(1)}, bf16[416,256]{1,0:T(8,128)(2,1)S(1)}, u32[]{:S(2)}, u32[]{:S(2)}) %collective-permute-start.2) | collective-permute-done | bytes 213024 | tf_op jit(solution)/shard_map/ppermute | solution.py:730
  31.3 0.1 add_convert_fusion.7
  31.3 2.1 %collective-permute-start.3 = (bf16[208,256]{1,0:T(8,128)(2,1)S(1)}, bf16[208,256]{1,0:T(8,128)(2,1)S(1)}, u32[]{:S(2)}, u32[]{:S(2)}) collective-permute-start(bf16[208,256]{1,0:T(8,128)(2,1)S(1)} %get-tuple-element.74), channel_id=1, source_target_pairs={{0,9},{1,25},{2,26},{3,10},{4,28},{5,12},{6,15},{7,31},{8,16},{9,0... | collective-permute-start | bytes 319496 | tf_op jit(solution)/shard_map/ppermute | solution.py:730
  33.4 0.1 collective-permute-done.11
  33.5 0.1 add_convert_fusion.5
  33.6 1.8 %collective-permute-start.12 = (bf16[208,256]{1,0:T(8,128)(2,1)S(1)}, bf16[208,256]{1,0:T(8,128)(2,1)S(1)}, u32[]{:S(2)}, u32[]{:S(2)}) collective-permute-start(bf16[208,256]{1,0:T(8,128)(2,1)S(1)} %get-tuple-element.68), channel_id=1, source_target_pairs={{0,9},{1,25},{2,26},{3,10},{4,28},{5,12},{6,15},{7,31},{8,16},{9,0... | collective-permute-start | bytes 319496 | tf_op jit(solution)/shard_map/ppermute | solution.py:730
  35.4 0.4 collective-permute-done.3
  35.8 1.9 %collective-permute-start.4 = (bf16[104,256]{1,0:T(8,128)(2,1)S(1)}, bf16[104,256]{1,0:T(8,128)(2,1)S(1)}, u32[]{:S(2)}, u32[]{:S(2)}) collective-permute-start(bf16[104,256]{1,0:T(8,128)(2,1)S(1)} %add_convert_fusion.14), channel_id=1, source_target_pairs={{0,10},{1,11},{2,8},{3,9},{4,14},{5,15},{6,12},{7,13},{8,2},{9,3},... | collective-permute-start | bytes 159752 | tf_op jit(solution)/shard_map/ppermute | solution.py:730
  37.7 0.1 collective-permute-done.12
  37.8 1.9 %collective-permute-start.13 = (bf16[104,256]{1,0:T(8,128)(2,1)S(1)}, bf16[104,256]{1,0:T(8,128)(2,1)S(1)}, u32[]{:S(2)}, u32[]{:S(2)}) collective-permute-start(bf16[104,256]{1,0:T(8,128)(2,1)S(1)} %add_convert_fusion.10), channel_id=1, source_target_pairs={{0,10},{1,11},{2,8},{3,9},{4,14},{5,15},{6,12},{7,13},{8,2},{9,3},... | collective-permute-start | bytes 159752 | tf_op jit(solution)/shard_map/ppermute | solution.py:730
  39.7 0.0 collective-permute-done.4
  39.7 2.7 %collective-permute-start.5 = (bf16[104,256]{1,0:T(8,128)(2,1)S(1)}, bf16[104,256]{1,0:T(8,128)(2,1)S(1)}, u32[]{:S(2)}, u32[]{:S(2)}) collective-permute-start(bf16[104,256]{1,0:T(8,128)(2,1)S(1)} %add_convert_fusion.13), channel_id=1, source_target_pairs={{0,12},{1,13},{2,14},{3,15},{4,8},{5,9},{6,10},{7,11},{8,4},{9,5},... | collective-permute-start | bytes 159752 | tf_op jit(solution)/shard_map/ppermute | solution.py:730
  42.4 0.0 collective-permute-done.13
  42.4 2.2 %collective-permute-start.14 = (bf16[104,256]{1,0:T(8,128)(2,1)S(1)}, bf16[104,256]{1,0:T(8,128)(2,1)S(1)}, u32[]{:S(2)}, u32[]{:S(2)}) collective-permute-start(bf16[104,256]{1,0:T(8,128)(2,1)S(1)} %add_convert_fusion.9), channel_id=1, source_target_pairs={{0,12},{1,13},{2,14},{3,15},{4,8},{5,9},{6,10},{7,11},{8,4},{9,5},... | collective-permute-start | bytes 159752 | tf_op jit(solution)/shard_map/ppermute | solution.py:730
  44.6 0.0 collective-permute-done.5
  44.6 1.7 %collective-permute-start.6 = (bf16[104,256]{1,0:T(8,128)(2,1)S(1)}, bf16[104,256]{1,0:T(8,128)(2,1)S(1)}, u32[]{:S(2)}, u32[]{:S(2)}) collective-permute-start(bf16[104,256]{1,0:T(8,128)(2,1)S(1)} %add_convert_fusion.12), channel_id=1, source_target_pairs={{0,10},{1,11},{2,8},{3,9},{4,14},{5,15},{6,12},{7,13},{8,2},{9,3},... | collective-permute-start | bytes 159752 | tf_op jit(solution)/shard_map/ppermute | solution.py:730
  46.4 0.9 %collective-permute-done.14 = bf16[104,256]{1,0:T(8,128)(2,1)S(1)} collective-permute-done((bf16[104,256]{1,0:T(8,128)(2,1)S(1)}, bf16[104,256]{1,0:T(8,128)(2,1)S(1)}, u32[]{:S(2)}, u32[]{:S(2)}) %collective-permute-start.14) | collective-permute-done | bytes 53280 | tf_op jit(solution)/shard_map/ppermute | solution.py:730
  47.3 1.6 %collective-permute-start.15 = (bf16[104,256]{1,0:T(8,128)(2,1)S(1)}, bf16[104,256]{1,0:T(8,128)(2,1)S(1)}, u32[]{:S(2)}, u32[]{:S(2)}) collective-permute-start(bf16[104,256]{1,0:T(8,128)(2,1)S(1)} %add_convert_fusion.8), channel_id=1, source_target_pairs={{0,10},{1,11},{2,8},{3,9},{4,14},{5,15},{6,12},{7,13},{8,2},{9,3},... | collective-permute-start | bytes 159752 | tf_op jit(solution)/shard_map/ppermute | solution.py:730
  48.9 0.0 collective-permute-done.6
  48.9 1.7 %collective-permute-start.7 = (bf16[208,256]{1,0:T(8,128)(2,1)S(1)}, bf16[208,256]{1,0:T(8,128)(2,1)S(1)}, u32[]{:S(2)}, u32[]{:S(2)}) collective-permute-start(bf16[208,256]{1,0:T(8,128)(2,1)S(1)} %pad_maximum_fusion.4), channel_id=1, source_target_pairs={{0,9},{1,25},{2,26},{3,10},{4,28},{5,12},{6,15},{7,31},{8,16},{9,0... | collective-permute-start | bytes 319496 | tf_op jit(solution)/shard_map/ppermute | solution.py:730
  50.6 0.3 collective-permute-done.15
  50.9 2.7 %collective-permute-start.16 = (bf16[208,256]{1,0:T(8,128)(2,1)S(1)}, bf16[208,256]{1,0:T(8,128)(2,1)S(1)}, u32[]{:S(2)}, u32[]{:S(2)}) collective-permute-start(bf16[208,256]{1,0:T(8,128)(2,1)S(1)} %pad_maximum_fusion.5), channel_id=1, source_target_pairs={{0,9},{1,25},{2,26},{3,10},{4,28},{5,12},{6,15},{7,31},{8,16},{9,0... | collective-permute-start | bytes 319496 | tf_op jit(solution)/shard_map/ppermute | solution.py:730
  53.6 0.0 collective-permute-done.7
  53.7 1.2 %collective-permute-start.8 = (bf16[416,256]{1,0:T(8,128)(2,1)S(1)}, bf16[416,256]{1,0:T(8,128)(2,1)S(1)}, u32[]{:S(2)}, u32[]{:S(2)}) collective-permute-start(bf16[416,256]{1,0:T(8,128)(2,1)S(1)} %pad_maximum_fusion.2), channel_id=1, source_target_pairs={{0,24},{1,8},{2,11},{3,27},{4,13},{5,29},{6,30},{7,14},{8,1},{9,17... | collective-permute-start | bytes 638984 | tf_op jit(solution)/shard_map/ppermute | solution.py:730
  54.9 1.1 %collective-permute-done.16 = bf16[208,256]{1,0:T(8,128)(2,1)S(1)} collective-permute-done((bf16[208,256]{1,0:T(8,128)(2,1)S(1)}, bf16[208,256]{1,0:T(8,128)(2,1)S(1)}, u32[]{:S(2)}, u32[]{:S(2)}) %collective-permute-start.16) | collective-permute-done | bytes 106528 | tf_op jit(solution)/shard_map/ppermute | solution.py:730
  56.1 2.8 %collective-permute-start.17 = (bf16[416,256]{1,0:T(8,128)(2,1)S(1)}, bf16[416,256]{1,0:T(8,128)(2,1)S(1)}, u32[]{:S(2)}, u32[]{:S(2)}) collective-permute-start(bf16[416,256]{1,0:T(8,128)(2,1)S(1)} %pad_maximum_fusion.3), channel_id=1, source_target_pairs={{0,24},{1,8},{2,11},{3,27},{4,13},{5,29},{6,30},{7,14},{8,1},{9,17... | collective-permute-start | bytes 638984 | tf_op jit(solution)/shard_map/ppermute | solution.py:730
  58.9 0.3 collective-permute-done.8
  59.1 0.1 broadcast_select_fusion.3
  59.2 0.2 collective-permute-start.9
  59.4 3.0 %collective-permute-done.17 = bf16[416,256]{1,0:T(8,128)(2,1)S(1)} collective-permute-done((bf16[416,256]{1,0:T(8,128)(2,1)S(1)}, bf16[416,256]{1,0:T(8,128)(2,1)S(1)}, u32[]{:S(2)}, u32[]{:S(2)}) %collective-permute-start.17) | collective-permute-done | bytes 213024 | tf_op jit(solution)/shard_map/ppermute | solution.py:730
  62.4 0.1 broadcast_select_fusion.1
  62.5 0.0 copy-start
  62.5 0.2 collective-permute-start.18
  62.7 0.0 collective-permute-done.9.other
  62.7 1.3 %unpack_first.1 = (f32[256,1024]{1,0:T(8,128)}, f32[1024,256]{1,0:T(8,128)}, f32[256,256]{1,0:T(8,128)}) custom-call(bf16[832,256]{1,0:T(8,128)(2,1)S(1)} %pad_maximum_fusion.own, bf16[832,256]{1,0:T(8,128)(2,1)S(1)} %collective-permute-done.9.other), custom_call_target="tpu_custom_call" | custom-call | tf_op jit(solution)/shard_map/unpack_first/pallas_call | solution.py:673
  64.1 0.3 collective-permute-done.18.other
  64.4 0.0 copy-done
  64.4 1.6 %unpack_second.1 = (f32[256,1024]{1,0:T(8,128)}, f32[1024,256]{1,0:T(8,128)}, f32[256,256]{1,0:T(8,128)}, f32[256,256]{1,0:T(8,128)}, f32[256,256]{1,0:T(8,128)}...) custom-call(f32[256,1024]{1,0:T(8,128)} %get-tuple-element.45.w1_old, ...), custom_call_target="tpu_custom_call", output_to_operand_aliasing={{0}: (0, {}), {1}: (1, {}), {2}: (2, {})} | custom-call | tf_op jit(solution)/shard_map/unpack_second/pallas_call | solution.py:688
  (17 shorter events, 0.3 us)
Async XLA Ops:
  1.4 3.9 %collective-permute-start = (bf16[48,256]{1,0:T(8,128)(2,1)S(1)}, bf16[48,256]{1,0:T(8,128)(2,1)S(1)}, u32[]{:S(2)}, u32[]{:S(2)}) collective-permute-start(bf16[48,256]{1,0:T(8,128)(2,1)S(1)} %slice_bitcast_fusion), channel_id=1, source_target_pairs={{0,8},{8,16},{16,24},{24,0},{1,9},{9,17},{17,25},{25,1},{2,10},{10... | collective-permute-start | bytes 73736 | tf_op jit(solution)/shard_map/ppermute | solution.py:779
  5.3 0.6 copy-start.3
  23.4 1.6 %copy-start.1 = (bf16[832,256]{1,0:T(8,128)(2,1)S(1)}, bf16[832,256]{1,0:T(8,128)(2,1)}, u32[]{:S(2)}) copy-start(bf16[832,256]{1,0:T(8,128)(2,1)} %get-tuple-element.48) | copy-start | bytes 1277956
  23.4 2.0 %collective-permute-start.1 = (bf16[832,256]{1,0:T(8,128)(2,1)}, bf16[832,256]{1,0:T(8,128)(2,1)S(1)}, u32[]{:S(2)}, u32[]{:S(2)}) collective-permute-start(bf16[832,256]{1,0:T(8,128)(2,1)} %get-tuple-element.44), channel_id=1, source_target_pairs={{0,8},{1,9},{2,10},{3,11},{4,12},{5,13},{6,14},{7,15},{8,0},{9,1},... | collective-permute-start | bytes 1277960 | tf_op jit(solution)/shard_map/ppermute | solution.py:726
  23.6 4.1 %collective-permute-start.10 = (bf16[832,256]{1,0:T(8,128)(2,1)}, bf16[832,256]{1,0:T(8,128)(2,1)S(1)}, u32[]{:S(2)}, u32[]{:S(2)}) collective-permute-start(bf16[832,256]{1,0:T(8,128)(2,1)} %get-tuple-element.49), channel_id=1, source_target_pairs={{0,8},{1,9},{2,10},{3,11},{4,12},{5,13},{6,14},{7,15},{8,0},{9,1},... | collective-permute-start | bytes 1277960 | tf_op jit(solution)/shard_map/ppermute | solution.py:726
  24.0 1.5 %copy-start.2 = (bf16[832,256]{1,0:T(8,128)(2,1)S(1)}, bf16[832,256]{1,0:T(8,128)(2,1)}, u32[]{:S(2)}) copy-start(bf16[832,256]{1,0:T(8,128)(2,1)} %get-tuple-element.43) | copy-start | bytes 1277956
  25.6 5.6 %collective-permute-start.2 = (bf16[416,256]{1,0:T(8,128)(2,1)S(1)}, bf16[416,256]{1,0:T(8,128)(2,1)S(1)}, u32[]{:S(2)}, u32[]{:S(2)}) collective-permute-start(bf16[416,256]{1,0:T(8,128)(2,1)S(1)} %get-tuple-element.76), channel_id=1, source_target_pairs={{0,24},{1,8},{2,11},{3,27},{4,13},{5,29},{6,30},{7,14},{8,1},{9,17... | collective-permute-start | bytes 638984 | tf_op jit(solution)/shard_map/ppermute | solution.py:730
  27.9 5.7 %collective-permute-start.11 = (bf16[416,256]{1,0:T(8,128)(2,1)S(1)}, bf16[416,256]{1,0:T(8,128)(2,1)S(1)}, u32[]{:S(2)}, u32[]{:S(2)}) collective-permute-start(bf16[416,256]{1,0:T(8,128)(2,1)S(1)} %get-tuple-element.70), channel_id=1, source_target_pairs={{0,24},{1,8},{2,11},{3,27},{4,13},{5,29},{6,30},{7,14},{8,1},{9,17... | collective-permute-start | bytes 638984 | tf_op jit(solution)/shard_map/ppermute | solution.py:730
  31.3 4.5 %collective-permute-start.3 = (bf16[208,256]{1,0:T(8,128)(2,1)S(1)}, bf16[208,256]{1,0:T(8,128)(2,1)S(1)}, u32[]{:S(2)}, u32[]{:S(2)}) collective-permute-start(bf16[208,256]{1,0:T(8,128)(2,1)S(1)} %get-tuple-element.74), channel_id=1, source_target_pairs={{0,9},{1,25},{2,26},{3,10},{4,28},{5,12},{6,15},{7,31},{8,16},{9,0... | collective-permute-start | bytes 319496 | tf_op jit(solution)/shard_map/ppermute | solution.py:730
  33.6 4.2 %collective-permute-start.12 = (bf16[208,256]{1,0:T(8,128)(2,1)S(1)}, bf16[208,256]{1,0:T(8,128)(2,1)S(1)}, u32[]{:S(2)}, u32[]{:S(2)}) collective-permute-start(bf16[208,256]{1,0:T(8,128)(2,1)S(1)} %get-tuple-element.68), channel_id=1, source_target_pairs={{0,9},{1,25},{2,26},{3,10},{4,28},{5,12},{6,15},{7,31},{8,16},{9,0... | collective-permute-start | bytes 319496 | tf_op jit(solution)/shard_map/ppermute | solution.py:730
  35.8 3.9 %collective-permute-start.4 = (bf16[104,256]{1,0:T(8,128)(2,1)S(1)}, bf16[104,256]{1,0:T(8,128)(2,1)S(1)}, u32[]{:S(2)}, u32[]{:S(2)}) collective-permute-start(bf16[104,256]{1,0:T(8,128)(2,1)S(1)} %add_convert_fusion.14), channel_id=1, source_target_pairs={{0,10},{1,11},{2,8},{3,9},{4,14},{5,15},{6,12},{7,13},{8,2},{9,3},... | collective-permute-start | bytes 159752 | tf_op jit(solution)/shard_map/ppermute | solution.py:730
  37.8 4.6 %collective-permute-start.13 = (bf16[104,256]{1,0:T(8,128)(2,1)S(1)}, bf16[104,256]{1,0:T(8,128)(2,1)S(1)}, u32[]{:S(2)}, u32[]{:S(2)}) collective-permute-start(bf16[104,256]{1,0:T(8,128)(2,1)S(1)} %add_convert_fusion.10), channel_id=1, source_target_pairs={{0,10},{1,11},{2,8},{3,9},{4,14},{5,15},{6,12},{7,13},{8,2},{9,3},... | collective-permute-start | bytes 159752 | tf_op jit(solution)/shard_map/ppermute | solution.py:730
  39.7 4.9 %collective-permute-start.5 = (bf16[104,256]{1,0:T(8,128)(2,1)S(1)}, bf16[104,256]{1,0:T(8,128)(2,1)S(1)}, u32[]{:S(2)}, u32[]{:S(2)}) collective-permute-start(bf16[104,256]{1,0:T(8,128)(2,1)S(1)} %add_convert_fusion.13), channel_id=1, source_target_pairs={{0,12},{1,13},{2,14},{3,15},{4,8},{5,9},{6,10},{7,11},{8,4},{9,5},... | collective-permute-start | bytes 159752 | tf_op jit(solution)/shard_map/ppermute | solution.py:730
  42.4 4.8 %collective-permute-start.14 = (bf16[104,256]{1,0:T(8,128)(2,1)S(1)}, bf16[104,256]{1,0:T(8,128)(2,1)S(1)}, u32[]{:S(2)}, u32[]{:S(2)}) collective-permute-start(bf16[104,256]{1,0:T(8,128)(2,1)S(1)} %add_convert_fusion.9), channel_id=1, source_target_pairs={{0,12},{1,13},{2,14},{3,15},{4,8},{5,9},{6,10},{7,11},{8,4},{9,5},... | collective-permute-start | bytes 159752 | tf_op jit(solution)/shard_map/ppermute | solution.py:730
  44.6 4.3 %collective-permute-start.6 = (bf16[104,256]{1,0:T(8,128)(2,1)S(1)}, bf16[104,256]{1,0:T(8,128)(2,1)S(1)}, u32[]{:S(2)}, u32[]{:S(2)}) collective-permute-start(bf16[104,256]{1,0:T(8,128)(2,1)S(1)} %add_convert_fusion.12), channel_id=1, source_target_pairs={{0,10},{1,11},{2,8},{3,9},{4,14},{5,15},{6,12},{7,13},{8,2},{9,3},... | collective-permute-start | bytes 159752 | tf_op jit(solution)/shard_map/ppermute | solution.py:730
  47.3 3.6 %collective-permute-start.15 = (bf16[104,256]{1,0:T(8,128)(2,1)S(1)}, bf16[104,256]{1,0:T(8,128)(2,1)S(1)}, u32[]{:S(2)}, u32[]{:S(2)}) collective-permute-start(bf16[104,256]{1,0:T(8,128)(2,1)S(1)} %add_convert_fusion.8), channel_id=1, source_target_pairs={{0,10},{1,11},{2,8},{3,9},{4,14},{5,15},{6,12},{7,13},{8,2},{9,3},... | collective-permute-start | bytes 159752 | tf_op jit(solution)/shard_map/ppermute | solution.py:730
  48.9 4.7 %collective-permute-start.7 = (bf16[208,256]{1,0:T(8,128)(2,1)S(1)}, bf16[208,256]{1,0:T(8,128)(2,1)S(1)}, u32[]{:S(2)}, u32[]{:S(2)}) collective-permute-start(bf16[208,256]{1,0:T(8,128)(2,1)S(1)} %pad_maximum_fusion.4), channel_id=1, source_target_pairs={{0,9},{1,25},{2,26},{3,10},{4,28},{5,12},{6,15},{7,31},{8,16},{9,0... | collective-permute-start | bytes 319496 | tf_op jit(solution)/shard_map/ppermute | solution.py:730
  50.9 5.1 %collective-permute-start.16 = (bf16[208,256]{1,0:T(8,128)(2,1)S(1)}, bf16[208,256]{1,0:T(8,128)(2,1)S(1)}, u32[]{:S(2)}, u32[]{:S(2)}) collective-permute-start(bf16[208,256]{1,0:T(8,128)(2,1)S(1)} %pad_maximum_fusion.5), channel_id=1, source_target_pairs={{0,9},{1,25},{2,26},{3,10},{4,28},{5,12},{6,15},{7,31},{8,16},{9,0... | collective-permute-start | bytes 319496 | tf_op jit(solution)/shard_map/ppermute | solution.py:730
  53.7 5.4 %collective-permute-start.8 = (bf16[416,256]{1,0:T(8,128)(2,1)S(1)}, bf16[416,256]{1,0:T(8,128)(2,1)S(1)}, u32[]{:S(2)}, u32[]{:S(2)}) collective-permute-start(bf16[416,256]{1,0:T(8,128)(2,1)S(1)} %pad_maximum_fusion.2), channel_id=1, source_target_pairs={{0,24},{1,8},{2,11},{3,27},{4,13},{5,29},{6,30},{7,14},{8,1},{9,17... | collective-permute-start | bytes 638984 | tf_op jit(solution)/shard_map/ppermute | solution.py:730
  56.1 6.3 %collective-permute-start.17 = (bf16[416,256]{1,0:T(8,128)(2,1)S(1)}, bf16[416,256]{1,0:T(8,128)(2,1)S(1)}, u32[]{:S(2)}, u32[]{:S(2)}) collective-permute-start(bf16[416,256]{1,0:T(8,128)(2,1)S(1)} %pad_maximum_fusion.3), channel_id=1, source_target_pairs={{0,24},{1,8},{2,11},{3,27},{4,13},{5,29},{6,30},{7,14},{8,1},{9,17... | collective-permute-start | bytes 638984 | tf_op jit(solution)/shard_map/ppermute | solution.py:730
  59.2 3.5 %collective-permute-start.9 = (bf16[832,256]{1,0:T(8,128)(2,1)S(1)}, bf16[832,256]{1,0:T(8,128)(2,1)S(1)}, u32[]{:S(2)}, u32[]{:S(2)}) collective-permute-start(bf16[832,256]{1,0:T(8,128)(2,1)S(1)} %pad_maximum_fusion.own), channel_id=1, source_target_pairs={{0,8},{1,9},{2,10},{3,11},{4,12},{5,13},{6,14},{7,15},{8,0},{9,1},... | collective-permute-start | bytes 1277960 | tf_op jit(solution)/shard_map/ppermute | solution.py:726
  62.5 1.9 %copy-start = (bf16[256,256]{1,0:T(8,128)(2,1)S(1)}, bf16[256,256]{1,0:T(8,128)(2,1)}, u32[]{:S(2)}) copy-start(bf16[256,256]{1,0:T(8,128)(2,1)} %constant.36.clone.turned) | copy-start | bytes 393220
  62.5 1.8 %collective-permute-start.18 = (bf16[832,256]{1,0:T(8,128)(2,1)S(1)}, bf16[832,256]{1,0:T(8,128)(2,1)S(1)}, u32[]{:S(2)}, u32[]{:S(2)}) collective-permute-start(bf16[832,256]{1,0:T(8,128)(2,1)S(1)} %pad_maximum_fusion.1.own), channel_id=1, source_target_pairs={{0,8},{1,9},{2,10},{3,11},{4,12},{5,13},{6,14},{7,15},{8,0},{9,1},... | collective-permute-start | bytes 1277960 | tf_op jit(solution)/shard_map/ppermute | solution.py:726
